TPU v7x, 1024 devices: a whole 4x8x16 slice. The times are simulated.
1024 devices in a mesh: dp: 8 (over x, core), ep: 32 (over z, y_hi), tp: 4 (over y_lo).
Axes of the slice: x: 4, y: 8 (y_hi: 2, y_lo: 4; y = y_hi * 4 + y_lo), z: 16, core: 2. Of those that a mesh axis runs over, the one named last changes fastest.
Arguments:
- tokens: bfloat16 [32768, 4096], P(('dp', 'ep'), 'tp'), may hold values from -6 to 6
- expert_ids: int32 [32768, 8], P(('dp', 'ep')), may hold values from 0 to 127, all different within a row; in each aligned block of 128 rows (0 to 127, 128 to 255, ...) at most 10 rows name the same one
- route_weight: float32 [32768, 8], P(('dp', 'ep')), may hold values from 0.05 to 0.5
- gate_up: bfloat16 [32, 2, 1536, 4096], P('ep', None, None, 'tp'), may hold values from -0.09375 to 0.09375
- down_proj: bfloat16 [32, 1536, 4096], P('ep', None, 'tp'), may hold values from -0.15625 to 0.15625
Outputs:
- mixed: bfloat16 [32768, 4096], P(('dp', 'ep'), 'tp')
Inputs may be any that keep to these rules, and one draw needn't show every extreme that they name: `expert_ids`: each row names 8 different experts. Among the 128 rows of one block no expert is named more than 10 times, and in some block one expert is named exactly 10 times.
All inputs are finite; a program needn't handle non-finite values.
Results may differ from a plain program's by a relative error of at most 0.024.
Values may be sent and summed in bfloat16 or wider, within the bound.
No kernel may reach another device: no remote copies, remote signals or barrier semaphores. Data moves between devices by JAX's collectives and lax.ppermute only.
A program may use at most 32 MiB of HBM per device.

v0:
```python
import jax
import jax.numpy as jnp
from jax import lax
from jax.sharding import PartitionSpec as P

CAP = 10


def slot_table(routed_ids, flight, capacity):
    flat_ids = routed_ids.reshape(-1)
    matches = (flat_ids[:, None] == jnp.arange(flight, dtype=jnp.int32)[None, :]).astype(jnp.int32)
    before = jnp.cumsum(matches, axis=0) - matches
    slot_index = jnp.sum(before * matches, axis=1)
    placed = jnp.where(flat_ids < flight, flat_ids * capacity + slot_index, -1)
    return placed.reshape(routed_ids.shape)


def pack_rows(position, token_rows, places):
    target_hits = position[:, :, None] == jnp.arange(places, dtype=jnp.int32)[None, None, :]
    selector = jnp.any(target_hits, axis=1).T.astype(token_rows.dtype)
    return jnp.dot(selector, token_rows, preferred_element_type=jnp.float32).astype(jnp.bfloat16)


def combine(position, weight, returned):
    picked = returned[jnp.maximum(position, 0)].astype(jnp.float32)
    coefficient = jnp.where(position >= 0, weight, 0.0)
    return jnp.sum(coefficient[:, :, None] * picked, axis=1).astype(jnp.bfloat16)


def local(tokens, expert_ids, route_weight, gate_up, down_proj):
    flight = lax.axis_size("ep")
    places = flight * CAP
    feature_cols = tokens.shape[1]
    position = slot_table(expert_ids, flight, CAP)
    sent = pack_rows(position, tokens, places).reshape(flight, CAP, feature_cols)
    weights_in = gate_up[0]
    weights_out = down_proj[0]
    received = lax.all_to_all(sent, "ep", split_axis=0, concat_axis=0, tiled=True)
    sources = received.shape[0]
    slot_count = received.shape[1]
    row_block = received.reshape(sources * slot_count, feature_cols)
    preact = jnp.einsum("rd,gfd->rgf", row_block, weights_in, preferred_element_type=jnp.float32)
    summed = lax.psum(preact.astype(jnp.bfloat16), "tp").astype(jnp.float32)
    hidden = (jax.nn.silu(summed[:, 0]) * summed[:, 1]).astype(jnp.bfloat16)
    result = jnp.dot(hidden, weights_out, preferred_element_type=jnp.float32).astype(jnp.bfloat16)
    result = result.reshape(sources, slot_count, feature_cols)
    returned = lax.all_to_all(result, "ep", split_axis=0, concat_axis=0, tiled=True)
    return combine(position, route_weight, returned.reshape(places, feature_cols))


def solution(mesh):
    return jax.shard_map(
        local,
        mesh=mesh,
        in_specs=(
            P(("dp", "ep"), "tp"),
            P(("dp", "ep"), None),
            P(("dp", "ep"), None),
            P("ep", None, None, "tp"),
            P("ep", None, "tp"),
        ),
        out_specs=P(("dp", "ep"), "tp"),
        check_vma=False,
    )
```

profile of v0, /device:TPU:56, one launch (start us, length us, event | category | flops | bytes accessed | tf_op | source)
XLA Modules:
  0.0 309.7 jit_solution(6997824442652071635)
XLA Ops:
  6.5 0.9 copy.31
  7.5 0.1 eq.42
  7.7 9.0 %reduce-window.6 = s32[32,8,128]{2,1,0:T(8,128)S(1)} reduce-window(s32[32,8,128]{2,1,0:T(8,128)S(1)} %fusion.18, s32[]{:T(128)} %constant.5.clone.1), window={size=1x1x128 pad=0_0x0_0x127_0}, to_apply=%region_0.0 | reduce-window | flops 4161536 | bytes 262148 | tf_op jit(solution)/shard_map/reduce-window
  16.8 0.1 copy.33
  17.0 0.1 broadcast_add_fusion
  17.3 0.7 compare_select_fusion
  18.1 0.2 fusion.12
  18.2 2.1 convolution_convert_fusion
  20.4 2.1 reshape.43
  22.5 77.9 %all_to_all.10 = bf16[32,10,1024]{2,1,0:T(8,128)(2,1)} all-to-all(bf16[32,10,1024]{2,1,0:T(8,128)(2,1)} %reshape.43), channel_id=1, replica_groups=mesh['dp'=8,'ep'=32,'tp'=4] {'ep'}, dimensions={0} | all-to-all | bytes 1310720 | tf_op jit(solution)/shard_map/all_to_all | solution.py:38
  100.4 2.1 reshape.58
  102.4 6.5 %fusion.3 = bf16[320,2,1536]{2,0,1:T(8,128)(2,1)} fusion(bf16[320,1024,1]{1,0,2:T(8,128)(2,1)} %reshape.58, bf16[1,2,1536,1024]{3,2,1,0:T(8,128)(2,1)} %param.8), kind=kOutput, calls=%fused_computation.5 | convolution fusion | flops 2014248960 | bytes 8912896 | tf_op jit(solution)/shard_map/rd,gfd->rgf/dot_general | solution.py:42
  109.0 102.5 %all-reduce.2.cloned.1.call-done = bf16[320,2,1536]{2,0,1:T(8,128)(2,1)} async-done(((bf16[320,2,1536]{2,0,1:T(8,128)(2,1)}), bf16[320,2,1536]{2,0,1:T(8,128)(2,1)}) %all-reduce.2.cloned.1.call-update) | async-done | bytes 1966096 | tf_op jit(solution)/shard_map/psum | solution.py:43
  211.5 2.1 convert_element_type.36
  213.6 2.1 fusion.9
  215.7 2.2 reshape.45
  217.9 18.5 %all-to-all-start.1 = ((bf16[32,10,1024]{2,1,0:T(8,128)(2,1)}), bf16[32,10,1024]{2,1,0:T(8,128)(2,1)}, u32[]{:S(2)}, u32[]{:S(2)}) async-start(bf16[32,10,1024]{2,1,0:T(8,128)(2,1)} %reshape.45), calls=%async_computation.1 | async-start | bytes 2097152 | tf_op jit(solution)/shard_map/all_to_all | solution.py:47
  236.4 0.1 copy.37
  236.5 0.1 reshape.49
  236.6 0.1 copy.36
  236.7 53.2 %all-to-all-done.1 = bf16[32,10,1024]{2,1,0:T(8,128)(2,1)} async-done(((bf16[32,10,1024]{2,1,0:T(8,128)(2,1)}), bf16[32,10,1024]{2,1,0:T(8,128)(2,1)}, u32[]{:S(2)}, u32[]{:S(2)}) %all-to-all-start.1) | async-done | bytes 655392 | tf_op jit(solution)/shard_map/all_to_all | solution.py:47
  289.9 2.1 reshape.46
  292.0 7.2 %gather_fusion = bf16[1024,1024]{1,0:T(8,128)(2,1)} fusion(bf16[320,1024]{1,0:T(8,128)(2,1)} %reshape.46, s32[1024]{0:T(1024)S(1)} %broadcast_clamp_fusion), kind=kCustom, calls=%fused_computation | custom fusion | bytes 4198400 | tf_op jit(solution)/shard_map/gather | solution.py:25
  299.2 3.7 %fusion.2 = bf16[128,1024]{1,0:T(8,128)(2,1)} fusion(bf16[1024,1024]{1,0:T(8,128)(2,1)} %gather_fusion, f32[128,8]{1,0:T(8,128)S(1)} %copy.36), kind=kLoop, calls=%fused_computation.4 | loop fusion | flops 3014656 | bytes 2363392 | tf_op jit(solution)/shard_map/reduce_sum | solution.py:27
  (15 shorter events, 0.5 us)
Async XLA Ops:
  6.5 207.0 %copy-start = (bf16[1,1536,1024]{2,1,0:T(8,128)(2,1)S(1)}, bf16[1,1536,1024]{2,1,0:T(8,128)(2,1)}, u32[]{:S(2)}) copy-start(bf16[1,1536,1024]{2,1,0:T(8,128)(2,1)} %param.9) | copy-start | bytes 9437188
  6.5 204.9 %all-reduce.2.cloned.1.call-start = ((), (), s32[]{:S(2)}) async-start(), calls=%async_computation.2 | async-start | bytes 3932160 | tf_op jit(solution)/shard_map/psum | solution.py:43
  217.9 72.0 %all-to-all-start.1 = ((bf16[32,10,1024]{2,1,0:T(8,128)(2,1)}), bf16[32,10,1024]{2,1,0:T(8,128)(2,1)}, u32[]{:S(2)}, u32[]{:S(2)}) async-start(bf16[32,10,1024]{2,1,0:T(8,128)(2,1)} %reshape.45), calls=%async_computation.1 | async-start | bytes 2097152 | tf_op jit(solution)/shard_map/all_to_all | solution.py:47
Sparse Core Ops, SparseCore 0:
  109.1 102.3 all-reduce.1
where the time goes:
time: 310 us
  waiting for transfers between devices  156 us (50%)
  blocking collectives  77.9 us (25%)
  starting transfers between devices  18.5 us (6%)
  local copies, waits for them, and re-layouts  17.5 us (6%)
  other arithmetic  15.8 us (5%)
  between operations  13.5 us (4%)
  matrix products  10.8 us (3%)
    psum x1, waiting for transfers between devices, local(): summed = lax.psum(preact.astype(jnp.bfloat16), 'tp').astype(jnp.float32)  102 us
    all_to_all x1, blocking collectives, local(): lax.all_to_all(sent, 'ep', split_axis=0, concat_axis=0, tiled=True)  77.9 us
    all_to_all x1, waiting for transfers between devices, local(): lax.all_to_all(result, 'ep', split_axis=0, concat_axis=0, tiled=True)  53.2 us
    all_to_all x1, starting transfers between devices, local(): lax.all_to_all(result, 'ep', split_axis=0, concat_axis=0, tiled=True)  18.5 us
    another operation x3, other arithmetic  9.15 us
    gather x1, local copies, waits for them, and re-layouts, combine(): picked = returned[jnp.maximum(position, 0)].astype(jnp.float32)  7.21 us
    dot_general x1, matrix products, local(): jnp.einsum('rd,gfd->rgf', row_block, weights_in, preferred_element_type=j...  6.53 us
  transfers between devices with their start and end apart: 2, of which 2 were waited for; matrix products, arithmetic and copies ran while one was open for 0% of the time, Pallas kernels for 0%

commit v1 on v0

v1 whole, which is shorter than its diff:
```python
import jax
import jax.numpy as jnp
import numpy as np
from jax import lax
from jax.experimental import pallas as pl
from jax.experimental.pallas import tpu as pltpu
from jax.sharding import PartitionSpec as P

CAP = 10
QUARTERS = 4
FAR = 200.0
APART = 512.0
BF16 = jnp.bfloat16
F32 = jnp.float32
PARAMS = pltpu.CompilerParams(vmem_limit_bytes=48 * 1024 * 1024)
BLOCK = QUARTERS * CAP
GROUP = 8


def mm(a, b):
    return jnp.dot(a, b, preferred_element_type=F32)


def mm_t(a, b):
    return lax.dot_general(a, b, (((1,), (1,)), ((), ())), preferred_element_type=F32)


def place_code(flight):
    rows = np.arange(flight * BLOCK)
    expert, quarter, slot = rows // BLOCK, rows // CAP % QUARTERS, rows % CAP
    code = np.zeros((rows.size, flight + 16), np.float32)
    code[rows, expert] = 1
    code[:, flight] = -slot
    code[rows, flight + 1 + quarter] = APART
    return code


def quarter_code(rows):
    code = np.zeros((16, QUARTERS * rows), np.float32)
    code[0] = 1
    for quarter in range(QUARTERS):
        code[1 + quarter] = np.arange(QUARTERS * rows) // rows != quarter
    return code


def regroup_code():
    source, quarter, slot = np.meshgrid(np.arange(GROUP), np.arange(QUARTERS), np.arange(CAP), indexing="ij")
    code = np.zeros((GROUP * BLOCK, GROUP * BLOCK), np.float32)
    code[(quarter * GROUP + source) * CAP + slot, (source * QUARTERS + quarter) * CAP + slot] = 1
    return code


def pack_kernel(ids_ref, token_ref, earlier_ref, place_ref, quarter_ref, out_ref):
    top, rows = ids_ref.shape
    flight = place_ref.shape[1] - 16
    cols = out_ref.shape[1]
    expert = lax.broadcasted_iota(jnp.int32, (flight, rows), 0)
    named = jnp.zeros((flight, rows), F32)
    for k in range(top):
        named += jnp.where(ids_ref[k : k + 1, :] == expert, 1.0, 0.0)
    slot = mm(named.astype(BF16), earlier_ref[...])
    slot = jnp.where(named > 0, slot, FAR).astype(BF16)
    code = jnp.concatenate([jnp.concatenate([slot] * QUARTERS, axis=1), quarter_ref[...]], axis=0)
    gap = mm(place_ref[...], code)
    selector = jnp.where(gap == 0, 1.0, 0.0).astype(BF16)
    stacked = jnp.concatenate([token_ref[:, q * cols : (q + 1) * cols] for q in range(QUARTERS)], axis=0)
    out_ref[...] = mm(selector, stacked).astype(BF16)


def pack(ids_t, tokens, flight):
    rows, features = tokens.shape
    places = flight * BLOCK
    steps = 4
    earlier = jnp.asarray(np.triu(np.ones((rows, rows), np.float32), 1), BF16)
    place = jnp.asarray(place_code(flight), BF16)
    quarter = jnp.asarray(quarter_code(rows), BF16)
    whole = lambda a: pl.BlockSpec(a.shape, lambda i: (0, 0))
    return pl.pallas_call(
        pack_kernel,
        out_shape=jax.ShapeDtypeStruct((places, features // QUARTERS), BF16),
        grid=(steps,),
        in_specs=[whole(ids_t), whole(tokens), whole(earlier),
                  pl.BlockSpec((places // steps, place.shape[1]), lambda i: (i, 0)), whole(quarter)],
        out_specs=pl.BlockSpec((places // steps, features // QUARTERS), lambda i: (i, 0)),
        compiler_params=PARAMS,
        name="pack",
    )(ids_t, tokens, earlier, place, quarter)


def first_kernel(order_ref, x_ref, regroup_ref, weight_ref, rows_ref, out_ref):
    cols = x_ref.shape[1]
    span, slab = GROUP * BLOCK, GROUP * CAP
    for g in range(x_ref.shape[0] // span):
        sorted_rows = mm(regroup_ref[...], x_ref[g * span : (g + 1) * span, :]).astype(BF16)
        for q in range(QUARTERS):
            rows_ref[g * slab : (g + 1) * slab, q * cols : (q + 1) * cols] = sorted_rows[q * slab : (q + 1) * slab]
    units = weight_ref.shape[2]
    for h in range(2):
        out_ref[:, h * units : (h + 1) * units] = mm_t(rows_ref[...], weight_ref[h, 0]).astype(BF16)


def first_part(order, received, weights):
    places, cols = received.shape
    rows = places // QUARTERS
    features = weights.shape[3]
    units = weights.shape[2]
    regroup = jnp.asarray(regroup_code(), BF16)
    whole = lambda shape: pl.BlockSpec(shape, lambda i, order: (0, 0))
    return pl.pallas_call(
        first_kernel,
        out_shape=(jax.ShapeDtypeStruct((rows, features), BF16), jax.ShapeDtypeStruct((rows, 2 * units), BF16)),
        grid_spec=pltpu.PrefetchScalarGridSpec(
            num_scalar_prefetch=1,
            grid=(1,),
            in_specs=[whole((places, cols)), whole(regroup.shape),
                      pl.BlockSpec((2, 1, units, features), lambda i, order: (0, order[i], 0, 0))],
            out_specs=(whole((rows, features)), whole((rows, 2 * units))),
        ),
        compiler_params=PARAMS,
        cost_estimate=pl.CostEstimate(flops=4 * rows * units * features, bytes_accessed=4 * units * features, transcendentals=0),
        name="first",
    )(order, received, regroup, weights)


def rest_kernel(order_ref, rows_ref, weight_ref, *out_refs):
    units = weight_ref.shape[2]
    for j, out_ref in enumerate(out_refs):
        @pl.when(pl.program_id(0) == j)
        def _():
            for h in range(2):
                out_ref[:, h * units : (h + 1) * units] = mm_t(rows_ref[...], weight_ref[h, 0]).astype(BF16)


def rest_parts(order, rows_in, weights, count):
    rows, features = rows_in.shape
    units = weights.shape[2]
    whole = lambda shape: pl.BlockSpec(shape, lambda i, order: (0, 0))
    return pl.pallas_call(
        rest_kernel,
        out_shape=(jax.ShapeDtypeStruct((rows, 2 * units), BF16),) * count,
        grid_spec=pltpu.PrefetchScalarGridSpec(
            num_scalar_prefetch=1,
            grid=(count,),
            in_specs=[whole((rows, features)),
                      pl.BlockSpec((2, 1, units, features), lambda i, order: (0, order[i], 0, 0))],
            out_specs=(whole((rows, 2 * units)),) * count,
        ),
        compiler_params=PARAMS,
        cost_estimate=pl.CostEstimate(flops=4 * count * rows * units * features, bytes_accessed=4 * count * units * features, transcendentals=0),
        name="rest",
    )(order, rows_in, weights)


def down_kernel(hidden_ref, weight_ref, spread_ref, out_ref, total):
    step = pl.program_id(0)
    cols = out_ref.shape[1]
    span, slab = GROUP * BLOCK, GROUP * CAP
    part = mm(hidden_ref[0], weight_ref[0])

    @pl.when(step == 0)
    def _():
        total[...] = part

    @pl.when(step > 0)
    def _():
        total[...] += part

    @pl.when(step == pl.num_programs(0) - 1)
    def _():
        for g in range(out_ref.shape[0] // span):
            block = total[g * slab : (g + 1) * slab, :].astype(BF16)
            stacked = jnp.concatenate([block[:, q * cols : (q + 1) * cols] for q in range(QUARTERS)], axis=0)
            out_ref[g * span : (g + 1) * span, :] = mm(spread_ref[...], stacked).astype(BF16)


def down(hidden, weights):
    parts, rows, units = hidden.shape
    features = weights.shape[2]
    cols = features // QUARTERS
    spread = jnp.asarray(regroup_code().T, BF16)
    return pl.pallas_call(
        down_kernel,
        out_shape=jax.ShapeDtypeStruct((rows * QUARTERS, cols), BF16),
        grid=(parts,),
        in_specs=[pl.BlockSpec((1, rows, units), lambda i: (i, 0, 0)),
                  pl.BlockSpec((1, units, features), lambda i: (i, 0, 0)),
                  pl.BlockSpec(spread.shape, lambda i: (0, 0))],
        out_specs=pl.BlockSpec((rows * QUARTERS, cols), lambda i: (0, 0)),
        scratch_shapes=[pltpu.VMEM((rows, features), F32)],
        compiler_params=PARAMS,
        name="down",
    )(hidden, weights, spread)


def mixer_kernel(ids_ref, weight_ref, earlier_ref, expert_ref, slot_ref, quarter_ref, out_ref):
    rows, top = ids_ref.shape
    flight = expert_ref.shape[0]
    expert = lax.broadcasted_iota(jnp.int32, (rows, flight), 1)
    named = jnp.zeros((rows, flight), F32)
    weight = jnp.zeros((rows, flight), F32)
    for k in range(top):
        hit = ids_ref[:, k : k + 1] == expert
        named += jnp.where(hit, 1.0, 0.0)
        weight += jnp.where(hit, weight_ref[:, k : k + 1], 0.0)
    slot = mm(earlier_ref[...], named.astype(BF16))
    slot = jnp.where(named > 0, slot, FAR).astype(BF16)
    gap = mm(slot, expert_ref[...]) + mm(quarter_ref[...], slot_ref[...])
    out_ref[...] = jnp.where(gap == 0, mm(weight.astype(BF16), expert_ref[...]), 0.0).astype(BF16)


def mixer(ids, weight, flight):
    rows = ids.shape[0]
    places = flight * BLOCK
    code = place_code(flight).T
    earlier = jnp.asarray(np.tril(np.ones((rows, rows), np.float32), -1), BF16)
    expert, slot = jnp.asarray(code[:flight], BF16), jnp.asarray(code[flight:], BF16)
    quarter = jnp.asarray(quarter_code(rows).T, BF16)
    whole = lambda a: pl.BlockSpec(a.shape, lambda i: (0, 0))
    return pl.pallas_call(
        mixer_kernel,
        out_shape=jax.ShapeDtypeStruct((QUARTERS * rows, places), BF16),
        grid=(QUARTERS,),
        in_specs=[whole(ids), whole(weight), whole(earlier), whole(expert), whole(slot),
                  pl.BlockSpec((rows, 16), lambda i: (i, 0))],
        out_specs=pl.BlockSpec((rows, places), lambda i: (i, 0)),
        compiler_params=PARAMS,
        name="mixer",
    )(ids, weight, earlier, expert, slot, quarter)


def combine_kernel(mixer_ref, returned_ref, out_ref):
    out_ref[...] = mm(mixer_ref[...], returned_ref[...]).astype(BF16)


def combine(mix, returned):
    places, cols = returned.shape
    rows = mix.shape[0] // QUARTERS
    return pl.pallas_call(
        combine_kernel,
        out_shape=jax.ShapeDtypeStruct((rows, QUARTERS * cols), BF16),
        grid=(QUARTERS,),
        in_specs=[pl.BlockSpec((rows, places), lambda i: (i, 0)), pl.BlockSpec((places, cols), lambda i: (0, 0))],
        out_specs=pl.BlockSpec((rows, cols), lambda i: (0, i)),
        compiler_params=PARAMS,
        name="combine",
    )(mix, returned)


def local(tokens, expert_ids, route_weight, gate_up, down_proj):
    flight = lax.axis_size("ep")
    n_tp = lax.axis_size("tp")
    features = tokens.shape[1]
    cols = features // QUARTERS
    units = gate_up.shape[2] // n_tp
    up_weights = gate_up.reshape(2, n_tp, units, features)
    down_weights = down_proj.reshape(n_tp, units, features)
    me = lax.axis_index("tp")
    order = jnp.stack([me ^ 3, me ^ 1, me ^ 2, me]).astype(jnp.int32)
    near = [(i, i ^ 1) for i in range(n_tp)]
    far = [(i, i ^ 2) for i in range(n_tp)]

    sent = pack(expert_ids.T, tokens, flight)
    received = lax.all_to_all(sent.reshape(flight, BLOCK, cols), "ep", 0, 0, tiled=True).reshape(flight * BLOCK, cols)

    row_block, for_far = first_part(order[:1], received, up_weights)
    got_far = lax.ppermute(for_far, "tp", near)
    for_near, keep_far, keep = rest_parts(order[1:], row_block, up_weights, 3)
    pair_far = (got_far.astype(F32) + keep_far.astype(F32)).astype(BF16)
    for_near, pair_far = lax.optimization_barrier((for_near, pair_far))
    got = lax.ppermute(pair_far, "tp", far)
    got_near = lax.ppermute(for_near, "tp", near)
    summed = got.astype(F32) + got_near.astype(F32) + keep.astype(F32)
    hidden = (jax.nn.silu(summed[:, :units]) * summed[:, units:]).astype(BF16)
    hidden = lax.all_gather(hidden, "tp", axis=0, tiled=False)

    result = down(hidden, down_weights)
    returned = lax.all_to_all(result.reshape(flight, BLOCK, cols), "ep", 0, 0, tiled=True).reshape(flight * BLOCK, cols)
    mix = mixer(expert_ids, route_weight, flight)
    return combine(mix, returned)


def solution(mesh):
    return jax.shard_map(
        local,
        mesh=mesh,
        in_specs=(
            P(("dp", "ep"), "tp"),
            P(("dp", "ep"), None),
            P(("dp", "ep"), None),
            P("ep", None, None, "tp"),
            P("ep", None, "tp"),
        ),
        out_specs=P(("dp", "ep"), "tp"),
        check_vma=False,
    )
```

time: 310 us -> 186 us (0.60)
  waiting for transfers between devices: 156 us -> 93.9 us
  blocking collectives: 77.9 us -> 19.9 us
  starting transfers between devices: 18.5 us -> 45.8 us
  Pallas kernels: 0 us -> 19.3 us
  other arithmetic: 15.8 us -> 0.5 us
  between operations: 13.5 us -> 0.17 us
  local copies, waits for them, and re-layouts: 17.5 us -> 5.27 us
  matrix products: 10.8 us -> 0 us
    psum x1 -> x0, waiting for transfers between devices: 102 us -> none  [local(): summed = lax.psum(preact.astype(jnp.bfloat16), 'tp').astype(jnp.float32)]
    all_to_all x1 -> x0, blocking collectives: 77.9 us -> none  [local(): lax.all_to_all(sent, 'ep', split_axis=0, concat_axis=0, tiled=True)]
    ppermute x0 -> x3, waiting for transfers between devices: none -> 24.9 us  [the longest x1 17.5 us: local(): got = lax.ppermute(pair_far, 'tp', far)]
    all_gather x0 -> x1, blocking collectives: none -> 19.9 us  [local(): hidden = lax.all_gather(hidden, 'tp', axis=0, tiled=False)]
    pallas_call x0 -> x6, Pallas kernels: none -> 19.3 us  [the longest x1 5.12 us: rest_parts(): pl.pallas_call(rest_kernel, out_shape=(jax.ShapeDtypeStruct((rows, 2 * un...]
    all_to_all x1 -> x2, starting transfers between devices: 18.5 us -> 35 us  [the longest x1 24.3 us: local(): lax.all_to_all(sent.reshape(flight, BLOCK, cols), 'ep', 0, 0, tiled=True)]
    all_to_all x1 -> x2, waiting for transfers between devices: 53.2 us -> 69 us  [the longest x1 37.4 us: local(): lax.all_to_all(sent.reshape(flight, BLOCK, cols), 'ep', 0, 0, tiled=True)]
    ppermute x0 -> x3, starting transfers between devices: none -> 10.8 us  [the longest x1 4.31 us: local(): got = lax.ppermute(pair_far, 'tp', far)]
  transfers between devices with their start and end apart: 2 -> 5, of which waited for: 2 -> 5; matrix products, arithmetic and copies ran while one was open for 0% -> 0% of each run, Pallas kernels for 0% -> 4%
where the time goes in v1:
time: 186 us; the launch traced here: 185 us
  waiting for transfers between devices  93.9 us (50%)
  starting transfers between devices  45.8 us (25%)
  blocking collectives  19.9 us (11%)
  Pallas kernels  19.3 us (10%)
  local copies, waits for them, and re-layouts  5.27 us (3%)
    all_to_all x1, waiting for transfers between devices, local(): lax.all_to_all(sent.reshape(flight, BLOCK, cols), 'ep', 0, 0, tiled=True)  37.4 us
    all_to_all x1, waiting for transfers between devices, local(): lax.all_to_all(result.reshape(flight, BLOCK, cols), 'ep', 0, 0, tiled=True)  31.6 us
    all_to_all x1, starting transfers between devices, local(): lax.all_to_all(sent.reshape(flight, BLOCK, cols), 'ep', 0, 0, tiled=True)  24.3 us
    all_gather x1, blocking collectives, local(): hidden = lax.all_gather(hidden, 'tp', axis=0, tiled=False)  19.9 us
    ppermute x1, waiting for transfers between devices, local(): got = lax.ppermute(pair_far, 'tp', far)  17.5 us
    all_to_all x1, starting transfers between devices, local(): lax.all_to_all(result.reshape(flight, BLOCK, cols), 'ep', 0, 0, tiled=True)  10.7 us
    ppermute x1, waiting for transfers between devices, local(): got_far = lax.ppermute(for_far, 'tp', near)  5.75 us
    unnamed x30, local copies, waits for them, and re-layouts  5.27 us
  transfers between devices with their start and end apart: 5, of which 5 were waited for; matrix products, arithmetic and copies ran while one was open for 0% of the time, Pallas kernels for 4%

profile of v1, /device:TPU:56, one launch (start us, length us, event | category | flops | bytes accessed | tf_op | source)
XLA Modules:
  0.0 184.9 jit_solution(11692793156266403001)
XLA Ops:
  0.0 1.0 copy-done.1
  1.0 0.9 copy-done.2
  1.9 0.8 copy-done.8
  2.7 0.7 copy-done.10
  3.4 0.7 copy-done.11
  4.1 2.8 %pack.1 = bf16[1280,256]{1,0:T(8,128)(2,1)} custom-call(s32[8,128]{1,0:T(8,128)S(1)} %bitcast.16, bf16[128,1024]{1,0:T(8,128)(2,1)S(1)} %copy-done.2, bf16[128,128]{1,0:T(8,128)(2,1)S(1)} %copy-done.8, bf16[1280,48]{1,0:T(8,128)(2,1)S(1)} %copy-done.1, bf16[16,512]{1,0:T(8,128)(2,1)S(1)} %copy-done.10), custom_call_target="tpu_custom_call" | custom-call | tf_op jit(solution)/shard_map/pack/pallas_call | solution.py:78
  6.9 24.3 %all-to-all-start = ((bf16[32,40,256]{2,1,0:T(8,128)(2,1)}), bf16[32,40,256]{2,1,0:T(8,128)(2,1)S(1)}, u32[]{:S(2)}, u32[]{:S(2)}) async-start(bf16[32,40,256]{2,1,0:T(8,128)(2,1)} %bitcast.5), calls=%async_computation | async-start | bytes 1310720 | tf_op jit(solution)/shard_map/all_to_all | solution.py:263
  31.2 37.4 %all-to-all-done = bf16[32,40,256]{2,1,0:T(8,128)(2,1)S(1)} async-done(((bf16[32,40,256]{2,1,0:T(8,128)(2,1)}), bf16[32,40,256]{2,1,0:T(8,128)(2,1)S(1)}, u32[]{:S(2)}, u32[]{:S(2)}) %all-to-all-start) | async-done | bytes 655392 | tf_op jit(solution)/shard_map/all_to_all | solution.py:263
  68.5 0.9 copy-done.3
  69.5 2.6 %first.1 = (bf16[320,1024]{1,0:T(8,128)(2,1)S(1)}, bf16[320,768]{1,0:T(8,128)(2,1)S(1)}) custom-call(s32[1]{0:T(128)} %bitcast.3.order_ref, bf16[1280,256]{1,0:T(8,128)(2,1)S(1)} %bitcast.14, bf16[320,320]{1,0:T(8,128)(2,1)S(1)} %copy-done.3, bf16[2,4,384,1024]{3,2,1,0:T(8,128)(2,1)} %bitcast.17), custom_call_target="tpu_custom_call" | custom-call | flops 503316480 | bytes 1572864 | tf_op jit(solution)/shard_map/first/pallas_call | solution.py:109
  72.1 3.3 %collective-permute-start = (bf16[320,768]{1,0:T(8,128)(2,1)S(1)}, bf16[320,768]{1,0:T(8,128)(2,1)S(1)}, u32[]{:S(2)}, u32[]{:S(2)}) collective-permute-start(bf16[320,768]{1,0:T(8,128)(2,1)S(1)} %get-tuple-element.14), channel_id=1, source_target_pairs={{0,1},{1,0},{2,3},{3,2},{4,5},{5,4},{6,7},{7,6},{8,9},{9,8},{10,11... | collective-permute-start | bytes 1474568 | tf_op jit(solution)/shard_map/ppermute | solution.py:266
  75.4 5.1 %rest.1 = (bf16[320,768]{1,0:T(8,128)(2,1)S(1)}, bf16[320,768]{1,0:T(8,128)(2,1)S(1)}, bf16[320,768]{1,0:T(8,128)(2,1)S(1)}) custom-call(s32[3]{0:T(128)S(1)} %pad_add_fusion.order_ref, bf16[320,1024]{1,0:T(8,128)(2,1)S(1)} %get-tuple-element.12.rows_ref, bf16[2,4,384,1024]{3,2,1,0:T(8,128)(2,1)} %bitcast.18), custom_call_target="tpu_custom_call" | custom-call | flops 1509949440 | bytes 4718592 | tf_op jit(solution)/shard_map/rest/pallas_call | solution.py:138
  80.5 5.7 %collective-permute-done = bf16[320,768]{1,0:T(8,128)(2,1)S(1)} collective-permute-done((bf16[320,768]{1,0:T(8,128)(2,1)S(1)}, bf16[320,768]{1,0:T(8,128)(2,1)S(1)}, u32[]{:S(2)}, u32[]{:S(2)}) %collective-permute-start) | collective-permute-done | bytes 491552 | tf_op jit(solution)/shard_map/ppermute | solution.py:266
  86.4 4.3 %collective-permute-start.1 = (bf16[320,768]{1,0:T(8,128)(2,1)S(1)}, bf16[320,768]{1,0:T(8,128)(2,1)S(1)}, u32[]{:S(2)}, u32[]{:S(2)}) collective-permute-start(bf16[320,768]{1,0:T(8,128)(2,1)S(1)} %add_convert_fusion), channel_id=1, source_target_pairs={{0,2},{1,3},{2,0},{3,1},{4,6},{5,7},{6,4},{7,5},{8,10},{9,11},{10,... | collective-permute-start | bytes 1474568 | tf_op jit(solution)/shard_map/ppermute | solution.py:270
  90.7 3.2 %collective-permute-start.2 = (bf16[320,768]{1,0:T(8,128)(2,1)S(1)}, bf16[320,768]{1,0:T(8,128)(2,1)S(1)}, u32[]{:S(2)}, u32[]{:S(2)}) collective-permute-start(bf16[320,768]{1,0:T(8,128)(2,1)S(1)} %get-tuple-element.17), channel_id=1, source_target_pairs={{0,1},{1,0},{2,3},{3,2},{4,5},{5,4},{6,7},{7,6},{8,9},{9,8},{10,11... | collective-permute-start | bytes 1474568 | tf_op jit(solution)/shard_map/ppermute | solution.py:271
  94.0 17.5 %collective-permute-done.1 = bf16[320,768]{1,0:T(8,128)(2,1)S(1)} collective-permute-done((bf16[320,768]{1,0:T(8,128)(2,1)S(1)}, bf16[320,768]{1,0:T(8,128)(2,1)S(1)}, u32[]{:S(2)}, u32[]{:S(2)}) %collective-permute-start.1) | collective-permute-done | bytes 491552 | tf_op jit(solution)/shard_map/ppermute | solution.py:270
  111.5 1.6 collective-permute-done.2
  113.1 0.2 convert_add_fusion
  113.5 19.9 %all-gather = bf16[1280,384]{1,0:T(8,128)(2,1)S(1)} all-gather(bf16[320,384]{1,0:T(8,128)(2,1)S(1)} %fusion), channel_id=2, replica_groups=mesh['dp'=8,'ep'=32,'tp'=4] {'tp'}, dimensions={0}, use_global_device_ids=true | all-gather | bytes 1228800 | tf_op jit(solution)/shard_map/all_gather | solution.py:274
  133.4 3.9 %down.1 = bf16[1280,256]{1,0:T(8,128)(2,1)} custom-call(bf16[4,320,384]{2,1,0:T(8,128)(2,1)S(1)} %bitcast.12, bf16[4,384,1024]{2,1,0:T(8,128)(2,1)S(1)} %bitcast.13, bf16[320,320]{1,0:T(8,128)(2,1)S(1)} %copy-done.4), custom_call_target="tpu_custom_call" | custom-call | tf_op jit(solution)/shard_map/down/pallas_call | solution.py:181
  137.3 10.7 %all-to-all-start.1 = ((bf16[32,40,256]{2,1,0:T(8,128)(2,1)}), bf16[32,40,256]{2,1,0:T(8,128)(2,1)S(1)}, u32[]{:S(2)}, u32[]{:S(2)}) async-start(bf16[32,40,256]{2,1,0:T(8,128)(2,1)} %bitcast.10), calls=%async_computation.1 | async-start | bytes 1310720 | tf_op jit(solution)/shard_map/all_to_all | solution.py:277
  148.3 2.9 %mixer.1.mixer_ref = bf16[512,1280]{1,0:T(8,128)(2,1)S(1)} custom-call(s32[128,8]{1,0:T(8,128)S(1)} %copy.15.ids_ref, f32[128,8]{1,0:T(8,128)S(1)} %copy.16.weight_ref, bf16[128,128]{1,0:T(8,128)(2,1)S(1)} %copy-done.9, bf16[32,1280]{1,0:T(8,128)(2,1)S(1)} %copy-done.6, bf16[16,1280]{1,0:T(8,128)(2,1)S(1)} %copy-done.7, bf16[512,16]{1,0:T(8,128)(2,1)S(1)} %copy-done.5), custom_call_target="tpu_custom_call" | custom-call | tf_op jit(solution)/shard_map/mixer/pallas_call | solution.py:219
  151.2 31.6 %all-to-all-done.1 = bf16[32,40,256]{2,1,0:T(8,128)(2,1)S(1)} async-done(((bf16[32,40,256]{2,1,0:T(8,128)(2,1)}), bf16[32,40,256]{2,1,0:T(8,128)(2,1)S(1)}, u32[]{:S(2)}, u32[]{:S(2)}) %all-to-all-start.1) | async-done | bytes 655392 | tf_op jit(solution)/shard_map/all_to_all | solution.py:277
  182.8 2.0 %combine.1 = bf16[128,1024]{1,0:T(8,128)(2,1)} custom-call(bf16[512,1280]{1,0:T(8,128)(2,1)S(1)} %mixer.1.mixer_ref, bf16[1280,256]{1,0:T(8,128)(2,1)S(1)} %bitcast.15), custom_call_target="tpu_custom_call" | custom-call | tf_op jit(solution)/shard_map/combine/pallas_call | solution.py:238
  (27 shorter events, 0.6 us)
Async XLA Ops:
  0.0 1.0 copy-start.1
  1.0 0.9 copy-start.2
  1.9 0.8 copy-start.8
  2.7 0.7 copy-start.10
  3.4 0.7 copy-start.11
  6.9 61.6 %all-to-all-start = ((bf16[32,40,256]{2,1,0:T(8,128)(2,1)}), bf16[32,40,256]{2,1,0:T(8,128)(2,1)S(1)}, u32[]{:S(2)}, u32[]{:S(2)}) async-start(bf16[32,40,256]{2,1,0:T(8,128)(2,1)} %bitcast.5), calls=%async_computation | async-start | bytes 1310720 | tf_op jit(solution)/shard_map/all_to_all | solution.py:263
  68.5 0.9 copy-start.3
  72.1 14.2 %collective-permute-start = (bf16[320,768]{1,0:T(8,128)(2,1)S(1)}, bf16[320,768]{1,0:T(8,128)(2,1)S(1)}, u32[]{:S(2)}, u32[]{:S(2)}) collective-permute-start(bf16[320,768]{1,0:T(8,128)(2,1)S(1)} %get-tuple-element.14), channel_id=1, source_target_pairs={{0,1},{1,0},{2,3},{3,2},{4,5},{5,4},{6,7},{7,6},{8,9},{9,8},{10,11... | collective-permute-start | bytes 1474568 | tf_op jit(solution)/shard_map/ppermute | solution.py:266
  86.3 47.1 %copy-start = (bf16[1,1536,1024]{2,1,0:T(8,128)(2,1)S(1)}, bf16[1,1536,1024]{2,1,0:T(8,128)(2,1)}, u32[]{:S(2)}) copy-start(bf16[1,1536,1024]{2,1,0:T(8,128)(2,1)} %param.18) | copy-start | bytes 9437188
  86.3 47.1 %copy-start.4 = (bf16[320,320]{1,0:T(8,128)(2,1)S(1)}, bf16[320,320]{1,0:T(8,128)(2,1)}, u32[]{:S(2)}) copy-start(bf16[320,320]{1,0:T(8,128)(2,1)} %constant.35.clone.spread_ref) | copy-start | bytes 614404
  86.4 25.1 %collective-permute-start.1 = (bf16[320,768]{1,0:T(8,128)(2,1)S(1)}, bf16[320,768]{1,0:T(8,128)(2,1)S(1)}, u32[]{:S(2)}, u32[]{:S(2)}) collective-permute-start(bf16[320,768]{1,0:T(8,128)(2,1)S(1)} %add_convert_fusion), channel_id=1, source_target_pairs={{0,2},{1,3},{2,0},{3,1},{4,6},{5,7},{6,4},{7,5},{8,10},{9,11},{10,... | collective-permute-start | bytes 1474568 | tf_op jit(solution)/shard_map/ppermute | solution.py:270
  90.7 22.4 %collective-permute-start.2 = (bf16[320,768]{1,0:T(8,128)(2,1)S(1)}, bf16[320,768]{1,0:T(8,128)(2,1)S(1)}, u32[]{:S(2)}, u32[]{:S(2)}) collective-permute-start(bf16[320,768]{1,0:T(8,128)(2,1)S(1)} %get-tuple-element.17), channel_id=1, source_target_pairs={{0,1},{1,0},{2,3},{3,2},{4,5},{5,4},{6,7},{7,6},{8,9},{9,8},{10,11... | collective-permute-start | bytes 1474568 | tf_op jit(solution)/shard_map/ppermute | solution.py:271
  133.4 14.6 %copy-start.12 = (s32[128,8]{0,1:T(8,128)S(1)}, s32[128,8]{0,1:T(8,128)}, u32[]{:S(2)}) copy-start(s32[128,8]{0,1:T(8,128)} %param.15) | copy-start | bytes 12292
  133.4 14.8 %copy-start.13 = (f32[128,8]{0,1:T(8,128)S(1)}, f32[128,8]{0,1:T(8,128)}, u32[]{:S(2)}) copy-start(f32[128,8]{0,1:T(8,128)} %param.16) | copy-start | bytes 12292
  133.4 14.9 %copy-start.5 = (bf16[512,16]{1,0:T(8,128)(2,1)S(1)}, bf16[512,16]{1,0:T(8,128)(2,1)}, u32[]{:S(2)}) copy-start(bf16[512,16]{1,0:T(8,128)(2,1)} %constant.39.clone.quarter_ref) | copy-start | bytes 49156
  133.4 14.8 %copy-start.6 = (bf16[32,1280]{1,0:T(8,128)(2,1)S(1)}, bf16[32,1280]{1,0:T(8,128)(2,1)}, u32[]{:S(2)}) copy-start(bf16[32,1280]{1,0:T(8,128)(2,1)} %constant.37.clone.expert_ref) | copy-start | bytes 245764
  133.4 14.8 %copy-start.7 = (bf16[16,1280]{1,0:T(8,128)(2,1)S(1)}, bf16[16,1280]{1,0:T(8,128)(2,1)}, u32[]{:S(2)}) copy-start(bf16[16,1280]{1,0:T(8,128)(2,1)} %constant.38.clone.slot_ref) | copy-start | bytes 122884
  133.4 14.8 %copy-start.9 = (bf16[128,128]{1,0:T(8,128)(2,1)S(1)}, bf16[128,128]{1,0:T(8,128)(2,1)}, u32[]{:S(2)}) copy-start(bf16[128,128]{1,0:T(8,128)(2,1)} %constant.36.clone.earlier_ref) | copy-start | bytes 98308
  137.3 45.5 %all-to-all-start.1 = ((bf16[32,40,256]{2,1,0:T(8,128)(2,1)}), bf16[32,40,256]{2,1,0:T(8,128)(2,1)S(1)}, u32[]{:S(2)}, u32[]{:S(2)}) async-start(bf16[32,40,256]{2,1,0:T(8,128)(2,1)} %bitcast.10), calls=%async_computation.1 | async-start | bytes 1310720 | tf_op jit(solution)/shard_map/all_to_all | solution.py:277

commit v2 on v1

--- a/solution.py
+++ b/solution.py
@@ -1,3 +1,5 @@
+import functools
+
 import jax
 import jax.numpy as jnp
 import numpy as np
@@ -43,25 +45,49 @@
     return code
 
 
-def regroup_code():
-    source, quarter, slot = np.meshgrid(np.arange(GROUP), np.arange(QUARTERS), np.arange(CAP), indexing="ij")
-    code = np.zeros((GROUP * BLOCK, GROUP * BLOCK), np.float32)
-    code[(quarter * GROUP + source) * CAP + slot, (source * QUARTERS + quarter) * CAP + slot] = 1
-    return code
-
-
-def pack_kernel(ids_ref, token_ref, earlier_ref, place_ref, quarter_ref, out_ref):
+def counter(shape, dim):
+    return lax.broadcasted_iota(jnp.int32, shape, dim).astype(F32)
+
+
+def split(number, size):
+    quotient = jnp.floor((number + 0.5) * (1.0 / size))
+    return quotient, number - size * quotient
+
+
+def regroup_matrix(back):
+    span = GROUP * BLOCK
+    row = counter((span, 1), 0)
+    if back:
+        source, rest = split(row, BLOCK)
+        quarter, slot = split(rest, CAP)
+        column = quarter * (GROUP * CAP) + source * CAP + slot
+    else:
+        quarter, rest = split(row, GROUP * CAP)
+        source, slot = split(rest, CAP)
+        column = source * BLOCK + quarter * CAP + slot
+    return jnp.where(counter((span, span), 1) == column, 1.0, 0.0).astype(BF16)
+
+
+def pack_kernel(flight, ids_ref, token_ref, out_ref):
     top, rows = ids_ref.shape
-    flight = place_ref.shape[1] - 16
-    cols = out_ref.shape[1]
+    places, cols = out_ref.shape
     expert = lax.broadcasted_iota(jnp.int32, (flight, rows), 0)
     named = jnp.zeros((flight, rows), F32)
     for k in range(top):
         named += jnp.where(ids_ref[k : k + 1, :] == expert, 1.0, 0.0)
-    slot = mm(named.astype(BF16), earlier_ref[...])
-    slot = jnp.where(named > 0, slot, FAR).astype(BF16)
-    code = jnp.concatenate([jnp.concatenate([slot] * QUARTERS, axis=1), quarter_ref[...]], axis=0)
-    gap = mm(place_ref[...], code)
+    earlier = jnp.where(counter((rows, rows), 0) < counter((rows, rows), 1), 1.0, 0.0).astype(BF16)
+    slot = jnp.where(named > 0, mm(named.astype(BF16), earlier), FAR)
+
+    line = counter((16, rows), 0)
+    other = [jnp.where((line <= QUARTERS) & (line != q + 1), 1.0, 0.0) for q in range(QUARTERS)]
+    code = jnp.concatenate([jnp.concatenate([slot, o], axis=0) for o in other], axis=1).astype(BF16)
+    place = counter((places, 1), 0) + (pl.program_id(0) * places).astype(F32)
+    owner, rest = split(place, BLOCK)
+    quarter, place_slot = split(rest, CAP)
+    column = counter((places, flight + 16), 1)
+    place_code = jnp.where(column == owner, 1.0, 0.0) + jnp.where(column == flight, -place_slot, 0.0)
+    place_code += jnp.where(column == flight + 1 + quarter, APART, 0.0)
+    gap = mm(place_code.astype(BF16), code)
     selector = jnp.where(gap == 0, 1.0, 0.0).astype(BF16)
     stacked = jnp.concatenate([token_ref[:, q * cols : (q + 1) * cols] for q in range(QUARTERS)], axis=0)
     out_ref[...] = mm(selector, stacked).astype(BF16)
@@ -71,32 +97,31 @@
     rows, features = tokens.shape
     places = flight * BLOCK
     steps = 4
-    earlier = jnp.asarray(np.triu(np.ones((rows, rows), np.float32), 1), BF16)
-    place = jnp.asarray(place_code(flight), BF16)
-    quarter = jnp.asarray(quarter_code(rows), BF16)
     whole = lambda a: pl.BlockSpec(a.shape, lambda i: (0, 0))
     return pl.pallas_call(
-        pack_kernel,
+        functools.partial(pack_kernel, flight),
         out_shape=jax.ShapeDtypeStruct((places, features // QUARTERS), BF16),
         grid=(steps,),
-        in_specs=[whole(ids_t), whole(tokens), whole(earlier),
-                  pl.BlockSpec((places // steps, place.shape[1]), lambda i: (i, 0)), whole(quarter)],
+        in_specs=[whole(ids_t), whole(tokens)],
         out_specs=pl.BlockSpec((places // steps, features // QUARTERS), lambda i: (i, 0)),
-        compiler_params=PARAMS,
+        compiler_params=pltpu.CompilerParams(vmem_limit_bytes=60 * 1024 * 1024),
         name="pack",
-    )(ids_t, tokens, earlier, place, quarter)
-
-
-def first_kernel(order_ref, x_ref, regroup_ref, weight_ref, rows_ref, out_ref):
+    )(ids_t, tokens)
+
+
+def first_kernel(order_ref, x_ref, weight_ref, rows_ref, out_ref):
     cols = x_ref.shape[1]
     span, slab = GROUP * BLOCK, GROUP * CAP
-    for g in range(x_ref.shape[0] // span):
-        sorted_rows = mm(regroup_ref[...], x_ref[g * span : (g + 1) * span, :]).astype(BF16)
-        for q in range(QUARTERS):
-            rows_ref[g * slab : (g + 1) * slab, q * cols : (q + 1) * cols] = sorted_rows[q * slab : (q + 1) * slab]
-    units = weight_ref.shape[2]
-    for h in range(2):
-        out_ref[:, h * units : (h + 1) * units] = mm_t(rows_ref[...], weight_ref[h, 0]).astype(BF16)
+
+    @pl.when(pl.program_id(0) == 0)
+    def _():
+        regroup = regroup_matrix(False)
+        for g in range(x_ref.shape[0] // span):
+            sorted_rows = mm(regroup, x_ref[g * span : (g + 1) * span, :]).astype(BF16)
+            for q in range(QUARTERS):
+                rows_ref[g * slab : (g + 1) * slab, q * cols : (q + 1) * cols] = sorted_rows[q * slab : (q + 1) * slab]
+
+    out_ref[...] = mm_t(rows_ref[...], weight_ref[0, 0]).astype(BF16)
 
 
 def first_part(order, received, weights):
@@ -104,22 +129,21 @@
     rows = places // QUARTERS
     features = weights.shape[3]
     units = weights.shape[2]
-    regroup = jnp.asarray(regroup_code(), BF16)
-    whole = lambda shape: pl.BlockSpec(shape, lambda i, order: (0, 0))
+    whole = lambda shape: pl.BlockSpec(shape, lambda h, order: (0, 0))
     return pl.pallas_call(
         first_kernel,
         out_shape=(jax.ShapeDtypeStruct((rows, features), BF16), jax.ShapeDtypeStruct((rows, 2 * units), BF16)),
         grid_spec=pltpu.PrefetchScalarGridSpec(
             num_scalar_prefetch=1,
-            grid=(1,),
-            in_specs=[whole((places, cols)), whole(regroup.shape),
-                      pl.BlockSpec((2, 1, units, features), lambda i, order: (0, order[i], 0, 0))],
-            out_specs=(whole((rows, features)), whole((rows, 2 * units))),
+            grid=(2,),
+            in_specs=[whole((places, cols)),
+                      pl.BlockSpec((1, 1, units, features), lambda h, order: (h, order[0], 0, 0))],
+            out_specs=(whole((rows, features)), pl.BlockSpec((rows, units), lambda h, order: (0, h))),
         ),
         compiler_params=PARAMS,
         cost_estimate=pl.CostEstimate(flops=4 * rows * units * features, bytes_accessed=4 * units * features, transcendentals=0),
         name="first",
-    )(order, received, regroup, weights)
+    )(order, received, weights)
 
 
 def rest_kernel(order_ref, rows_ref, weight_ref, *out_refs):
@@ -151,45 +175,32 @@
     )(order, rows_in, weights)
 
 
-def down_kernel(hidden_ref, weight_ref, spread_ref, out_ref, total):
-    step = pl.program_id(0)
+def down_kernel(hidden_ref, weight_ref, out_ref):
     cols = out_ref.shape[1]
     span, slab = GROUP * BLOCK, GROUP * CAP
-    part = mm(hidden_ref[0], weight_ref[0])
-
-    @pl.when(step == 0)
-    def _():
-        total[...] = part
-
-    @pl.when(step > 0)
-    def _():
-        total[...] += part
-
-    @pl.when(step == pl.num_programs(0) - 1)
-    def _():
-        for g in range(out_ref.shape[0] // span):
-            block = total[g * slab : (g + 1) * slab, :].astype(BF16)
-            stacked = jnp.concatenate([block[:, q * cols : (q + 1) * cols] for q in range(QUARTERS)], axis=0)
-            out_ref[g * span : (g + 1) * span, :] = mm(spread_ref[...], stacked).astype(BF16)
+    total = mm(hidden_ref[0], weight_ref[0])
+    for k in range(1, hidden_ref.shape[0]):
+        total += mm(hidden_ref[k], weight_ref[k])
+    total = total.astype(BF16)
+    spread = regroup_matrix(True)
+    for g in range(out_ref.shape[0] // span):
+        block = total[g * slab : (g + 1) * slab, :]
+        stacked = jnp.concatenate([block[:, q * cols : (q + 1) * cols] for q in range(QUARTERS)], axis=0)
+        out_ref[g * span : (g + 1) * span, :] = mm(spread, stacked).astype(BF16)
 
 
 def down(hidden, weights):
     parts, rows, units = hidden.shape
-    features = weights.shape[2]
-    cols = features // QUARTERS
-    spread = jnp.asarray(regroup_code().T, BF16)
+    cols = weights.shape[2] // QUARTERS
+    vmem = pl.BlockSpec(memory_space=pltpu.VMEM)
     return pl.pallas_call(
         down_kernel,
         out_shape=jax.ShapeDtypeStruct((rows * QUARTERS, cols), BF16),
-        grid=(parts,),
-        in_specs=[pl.BlockSpec((1, rows, units), lambda i: (i, 0, 0)),
-                  pl.BlockSpec((1, units, features), lambda i: (i, 0, 0)),
-                  pl.BlockSpec(spread.shape, lambda i: (0, 0))],
-        out_specs=pl.BlockSpec((rows * QUARTERS, cols), lambda i: (0, 0)),
-        scratch_shapes=[pltpu.VMEM((rows, features), F32)],
-        compiler_params=PARAMS,
+        in_specs=[vmem, vmem],
+        out_specs=vmem,
+        compiler_params=pltpu.CompilerParams(vmem_limit_bytes=24 * 1024 * 1024),
         name="down",
-    )(hidden, weights, spread)
+    )(hidden, weights)
 
 
 def mixer_kernel(ids_ref, weight_ref, earlier_ref, expert_ref, slot_ref, quarter_ref, out_ref):

time: 186 us -> 180 us (0.968)
  local copies, waits for them, and re-layouts: 5.27 us -> 0.24 us
    unnamed x30 -> x16, local copies, waits for them, and re-layouts: 5.27 us -> 0.24 us
where the time goes in v2:
time: 180 us
  waiting for transfers between devices  94.7 us (53%)
  starting transfers between devices  44.1 us (24%)
  blocking collectives  20.9 us (12%)
  Pallas kernels  19.4 us (11%)
    all_to_all x1, waiting for transfers between devices, local(): lax.all_to_all(sent.reshape(flight, BLOCK, cols), 'ep', 0, 0, tiled=True)  38.3 us
    all_to_all x1, waiting for transfers between devices, local(): lax.all_to_all(result.reshape(flight, BLOCK, cols), 'ep', 0, 0, tiled=True)  31.8 us
    all_to_all x1, starting transfers between devices, local(): lax.all_to_all(sent.reshape(flight, BLOCK, cols), 'ep', 0, 0, tiled=True)  24.3 us
    all_gather x1, blocking collectives, local(): hidden = lax.all_gather(hidden, 'tp', axis=0, tiled=False)  20.9 us
    ppermute x1, waiting for transfers between devices, local(): got = lax.ppermute(pair_far, 'tp', far)  17 us
    all_to_all x1, starting transfers between devices, local(): lax.all_to_all(result.reshape(flight, BLOCK, cols), 'ep', 0, 0, tiled=True)  9.93 us
    ppermute x1, waiting for transfers between devices, local(): got_far = lax.ppermute(for_far, 'tp', near)  5.75 us
    pallas_call x1, Pallas kernels, rest_parts(): pl.pallas_call(rest_kernel, out_shape=(jax.ShapeDtypeStruct((rows, 2 * un...  5.11 us
  transfers between devices with their start and end apart: 5, of which 5 were waited for; matrix products, arithmetic and copies ran while one was open for 0% of the time, Pallas kernels for 4%

profile of v2, /device:TPU:56, one launch (start us, length us, event | category | flops | bytes accessed | tf_op | source)
XLA Modules:
  0.0 180.0 jit_solution(13472315079858106489)
XLA Ops:
  0.0 3.8 %pack.1 = bf16[1280,256]{1,0:T(8,128)(2,1)} custom-call(s32[8,128]{1,0:T(8,128)} %bitcast.19, bf16[128,1024]{1,0:T(8,128)(2,1)} %token_ref.1), custom_call_target="tpu_custom_call" | custom-call | tf_op jit(solution)/shard_map/pack/pallas_call | solution.py:101
  3.8 24.3 %all-to-all-start = ((bf16[32,40,256]{2,1,0:T(8,128)(2,1)}), bf16[32,40,256]{2,1,0:T(8,128)(2,1)S(1)}, u32[]{:S(2)}, u32[]{:S(2)}) async-start(bf16[32,40,256]{2,1,0:T(8,128)(2,1)} %bitcast.18), calls=%async_computation | async-start | bytes 1310720 | tf_op jit(solution)/shard_map/all_to_all | solution.py:274
  28.1 38.3 %all-to-all-done = bf16[32,40,256]{2,1,0:T(8,128)(2,1)S(1)} async-done(((bf16[32,40,256]{2,1,0:T(8,128)(2,1)}), bf16[32,40,256]{2,1,0:T(8,128)(2,1)S(1)}, u32[]{:S(2)}, u32[]{:S(2)}) %all-to-all-start) | async-done | bytes 655392 | tf_op jit(solution)/shard_map/all_to_all | solution.py:274
  66.4 2.8 %first.1 = (bf16[320,1024]{1,0:T(8,128)(2,1)S(1)}, bf16[320,768]{1,0:T(8,128)(2,1)S(1)}) custom-call(s32[1]{0:T(128)} %bitcast.3.order_ref, bf16[1280,256]{1,0:T(8,128)(2,1)S(1)} %bitcast.15, bf16[2,4,384,1024]{3,2,1,0:T(8,128)(2,1)} %bitcast.16), custom_call_target="tpu_custom_call" | custom-call | flops 503316480 | bytes 1572864 | tf_op jit(solution)/shard_map/first/pallas_call | solution.py:133
  69.1 2.3 %collective-permute-start = (bf16[320,768]{1,0:T(8,128)(2,1)S(1)}, bf16[320,768]{1,0:T(8,128)(2,1)S(1)}, u32[]{:S(2)}, u32[]{:S(2)}) collective-permute-start(bf16[320,768]{1,0:T(8,128)(2,1)S(1)} %get-tuple-element.14), channel_id=1, source_target_pairs={{0,1},{1,0},{2,3},{3,2},{4,5},{5,4},{6,7},{7,6},{8,9},{9,8},{10,11... | collective-permute-start | bytes 1474568 | tf_op jit(solution)/shard_map/ppermute | solution.py:277
  71.5 0.1 pad_add_fusion.order_ref
  71.6 5.1 %rest.1 = (bf16[320,768]{1,0:T(8,128)(2,1)S(1)}, bf16[320,768]{1,0:T(8,128)(2,1)S(1)}, bf16[320,768]{1,0:T(8,128)(2,1)S(1)}) custom-call(s32[3]{0:T(128)S(1)} %pad_add_fusion.order_ref, bf16[320,1024]{1,0:T(8,128)(2,1)S(1)} %get-tuple-element.12.rows_ref, bf16[2,4,384,1024]{3,2,1,0:T(8,128)(2,1)} %bitcast.17), custom_call_target="tpu_custom_call" | custom-call | flops 1509949440 | bytes 4718592 | tf_op jit(solution)/shard_map/rest/pallas_call | solution.py:162
  76.7 5.7 %collective-permute-done = bf16[320,768]{1,0:T(8,128)(2,1)S(1)} collective-permute-done((bf16[320,768]{1,0:T(8,128)(2,1)S(1)}, bf16[320,768]{1,0:T(8,128)(2,1)S(1)}, u32[]{:S(2)}, u32[]{:S(2)}) %collective-permute-start) | collective-permute-done | bytes 491552 | tf_op jit(solution)/shard_map/ppermute | solution.py:277
  82.4 0.1 add_convert_fusion
  82.6 4.3 %collective-permute-start.1 = (bf16[320,768]{1,0:T(8,128)(2,1)S(1)}, bf16[320,768]{1,0:T(8,128)(2,1)S(1)}, u32[]{:S(2)}, u32[]{:S(2)}) collective-permute-start(bf16[320,768]{1,0:T(8,128)(2,1)S(1)} %add_convert_fusion), channel_id=1, source_target_pairs={{0,2},{1,3},{2,0},{3,1},{4,6},{5,7},{6,4},{7,5},{8,10},{9,11},{10,... | collective-permute-start | bytes 1474568 | tf_op jit(solution)/shard_map/ppermute | solution.py:281
  86.9 3.3 %collective-permute-start.2 = (bf16[320,768]{1,0:T(8,128)(2,1)S(1)}, bf16[320,768]{1,0:T(8,128)(2,1)S(1)}, u32[]{:S(2)}, u32[]{:S(2)}) collective-permute-start(bf16[320,768]{1,0:T(8,128)(2,1)S(1)} %get-tuple-element.17), channel_id=1, source_target_pairs={{0,1},{1,0},{2,3},{3,2},{4,5},{5,4},{6,7},{7,6},{8,9},{9,8},{10,11... | collective-permute-start | bytes 1474568 | tf_op jit(solution)/shard_map/ppermute | solution.py:282
  90.1 17.0 %collective-permute-done.1 = bf16[320,768]{1,0:T(8,128)(2,1)S(1)} collective-permute-done((bf16[320,768]{1,0:T(8,128)(2,1)S(1)}, bf16[320,768]{1,0:T(8,128)(2,1)S(1)}, u32[]{:S(2)}, u32[]{:S(2)}) %collective-permute-start.1) | collective-permute-done | bytes 491552 | tf_op jit(solution)/shard_map/ppermute | solution.py:281
  107.2 1.9 %collective-permute-done.2 = bf16[320,768]{1,0:T(8,128)(2,1)S(1)} collective-permute-done((bf16[320,768]{1,0:T(8,128)(2,1)S(1)}, bf16[320,768]{1,0:T(8,128)(2,1)S(1)}, u32[]{:S(2)}, u32[]{:S(2)}) %collective-permute-start.2) | collective-permute-done | bytes 491552 | tf_op jit(solution)/shard_map/ppermute | solution.py:282
  109.0 0.2 convert_add_fusion
  109.2 0.1 fusion
  109.4 20.9 %all-gather = bf16[1280,384]{1,0:T(8,128)(2,1)S(1)} all-gather(bf16[320,384]{1,0:T(8,128)(2,1)S(1)} %fusion), channel_id=2, replica_groups=mesh['dp'=8,'ep'=32,'tp'=4] {'tp'}, dimensions={0}, use_global_device_ids=true | all-gather | bytes 1228800 | tf_op jit(solution)/shard_map/all_gather | solution.py:285
  130.3 0.0 copy-start.3
  130.3 2.8 %down.1 = bf16[1280,256]{1,0:T(8,128)(2,1)} custom-call(bf16[4,320,384]{2,1,0:T(8,128)(2,1)S(1)} %bitcast.12, bf16[4,384,1024]{2,1,0:T(8,128)(2,1)S(1)} %bitcast.13), custom_call_target="tpu_custom_call" | custom-call | tf_op jit(solution)/shard_map/down/pallas_call | solution.py:196
  133.1 9.9 %all-to-all-start.1 = ((bf16[32,40,256]{2,1,0:T(8,128)(2,1)}), bf16[32,40,256]{2,1,0:T(8,128)(2,1)S(1)}, u32[]{:S(2)}, u32[]{:S(2)}) async-start(bf16[32,40,256]{2,1,0:T(8,128)(2,1)} %bitcast.10), calls=%async_computation.1 | async-start | bytes 1310720 | tf_op jit(solution)/shard_map/all_to_all | solution.py:288
  143.1 0.1 copy.10.ids_ref
  143.2 0.1 copy.11.weight_ref
  143.3 2.9 %mixer.1.mixer_ref = bf16[512,1280]{1,0:T(8,128)(2,1)S(1)} custom-call(s32[128,8]{1,0:T(8,128)S(1)} %copy.10.ids_ref, f32[128,8]{1,0:T(8,128)S(1)} %copy.11.weight_ref, bf16[128,128]{1,0:T(8,128)(2,1)S(1)} %copy-done.4, bf16[32,1280]{1,0:T(8,128)(2,1)S(1)} %copy-done.2, bf16[16,1280]{1,0:T(8,128)(2,1)S(1)} %copy-done.3, bf16[512,16]{1,0:T(8,128)(2,1)S(1)} %copy-done.1), custom_call_target="tpu_custom_call" | custom-call | tf_op jit(solution)/shard_map/mixer/pallas_call | solution.py:230
  146.2 31.8 %all-to-all-done.1 = bf16[32,40,256]{2,1,0:T(8,128)(2,1)S(1)} async-done(((bf16[32,40,256]{2,1,0:T(8,128)(2,1)}), bf16[32,40,256]{2,1,0:T(8,128)(2,1)S(1)}, u32[]{:S(2)}, u32[]{:S(2)}) %all-to-all-start.1) | async-done | bytes 655392 | tf_op jit(solution)/shard_map/all_to_all | solution.py:288
  178.0 2.0 %combine.1 = bf16[128,1024]{1,0:T(8,128)(2,1)} custom-call(bf16[512,1280]{1,0:T(8,128)(2,1)S(1)} %mixer.1.mixer_ref, bf16[1280,256]{1,0:T(8,128)(2,1)S(1)} %bitcast.14), custom_call_target="tpu_custom_call" | custom-call | tf_op jit(solution)/shard_map/combine/pallas_call | solution.py:249
  (13 shorter events, 0.0 us)
Async XLA Ops:
  3.8 62.6 %all-to-all-start = ((bf16[32,40,256]{2,1,0:T(8,128)(2,1)}), bf16[32,40,256]{2,1,0:T(8,128)(2,1)S(1)}, u32[]{:S(2)}, u32[]{:S(2)}) async-start(bf16[32,40,256]{2,1,0:T(8,128)(2,1)} %bitcast.18), calls=%async_computation | async-start | bytes 1310720 | tf_op jit(solution)/shard_map/all_to_all | solution.py:274
  69.1 13.3 %collective-permute-start = (bf16[320,768]{1,0:T(8,128)(2,1)S(1)}, bf16[320,768]{1,0:T(8,128)(2,1)S(1)}, u32[]{:S(2)}, u32[]{:S(2)}) collective-permute-start(bf16[320,768]{1,0:T(8,128)(2,1)S(1)} %get-tuple-element.14), channel_id=1, source_target_pairs={{0,1},{1,0},{2,3},{3,2},{4,5},{5,4},{6,7},{7,6},{8,9},{9,8},{10,11... | collective-permute-start | bytes 1474568 | tf_op jit(solution)/shard_map/ppermute | solution.py:277
  82.4 47.9 %copy-start = (bf16[1,1536,1024]{2,1,0:T(8,128)(2,1)S(1)}, bf16[1,1536,1024]{2,1,0:T(8,128)(2,1)}, u32[]{:S(2)}) copy-start(bf16[1,1536,1024]{2,1,0:T(8,128)(2,1)} %param.13) | copy-start | bytes 9437188
  82.6 24.6 %collective-permute-start.1 = (bf16[320,768]{1,0:T(8,128)(2,1)S(1)}, bf16[320,768]{1,0:T(8,128)(2,1)S(1)}, u32[]{:S(2)}, u32[]{:S(2)}) collective-permute-start(bf16[320,768]{1,0:T(8,128)(2,1)S(1)} %add_convert_fusion), channel_id=1, source_target_pairs={{0,2},{1,3},{2,0},{3,1},{4,6},{5,7},{6,4},{7,5},{8,10},{9,11},{10,... | collective-permute-start | bytes 1474568 | tf_op jit(solution)/shard_map/ppermute | solution.py:281
  86.9 22.2 %collective-permute-start.2 = (bf16[320,768]{1,0:T(8,128)(2,1)S(1)}, bf16[320,768]{1,0:T(8,128)(2,1)S(1)}, u32[]{:S(2)}, u32[]{:S(2)}) collective-permute-start(bf16[320,768]{1,0:T(8,128)(2,1)S(1)} %get-tuple-element.17), channel_id=1, source_target_pairs={{0,1},{1,0},{2,3},{3,2},{4,5},{5,4},{6,7},{7,6},{8,9},{9,8},{10,11... | collective-permute-start | bytes 1474568 | tf_op jit(solution)/shard_map/ppermute | solution.py:282
  130.3 12.8 %copy-start.5 = (s32[128,8]{0,1:T(8,128)S(1)}, s32[128,8]{0,1:T(8,128)}, u32[]{:S(2)}) copy-start(s32[128,8]{0,1:T(8,128)} %param.10) | copy-start | bytes 12292
  130.3 12.9 %copy-start.6 = (f32[128,8]{0,1:T(8,128)S(1)}, f32[128,8]{0,1:T(8,128)}, u32[]{:S(2)}) copy-start(f32[128,8]{0,1:T(8,128)} %param.11) | copy-start | bytes 12292
  130.3 13.0 %copy-start.1 = (bf16[512,16]{1,0:T(8,128)(2,1)S(1)}, bf16[512,16]{1,0:T(8,128)(2,1)}, u32[]{:S(2)}) copy-start(bf16[512,16]{1,0:T(8,128)(2,1)} %constant.24.clone.quarter_ref) | copy-start | bytes 49156
  130.3 13.0 %copy-start.2 = (bf16[32,1280]{1,0:T(8,128)(2,1)S(1)}, bf16[32,1280]{1,0:T(8,128)(2,1)}, u32[]{:S(2)}) copy-start(bf16[32,1280]{1,0:T(8,128)(2,1)} %constant.22.clone.expert_ref) | copy-start | bytes 245764
  130.3 13.0 %copy-start.3 = (bf16[16,1280]{1,0:T(8,128)(2,1)S(1)}, bf16[16,1280]{1,0:T(8,128)(2,1)}, u32[]{:S(2)}) copy-start(bf16[16,1280]{1,0:T(8,128)(2,1)} %constant.23.clone.slot_ref) | copy-start | bytes 122884
  130.3 13.0 %copy-start.4 = (bf16[128,128]{1,0:T(8,128)(2,1)S(1)}, bf16[128,128]{1,0:T(8,128)(2,1)}, u32[]{:S(2)}) copy-start(bf16[128,128]{1,0:T(8,128)(2,1)} %constant.21.clone.earlier_ref) | copy-start | bytes 98308
  133.1 44.9 %all-to-all-start.1 = ((bf16[32,40,256]{2,1,0:T(8,128)(2,1)}), bf16[32,40,256]{2,1,0:T(8,128)(2,1)S(1)}, u32[]{:S(2)}, u32[]{:S(2)}) async-start(bf16[32,40,256]{2,1,0:T(8,128)(2,1)} %bitcast.10), calls=%async_computation.1 | async-start | bytes 1310720 | tf_op jit(solution)/shard_map/all_to_all | solution.py:288

commit v3 on v2

--- a/solution.py
+++ b/solution.py
@@ -2,7 +2,6 @@
 
 import jax
 import jax.numpy as jnp
-import numpy as np
 from jax import lax
 from jax.experimental import pallas as pl
 from jax.experimental.pallas import tpu as pltpu
@@ -17,6 +16,7 @@
 PARAMS = pltpu.CompilerParams(vmem_limit_bytes=48 * 1024 * 1024)
 BLOCK = QUARTERS * CAP
 GROUP = 8
+HALVES = 2
 
 
 def mm(a, b):
@@ -25,24 +25,6 @@
 
 def mm_t(a, b):
     return lax.dot_general(a, b, (((1,), (1,)), ((), ())), preferred_element_type=F32)
-
-
-def place_code(flight):
-    rows = np.arange(flight * BLOCK)
-    expert, quarter, slot = rows // BLOCK, rows // CAP % QUARTERS, rows % CAP
-    code = np.zeros((rows.size, flight + 16), np.float32)
-    code[rows, expert] = 1
-    code[:, flight] = -slot
-    code[rows, flight + 1 + quarter] = APART
-    return code
-
-
-def quarter_code(rows):
-    code = np.zeros((16, QUARTERS * rows), np.float32)
-    code[0] = 1
-    for quarter in range(QUARTERS):
-        code[1 + quarter] = np.arange(QUARTERS * rows) // rows != quarter
-    return code
 
 
 def counter(shape, dim):
@@ -68,7 +50,7 @@
     return jnp.where(counter((span, span), 1) == column, 1.0, 0.0).astype(BF16)
 
 
-def pack_kernel(flight, ids_ref, token_ref, out_ref):
+def pack_kernel(flight, which_ref, ids_ref, token_ref, out_ref):
     top, rows = ids_ref.shape
     places, cols = out_ref.shape
     expert = lax.broadcasted_iota(jnp.int32, (flight, rows), 0)
@@ -82,7 +64,8 @@
     other = [jnp.where((line <= QUARTERS) & (line != q + 1), 1.0, 0.0) for q in range(QUARTERS)]
     code = jnp.concatenate([jnp.concatenate([slot, o], axis=0) for o in other], axis=1).astype(BF16)
     place = counter((places, 1), 0) + (pl.program_id(0) * places).astype(F32)
-    owner, rest = split(place, BLOCK)
+    pair, rest = split(place, BLOCK)
+    owner = HALVES * pair + which_ref[0].astype(F32)
     quarter, place_slot = split(rest, CAP)
     column = counter((places, flight + 16), 1)
     place_code = jnp.where(column == owner, 1.0, 0.0) + jnp.where(column == flight, -place_slot, 0.0)
@@ -93,20 +76,23 @@
     out_ref[...] = mm(selector, stacked).astype(BF16)
 
 
-def pack(ids_t, tokens, flight):
+def pack(which, ids_t, tokens, flight):
     rows, features = tokens.shape
-    places = flight * BLOCK
-    steps = 4
-    whole = lambda a: pl.BlockSpec(a.shape, lambda i: (0, 0))
+    places = flight // HALVES * BLOCK
+    steps = 2
+    whole = lambda a: pl.BlockSpec(a.shape, lambda i, which: (0, 0))
     return pl.pallas_call(
         functools.partial(pack_kernel, flight),
         out_shape=jax.ShapeDtypeStruct((places, features // QUARTERS), BF16),
-        grid=(steps,),
-        in_specs=[whole(ids_t), whole(tokens)],
-        out_specs=pl.BlockSpec((places // steps, features // QUARTERS), lambda i: (i, 0)),
+        grid_spec=pltpu.PrefetchScalarGridSpec(
+            num_scalar_prefetch=1,
+            grid=(steps,),
+            in_specs=[whole(ids_t), whole(tokens)],
+            out_specs=pl.BlockSpec((places // steps, features // QUARTERS), lambda i, which: (i, 0)),
+        ),
         compiler_params=pltpu.CompilerParams(vmem_limit_bytes=60 * 1024 * 1024),
         name="pack",
-    )(ids_t, tokens)
+    )(which, ids_t, tokens)
 
 
 def first_kernel(order_ref, x_ref, weight_ref, rows_ref, out_ref):
@@ -175,12 +161,13 @@
     )(order, rows_in, weights)
 
 
-def down_kernel(hidden_ref, weight_ref, out_ref):
+def down_kernel(order_ref, *refs):
+    *hidden_refs, weight_ref, out_ref = refs
     cols = out_ref.shape[1]
     span, slab = GROUP * BLOCK, GROUP * CAP
-    total = mm(hidden_ref[0], weight_ref[0])
-    for k in range(1, hidden_ref.shape[0]):
-        total += mm(hidden_ref[k], weight_ref[k])
+    total = mm(hidden_refs[0][...], weight_ref[order_ref[0]])
+    for k in range(1, len(hidden_refs)):
+        total += mm(hidden_refs[k][...], weight_ref[order_ref[k]])
     total = total.astype(BF16)
     spread = regroup_matrix(True)
     for g in range(out_ref.shape[0] // span):
@@ -189,23 +176,24 @@
         out_ref[g * span : (g + 1) * span, :] = mm(spread, stacked).astype(BF16)
 
 
-def down(hidden, weights):
-    parts, rows, units = hidden.shape
+def down(order, hidden, weights):
+    rows = hidden[0].shape[0]
     cols = weights.shape[2] // QUARTERS
     vmem = pl.BlockSpec(memory_space=pltpu.VMEM)
     return pl.pallas_call(
         down_kernel,
         out_shape=jax.ShapeDtypeStruct((rows * QUARTERS, cols), BF16),
-        in_specs=[vmem, vmem],
+        in_specs=[pl.BlockSpec(memory_space=pltpu.SMEM)] + [vmem] * (len(hidden) + 1),
         out_specs=vmem,
         compiler_params=pltpu.CompilerParams(vmem_limit_bytes=24 * 1024 * 1024),
+        cost_estimate=pl.CostEstimate(flops=2 * rows * weights.size, bytes_accessed=2 * weights.size, transcendentals=0),
         name="down",
-    )(hidden, weights)
-
-
-def mixer_kernel(ids_ref, weight_ref, earlier_ref, expert_ref, slot_ref, quarter_ref, out_ref):
+    )(order, *hidden, weights)
+
+
+def mixer_kernel(flight, half_ref, ids_ref, weight_ref, out_ref):
     rows, top = ids_ref.shape
-    flight = expert_ref.shape[0]
+    places = out_ref.shape[1]
     expert = lax.broadcasted_iota(jnp.int32, (rows, flight), 1)
     named = jnp.zeros((rows, flight), F32)
     weight = jnp.zeros((rows, flight), F32)
@@ -213,48 +201,62 @@
         hit = ids_ref[:, k : k + 1] == expert
         named += jnp.where(hit, 1.0, 0.0)
         weight += jnp.where(hit, weight_ref[:, k : k + 1], 0.0)
-    slot = mm(earlier_ref[...], named.astype(BF16))
+    earlier = jnp.where(counter((rows, rows), 1) < counter((rows, rows), 0), 1.0, 0.0).astype(BF16)
+    slot = mm(earlier, named.astype(BF16))
     slot = jnp.where(named > 0, slot, FAR).astype(BF16)
-    gap = mm(slot, expert_ref[...]) + mm(quarter_ref[...], slot_ref[...])
-    out_ref[...] = jnp.where(gap == 0, mm(weight.astype(BF16), expert_ref[...]), 0.0).astype(BF16)
-
-
-def mixer(ids, weight, flight):
+
+    part, rest = split(counter((1, places), 1), places // HALVES)
+    pair, rest = split(rest, BLOCK)
+    quarter, place_slot = split(rest, CAP)
+    half = half_ref[0].astype(F32)
+    owner = HALVES * pair + jnp.where(part == 0, half, HALVES - 1 - half)
+    owned = jnp.where(counter((flight, places), 0) == owner, 1.0, 0.0).astype(BF16)
+    here = quarter == pl.program_id(0).astype(F32)
+    gap = mm(slot, owned) - jnp.where(here, place_slot, -1.0)
+    out_ref[...] = jnp.where(gap == 0, mm(weight.astype(BF16), owned), 0.0).astype(BF16)
+
+
+def mixer(half, ids, weight, flight):
     rows = ids.shape[0]
     places = flight * BLOCK
-    code = place_code(flight).T
-    earlier = jnp.asarray(np.tril(np.ones((rows, rows), np.float32), -1), BF16)
-    expert, slot = jnp.asarray(code[:flight], BF16), jnp.asarray(code[flight:], BF16)
-    quarter = jnp.asarray(quarter_code(rows).T, BF16)
-    whole = lambda a: pl.BlockSpec(a.shape, lambda i: (0, 0))
-    return pl.pallas_call(
-        mixer_kernel,
+    whole = lambda a: pl.BlockSpec(a.shape, lambda i, half: (0, 0))
+    return pl.pallas_call(
+        functools.partial(mixer_kernel, flight),
         out_shape=jax.ShapeDtypeStruct((QUARTERS * rows, places), BF16),
-        grid=(QUARTERS,),
-        in_specs=[whole(ids), whole(weight), whole(earlier), whole(expert), whole(slot),
-                  pl.BlockSpec((rows, 16), lambda i: (i, 0))],
-        out_specs=pl.BlockSpec((rows, places), lambda i: (i, 0)),
-        compiler_params=PARAMS,
+        grid_spec=pltpu.PrefetchScalarGridSpec(
+            num_scalar_prefetch=1,
+            grid=(QUARTERS,),
+            in_specs=[whole(ids), whole(weight)],
+            out_specs=pl.BlockSpec((rows, places), lambda i, half: (i, 0)),
+        ),
+        compiler_params=pltpu.CompilerParams(vmem_limit_bytes=24 * 1024 * 1024),
         name="mixer",
-    )(ids, weight, earlier, expert, slot, quarter)
-
-
-def combine_kernel(mixer_ref, returned_ref, out_ref):
-    out_ref[...] = mm(mixer_ref[...], returned_ref[...]).astype(BF16)
-
-
-def combine(mix, returned):
-    places, cols = returned.shape
+    )(half, ids, weight)
+
+
+def combine_kernel(mixer_ref, same_ref, other_ref, out_ref):
+    places = same_ref.shape[0]
+    total = mm(mixer_ref[:, :places], same_ref[...]) + mm(mixer_ref[:, places:], other_ref[...])
+    out_ref[...] = total.astype(BF16)
+
+
+def combine(mix, same, other):
+    places, cols = same.shape
     rows = mix.shape[0] // QUARTERS
+    returned = pl.BlockSpec((places, cols), lambda i: (0, 0))
     return pl.pallas_call(
         combine_kernel,
         out_shape=jax.ShapeDtypeStruct((rows, QUARTERS * cols), BF16),
         grid=(QUARTERS,),
-        in_specs=[pl.BlockSpec((rows, places), lambda i: (i, 0)), pl.BlockSpec((places, cols), lambda i: (0, 0))],
+        in_specs=[pl.BlockSpec((rows, mix.shape[1]), lambda i: (i, 0)), returned, returned],
         out_specs=pl.BlockSpec((rows, cols), lambda i: (0, i)),
-        compiler_params=PARAMS,
+        compiler_params=pltpu.CompilerParams(vmem_limit_bytes=24 * 1024 * 1024),
         name="combine",
-    )(mix, returned)
+    )(mix, same, other)
+
+
+def tie(*values):
+    return lax.optimization_barrier(values)
 
 
 def local(tokens, expert_ids, route_weight, gate_up, down_proj):
@@ -266,28 +268,69 @@
     up_weights = gate_up.reshape(2, n_tp, units, features)
     down_weights = down_proj.reshape(n_tp, units, features)
     me = lax.axis_index("tp")
+    half = lax.axis_index("ep") % HALVES
     order = jnp.stack([me ^ 3, me ^ 1, me ^ 2, me]).astype(jnp.int32)
+    same_half = jnp.stack([half]).astype(jnp.int32)
+    other_half = jnp.stack([1 - half]).astype(jnp.int32)
     near = [(i, i ^ 1) for i in range(n_tp)]
     far = [(i, i ^ 2) for i in range(n_tp)]
-
-    sent = pack(expert_ids.T, tokens, flight)
-    received = lax.all_to_all(sent.reshape(flight, BLOCK, cols), "ep", 0, 0, tiled=True).reshape(flight * BLOCK, cols)
-
-    row_block, for_far = first_part(order[:1], received, up_weights)
+    cross = [(i, i ^ 3) for i in range(n_tp)]
+    lines = [list(range(h, flight, HALVES)) for h in range(HALVES)]
+    swap = [(i, i ^ 1) for i in range(flight)]
+
+    def exchange(rows):
+        blocks = rows.reshape(flight // HALVES, BLOCK, cols)
+        return lax.all_to_all(blocks, "ep", 0, 0, axis_index_groups=lines, tiled=True).reshape(rows.shape)
+
+    def swapped(rows):
+        return lax.ppermute(rows, "ep", swap)
+
+    def pair_sum(got_far, keep_far):
+        return (got_far.astype(F32) + keep_far.astype(F32)).astype(BF16)
+
+    def activated(got, got_near, keep):
+        summed = got.astype(F32) + got_near.astype(F32) + keep.astype(F32)
+        return (jax.nn.silu(summed[:, :units]) * summed[:, units:]).astype(BF16)
+
+    def gathered(hidden):
+        return [lax.ppermute(hidden, "tp", pairs) for pairs in (cross, near, far)] + [hidden]
+
+    for_other = pack(other_half, expert_ids.T, tokens, flight)
+    crossed = swapped(for_other)
+    for_same = pack(same_half, expert_ids.T, tokens, flight)
+    received = exchange(for_same)
+    received, crossed = tie(received, crossed)
+    received_2 = exchange(crossed)
+
+    rows, for_far = first_part(order[:1], received, up_weights)
     got_far = lax.ppermute(for_far, "tp", near)
-    for_near, keep_far, keep = rest_parts(order[1:], row_block, up_weights, 3)
-    pair_far = (got_far.astype(F32) + keep_far.astype(F32)).astype(BF16)
-    for_near, pair_far = lax.optimization_barrier((for_near, pair_far))
+    for_near, keep_far, keep = rest_parts(order[1:], rows, up_weights, 3)
+    pair_far, for_near = tie(pair_sum(got_far, keep_far), for_near)
     got = lax.ppermute(pair_far, "tp", far)
     got_near = lax.ppermute(for_near, "tp", near)
-    summed = got.astype(F32) + got_near.astype(F32) + keep.astype(F32)
-    hidden = (jax.nn.silu(summed[:, :units]) * summed[:, units:]).astype(BF16)
-    hidden = lax.all_gather(hidden, "tp", axis=0, tiled=False)
-
-    result = down(hidden, down_weights)
-    returned = lax.all_to_all(result.reshape(flight, BLOCK, cols), "ep", 0, 0, tiled=True).reshape(flight * BLOCK, cols)
-    mix = mixer(expert_ids, route_weight, flight)
-    return combine(mix, returned)
+
+    received_2, pair_far = tie(received_2, pair_far)
+    rows_2, for_far_2 = first_part(order[:1], received_2, up_weights)
+    got_far_2 = lax.ppermute(for_far_2, "tp", near)
+    for_near_2, keep_far_2, keep_2 = rest_parts(order[1:], rows_2, up_weights, 3)
+
+    got, got_near, keep, keep_2 = tie(got, got_near, keep, keep_2)
+    parts = gathered(activated(got, got_near, keep))
+    pair_far_2, for_near_2 = tie(pair_sum(got_far_2, keep_far_2), for_near_2)
+    got_2 = lax.ppermute(pair_far_2, "tp", far)
+    got_near_2 = lax.ppermute(for_near_2, "tp", near)
+
+    parts, pair_far_2 = tie(parts, pair_far_2)
+    result = down(order, parts, down_weights)
+    returned = exchange(result)
+    got_2, got_near_2, result = tie(got_2, got_near_2, result)
+    parts_2 = gathered(activated(got_2, got_near_2, keep_2))
+    result_2 = down(order, parts_2, down_weights)
+    result_2, returned = tie(result_2, returned)
+    returned_2 = swapped(exchange(result_2))
+    result_2, ids, weight = tie(result_2, expert_ids, route_weight)
+    mix = mixer(same_half, ids, weight, flight)
+    return combine(mix, returned, returned_2)
 
 
 def solution(mesh):

time: 180 us -> 200 us (1.11); the launches traced: 180 us -> 197 us
  waiting for transfers between devices: 94.7 us -> 45.3 us
  starting transfers between devices: 44.1 us -> 89 us
  Pallas kernels: 19.4 us -> 30.4 us
  blocking collectives: 20.9 us -> 28.4 us
  other arithmetic: 0.5 us -> 3.12 us
    all_to_all x2 -> x3, waiting for transfers between devices: 70 us -> 1.82 us  [exchange(): lax.all_to_all(blocks, 'ep', 0, 0, axis_index_groups=lines, tiled=True)]
    ppermute x0 -> x11, waiting for transfers between devices: none -> 42.9 us  [the longest x2 26.8 us: swapped(): return lax.ppermute(rows, 'ep', swap)]
    ppermute x0 -> x11, starting transfers between devices: none -> 37.9 us  [the longest x6 20.2 us: gathered(): lax.ppermute(hidden, 'tp', pairs)]
    all_to_all x0 -> x1, blocking collectives: none -> 28.4 us  [exchange(): lax.all_to_all(blocks, 'ep', 0, 0, axis_index_groups=lines, tiled=True)]
    all_gather x1 -> x0, blocking collectives: 20.9 us -> none  [local(): hidden = lax.all_gather(hidden, 'tp', axis=0, tiled=False)]
    ppermute x1, waiting for transfers between devices: 17 us -> 0.01 us  [local(): got = lax.ppermute(pair_far, 'tp', far)]
    all_to_all x2 -> x3, starting transfers between devices: 34.2 us -> 41.6 us  [exchange(): lax.all_to_all(blocks, 'ep', 0, 0, axis_index_groups=lines, tiled=True)]
    pallas_call x1 -> x2, Pallas kernels: 5.11 us -> 10.3 us  [rest_parts(): pl.pallas_call(rest_kernel, out_shape=(jax.ShapeDtypeStruct((rows, 2 * un...]
  transfers between devices with their start and end apart: 5 -> 17, of which waited for: 5 -> 9; matrix products, arithmetic and copies ran while one was open for 0% -> 2% of each run, Pallas kernels for 4% -> 11%
where the time goes in v3:
time: 200 us; the launch traced here: 197 us
  starting transfers between devices  89 us (44%)
  waiting for transfers between devices  45.3 us (23%)
  Pallas kernels  30.4 us (15%)
  blocking collectives  28.4 us (14%)
  other arithmetic  3.12 us (2%)
    all_to_all x3, starting transfers between devices, exchange(): lax.all_to_all(blocks, 'ep', 0, 0, axis_index_groups=lines, tiled=True)  41.6 us
    all_to_all x1, blocking collectives, exchange(): lax.all_to_all(blocks, 'ep', 0, 0, axis_index_groups=lines, tiled=True)  28.4 us
    ppermute x2, waiting for transfers between devices, swapped(): return lax.ppermute(rows, 'ep', swap)  26.8 us
    ppermute x6, starting transfers between devices, gathered(): lax.ppermute(hidden, 'tp', pairs)  20.2 us
    pallas_call x2, Pallas kernels, rest_parts(): pl.pallas_call(rest_kernel, out_shape=(jax.ShapeDtypeStruct((rows, 2 * un...  10.3 us
    ppermute x2, starting transfers between devices, swapped(): return lax.ppermute(rows, 'ep', swap)  8.39 us
    ppermute x6, waiting for transfers between devices, gathered(): lax.ppermute(hidden, 'tp', pairs)  6.4 us
    ppermute x1, waiting for transfers between devices, local(): got_2 = lax.ppermute(pair_far_2, 'tp', far)  5.9 us
  transfers between devices with their start and end apart: 17, of which 9 were waited for; matrix products, arithmetic and copies ran while one was open for 2% of the time, Pallas kernels for 11%

profile of v3, /device:TPU:56, one launch (start us, length us, event | category | flops | bytes accessed | tf_op | source)
XLA Modules:
  0.0 196.8 jit_solution(13185878344840179981)
XLA Ops:
  0.0 2.6 %pack.2 = bf16[640,256]{1,0:T(8,128)(2,1)} custom-call(s32[1]{0:T(128)} %bitcast.which_ref.half_ref, s32[8,128]{1,0:T(8,128)} %bitcast.28, bf16[128,1024]{1,0:T(8,128)(2,1)} %token_ref.3), custom_call_target="tpu_custom_call" | custom-call | tf_op jit(solution)/shard_map/pack/pallas_call | solution.py:84
  2.6 18.9 %all-to-all-start = ((bf16[16,40,256]{2,1,0:T(8,128)(2,1)}), bf16[16,40,256]{2,1,0:T(8,128)(2,1)S(1)}, u32[]{:S(2)}, u32[]{:S(2)}) async-start(bf16[16,40,256]{2,1,0:T(8,128)(2,1)} %bitcast.26), calls=%async_computation | async-start | bytes 655360 | tf_op jit(solution)/shard_map/all_to_all | solution.py:283
  21.5 2.7 %pack.3 = bf16[640,256]{1,0:T(8,128)(2,1)} custom-call(s32[1]{0:T(128)} %bitcast.8.which_ref, s32[8,128]{1,0:T(8,128)} %bitcast.29, bf16[128,1024]{1,0:T(8,128)(2,1)} %token_ref.3), custom_call_target="tpu_custom_call" | custom-call | tf_op jit(solution)/shard_map/pack/pallas_call | solution.py:84
  24.2 4.7 %collective-permute-start = (bf16[640,256]{1,0:T(8,128)(2,1)}, bf16[640,256]{1,0:T(8,128)(2,1)}, u32[]{:S(2)}, u32[]{:S(2)}) collective-permute-start(bf16[640,256]{1,0:T(8,128)(2,1)} %pack.3), channel_id=1, source_target_pairs={{0,4},{4,0},{8,12},{12,8},{16,20},{20,16},{24,28},{28,24},{32,36},... | collective-permute-start | bytes 983048 | tf_op jit(solution)/shard_map/ppermute | solution.py:286
  28.9 17.5 %collective-permute-done = bf16[640,256]{1,0:T(8,128)(2,1)} collective-permute-done((bf16[640,256]{1,0:T(8,128)(2,1)}, bf16[640,256]{1,0:T(8,128)(2,1)}, u32[]{:S(2)}, u32[]{:S(2)}) %collective-permute-start) | collective-permute-done | bytes 327712 | tf_op jit(solution)/shard_map/ppermute | solution.py:286
  46.4 11.7 %all-to-all-start.1 = ((bf16[16,40,256]{2,1,0:T(8,128)(2,1)}), bf16[16,40,256]{2,1,0:T(8,128)(2,1)S(1)}, u32[]{:S(2)}, u32[]{:S(2)}) async-start(bf16[16,40,256]{2,1,0:T(8,128)(2,1)} %bitcast.9), calls=%async_computation.1 | async-start | bytes 655360 | tf_op jit(solution)/shard_map/all_to_all | solution.py:283
  60.5 3.2 %collective-permute-start.1 = (bf16[160,768]{1,0:T(8,128)(2,1)S(1)}, bf16[160,768]{1,0:T(8,128)(2,1)S(1)}, u32[]{:S(2)}, u32[]{:S(2)}) collective-permute-start(bf16[160,768]{1,0:T(8,128)(2,1)S(1)} %get-tuple-element.38), channel_id=1, source_target_pairs={{0,1},{1,0},{2,3},{3,2},{4,5},{5,4},{6,7},{7,6},{8,9},{9,8},{10,11... | collective-permute-start | bytes 737288 | tf_op jit(solution)/shard_map/ppermute | solution.py:306
  63.8 5.3 %rest.2 = (bf16[160,768]{1,0:T(8,128)(2,1)}, bf16[160,768]{1,0:T(8,128)(2,1)S(1)}, bf16[160,768]{1,0:T(8,128)(2,1)S(1)}) custom-call(s32[3]{0:T(128)S(1)} %pad_add_fusion.1.order_ref, bf16[160,1024]{1,0:T(8,128)(2,1)S(1)} %get-tuple-element.39.rows_ref, bf16[2,4,384,1024]{3,2,1,0:T(8,128)(2,1)} %bitcast.23), custom_call_target="tpu_custom_call" | custom-call | flops 754974720 | bytes 4718592 | tf_op jit(solution)/shard_map/rest/pallas_call | solution.py:148
  72.7 4.1 %collective-permute-start.5 = (bf16[160,768]{1,0:T(8,128)(2,1)}, bf16[160,768]{1,0:T(8,128)(2,1)}, u32[]{:S(2)}, u32[]{:S(2)}) collective-permute-start(bf16[160,768]{1,0:T(8,128)(2,1)} %add_convert_fusion.1), channel_id=1, source_target_pairs={{0,2},{1,3},{2,0},{3,1},{4,6},{5,7},{6,4},{7,5},{8,10},{9,11},{10,... | collective-permute-start | bytes 737288 | tf_op jit(solution)/shard_map/ppermute | solution.py:309
  83.3 5.0 %rest.3 = (bf16[160,768]{1,0:T(8,128)(2,1)S(1)}, bf16[160,768]{1,0:T(8,128)(2,1)S(1)}, bf16[160,768]{1,0:T(8,128)(2,1)S(1)}) custom-call(s32[3]{0:T(128)S(1)} %pad_add_fusion.1.order_ref, bf16[160,1024]{1,0:T(8,128)(2,1)S(1)} %get-tuple-element.45.rows_ref, bf16[2,4,384,1024]{3,2,1,0:T(8,128)(2,1)} %bitcast.25), custom_call_target="tpu_custom_call" | custom-call | flops 754974720 | bytes 4718592 | tf_op jit(solution)/shard_map/rest/pallas_call | solution.py:148
  91.9 3.3 %collective-permute-start.8 = (bf16[160,384]{1,0:T(8,128)(2,1)S(1)}, bf16[160,384]{1,0:T(8,128)(2,1)S(1)}, u32[]{:S(2)}, u32[]{:S(2)}) collective-permute-start(bf16[160,384]{1,0:T(8,128)(2,1)S(1)} %fusion.1.refs_3_), channel_id=1, source_target_pairs={{0,1},{1,0},{2,3},{3,2},{4,5},{5,4},{6,7},{7,6},{8,9},{9,8},{10,11... | collective-permute-start | bytes 368648 | tf_op jit(solution)/shard_map/ppermute | solution.py:296
  95.2 4.5 %collective-permute-start.7 = (bf16[160,384]{1,0:T(8,128)(2,1)S(1)}, bf16[160,384]{1,0:T(8,128)(2,1)S(1)}, u32[]{:S(2)}, u32[]{:S(2)}) collective-permute-start(bf16[160,384]{1,0:T(8,128)(2,1)S(1)} %fusion.1.refs_3_), channel_id=1, source_target_pairs={{0,3},{1,2},{2,1},{3,0},{4,7},{5,6},{6,5},{7,4},{8,11},{9,10},{10,... | collective-permute-start | bytes 368648 | tf_op jit(solution)/shard_map/ppermute | solution.py:296
  100.5 3.4 %collective-permute-done.7.refs_0_ = bf16[160,384]{1,0:T(8,128)(2,1)S(1)} collective-permute-done((bf16[160,384]{1,0:T(8,128)(2,1)S(1)}, bf16[160,384]{1,0:T(8,128)(2,1)S(1)}, u32[]{:S(2)}, u32[]{:S(2)}) %collective-permute-start.7) | collective-permute-done | bytes 122912 | tf_op jit(solution)/shard_map/ppermute | solution.py:296
  106.3 11.0 %all-to-all-start.2 = ((bf16[16,40,256]{2,1,0:T(8,128)(2,1)}), bf16[16,40,256]{2,1,0:T(8,128)(2,1)}, u32[]{:S(2)}, u32[]{:S(2)}) async-start(bf16[16,40,256]{2,1,0:T(8,128)(2,1)} %bitcast.13), calls=%async_computation.2 | async-start | bytes 655360 | tf_op jit(solution)/shard_map/all_to_all | solution.py:283
  117.3 2.7 %collective-permute-start.4 = (bf16[160,768]{1,0:T(8,128)(2,1)}, bf16[160,768]{1,0:T(8,128)(2,1)S(1)}, u32[]{:S(2)}, u32[]{:S(2)}) collective-permute-start(bf16[160,768]{1,0:T(8,128)(2,1)} %copy-done.3), channel_id=1, source_target_pairs={{0,1},{1,0},{2,3},{3,2},{4,5},{5,4},{6,7},{7,6},{8,9},{9,8},{10,11... | collective-permute-start | bytes 737288 | tf_op jit(solution)/shard_map/ppermute | solution.py:321
  120.1 4.4 %collective-permute-start.3 = (bf16[160,768]{1,0:T(8,128)(2,1)}, bf16[160,768]{1,0:T(8,128)(2,1)S(1)}, u32[]{:S(2)}, u32[]{:S(2)}) collective-permute-start(bf16[160,768]{1,0:T(8,128)(2,1)} %add_convert_fusion), channel_id=1, source_target_pairs={{0,2},{1,3},{2,0},{3,1},{4,6},{5,7},{6,4},{7,5},{8,10},{9,11},{10,... | collective-permute-start | bytes 737288 | tf_op jit(solution)/shard_map/ppermute | solution.py:320
  124.5 3.8 %collective-permute-done.4 = bf16[160,768]{1,0:T(8,128)(2,1)S(1)} collective-permute-done((bf16[160,768]{1,0:T(8,128)(2,1)}, bf16[160,768]{1,0:T(8,128)(2,1)S(1)}, u32[]{:S(2)}, u32[]{:S(2)}) %collective-permute-start.4) | collective-permute-done | bytes 245792 | tf_op jit(solution)/shard_map/ppermute | solution.py:321
  128.3 5.9 %collective-permute-done.3 = bf16[160,768]{1,0:T(8,128)(2,1)S(1)} collective-permute-done((bf16[160,768]{1,0:T(8,128)(2,1)}, bf16[160,768]{1,0:T(8,128)(2,1)S(1)}, u32[]{:S(2)}, u32[]{:S(2)}) %collective-permute-start.3) | collective-permute-done | bytes 245792 | tf_op jit(solution)/shard_map/ppermute | solution.py:320
  138.8 5.6 %collective-permute-start.10 = (bf16[160,384]{1,0:T(8,128)(2,1)S(1)}, bf16[160,384]{1,0:T(8,128)(2,1)S(1)}, u32[]{:S(2)}, u32[]{:S(2)}) collective-permute-start(bf16[160,384]{1,0:T(8,128)(2,1)S(1)} %fusion.refs_3_), channel_id=1, source_target_pairs={{0,3},{1,2},{2,1},{3,0},{4,7},{5,6},{6,5},{7,4},{8,11},{9,10},{10,... | collective-permute-start | bytes 368648 | tf_op jit(solution)/shard_map/ppermute | solution.py:296
  149.2 28.4 %all_to_all.20 = bf16[16,40,256]{2,1,0:T(8,128)(2,1)S(1)} all-to-all(bf16[16,40,256]{2,1,0:T(8,128)(2,1)S(1)} %bitcast.19), channel_id=1, replica_groups={{0,8,16,24,32,40,48,56,64,72,80,88,96,104,112,120},{4,12,20,28,36,44,52..., dimensions={0} | all-to-all | bytes 655360 | tf_op jit(solution)/shard_map/all_to_all | solution.py:283
  177.6 3.7 %collective-permute-start.13 = (bf16[640,256]{1,0:T(8,128)(2,1)S(1)}, bf16[640,256]{1,0:T(8,128)(2,1)S(1)}, u32[]{:S(2)}, u32[]{:S(2)}) collective-permute-start(bf16[640,256]{1,0:T(8,128)(2,1)S(1)} %bitcast.27), channel_id=1, source_target_pairs={{0,4},{4,0},{8,12},{12,8},{16,20},{20,16},{24,28},{28,24},{32,36},... | collective-permute-start | bytes 983048 | tf_op jit(solution)/shard_map/ppermute | solution.py:286
  181.5 2.9 %mixer.1.mixer_ref = bf16[512,1280]{1,0:T(8,128)(2,1)S(1)} custom-call(s32[1]{0:T(128)} %bitcast.which_ref.half_ref, s32[128,8]{1,0:T(8,128)S(1)} %copy.6.ids_ref, f32[128,8]{1,0:T(8,128)S(1)} %copy.7.weight_ref), custom_call_target="tpu_custom_call" | custom-call | tf_op jit(solution)/shard_map/mixer/pallas_call | solution.py:223
  184.4 9.3 %collective-permute-done.13.other_ref = bf16[640,256]{1,0:T(8,128)(2,1)S(1)} collective-permute-done((bf16[640,256]{1,0:T(8,128)(2,1)S(1)}, bf16[640,256]{1,0:T(8,128)(2,1)S(1)}, u32[]{:S(2)}, u32[]{:S(2)}) %collective-permute-start.13) | collective-permute-done | bytes 327712 | tf_op jit(solution)/shard_map/ppermute | solution.py:286
  193.8 3.0 %combine.1 = bf16[128,1024]{1,0:T(8,128)(2,1)} custom-call(bf16[512,1280]{1,0:T(8,128)(2,1)S(1)} %mixer.1.mixer_ref, bf16[640,256]{1,0:T(8,128)(2,1)} %bitcast.14.same_ref, bf16[640,256]{1,0:T(8,128)(2,1)S(1)} %collective-permute-done.13.other_ref), custom_call_target="tpu_custom_call" | custom-call | tf_op jit(solution)/shard_map/combine/pallas_call | solution.py:247
  (43 shorter events, 28.8 us)
Async XLA Ops:
  2.6 43.8 %all-to-all-start = ((bf16[16,40,256]{2,1,0:T(8,128)(2,1)}), bf16[16,40,256]{2,1,0:T(8,128)(2,1)S(1)}, u32[]{:S(2)}, u32[]{:S(2)}) async-start(bf16[16,40,256]{2,1,0:T(8,128)(2,1)} %bitcast.26), calls=%async_computation | async-start | bytes 655360 | tf_op jit(solution)/shard_map/all_to_all | solution.py:283
  24.2 22.2 %collective-permute-start = (bf16[640,256]{1,0:T(8,128)(2,1)}, bf16[640,256]{1,0:T(8,128)(2,1)}, u32[]{:S(2)}, u32[]{:S(2)}) collective-permute-start(bf16[640,256]{1,0:T(8,128)(2,1)} %pack.3), channel_id=1, source_target_pairs={{0,4},{4,0},{8,12},{12,8},{16,20},{20,16},{24,28},{28,24},{32,36},... | collective-permute-start | bytes 983048 | tf_op jit(solution)/shard_map/ppermute | solution.py:286
  46.4 32.3 %all-to-all-start.1 = ((bf16[16,40,256]{2,1,0:T(8,128)(2,1)}), bf16[16,40,256]{2,1,0:T(8,128)(2,1)S(1)}, u32[]{:S(2)}, u32[]{:S(2)}) async-start(bf16[16,40,256]{2,1,0:T(8,128)(2,1)} %bitcast.9), calls=%async_computation.1 | async-start | bytes 655360 | tf_op jit(solution)/shard_map/all_to_all | solution.py:283
  60.5 9.2 %collective-permute-start.1 = (bf16[160,768]{1,0:T(8,128)(2,1)S(1)}, bf16[160,768]{1,0:T(8,128)(2,1)S(1)}, u32[]{:S(2)}, u32[]{:S(2)}) collective-permute-start(bf16[160,768]{1,0:T(8,128)(2,1)S(1)} %get-tuple-element.38), channel_id=1, source_target_pairs={{0,1},{1,0},{2,3},{3,2},{4,5},{5,4},{6,7},{7,6},{8,9},{9,8},{10,11... | collective-permute-start | bytes 737288 | tf_op jit(solution)/shard_map/ppermute | solution.py:306
  69.1 7.6 %copy-start.1 = (bf16[160,768]{1,0:T(8,128)(2,1)}, bf16[160,768]{1,0:T(8,128)(2,1)S(1)}, u32[]{:S(2)}) copy-start(bf16[160,768]{1,0:T(8,128)(2,1)S(1)} %get-tuple-element.55) | copy-start | bytes 737284
  70.5 17.8 %collective-permute-start.6 = (bf16[160,768]{1,0:T(8,128)(2,1)}, bf16[160,768]{1,0:T(8,128)(2,1)}, u32[]{:S(2)}, u32[]{:S(2)}) collective-permute-start(bf16[160,768]{1,0:T(8,128)(2,1)} %get-tuple-element.50), channel_id=1, source_target_pairs={{0,1},{1,0},{2,3},{3,2},{4,5},{5,4},{6,7},{7,6},{8,9},{9,8},{10,11... | collective-permute-start | bytes 737288 | tf_op jit(solution)/shard_map/ppermute | solution.py:310
  72.7 15.6 %collective-permute-start.5 = (bf16[160,768]{1,0:T(8,128)(2,1)}, bf16[160,768]{1,0:T(8,128)(2,1)}, u32[]{:S(2)}, u32[]{:S(2)}) collective-permute-start(bf16[160,768]{1,0:T(8,128)(2,1)} %add_convert_fusion.1), channel_id=1, source_target_pairs={{0,2},{1,3},{2,0},{3,1},{4,6},{5,7},{6,4},{7,5},{8,10},{9,11},{10,... | collective-permute-start | bytes 737288 | tf_op jit(solution)/shard_map/ppermute | solution.py:309
  81.1 18.7 %collective-permute-start.2 = (bf16[160,768]{1,0:T(8,128)(2,1)S(1)}, bf16[160,768]{1,0:T(8,128)(2,1)S(1)}, u32[]{:S(2)}, u32[]{:S(2)}) collective-permute-start(bf16[160,768]{1,0:T(8,128)(2,1)S(1)} %get-tuple-element.44), channel_id=1, source_target_pairs={{0,1},{1,0},{2,3},{3,2},{4,5},{5,4},{6,7},{7,6},{8,9},{9,8},{10,11... | collective-permute-start | bytes 737288 | tf_op jit(solution)/shard_map/ppermute | solution.py:314
  83.2 5.0 %copy-start.2 = (bf16[160,768]{1,0:T(8,128)(2,1)S(1)}, bf16[160,768]{1,0:T(8,128)(2,1)}, u32[]{:S(2)}) copy-start(bf16[160,768]{1,0:T(8,128)(2,1)} %copy-done.1) | copy-start | bytes 737284
  83.3 20.6 %copy-start = (bf16[1,1536,1024]{2,1,0:T(8,128)(2,1)S(1)}, bf16[1,1536,1024]{2,1,0:T(8,128)(2,1)}, u32[]{:S(2)}) copy-start(bf16[1,1536,1024]{2,1,0:T(8,128)(2,1)} %param.9) | copy-start | bytes 9437188
  88.3 15.6 %copy-start.3 = (bf16[160,768]{1,0:T(8,128)(2,1)}, bf16[160,768]{1,0:T(8,128)(2,1)S(1)}, u32[]{:S(2)}) copy-start(bf16[160,768]{1,0:T(8,128)(2,1)S(1)} %get-tuple-element.49) | copy-start | bytes 737284
  89.6 10.9 %collective-permute-start.9 = (bf16[160,384]{1,0:T(8,128)(2,1)S(1)}, bf16[160,384]{1,0:T(8,128)(2,1)S(1)}, u32[]{:S(2)}, u32[]{:S(2)}) collective-permute-start(bf16[160,384]{1,0:T(8,128)(2,1)S(1)} %fusion.1.refs_3_), channel_id=1, source_target_pairs={{0,2},{1,3},{2,0},{3,1},{4,6},{5,7},{6,4},{7,5},{8,10},{9,11},{10,... | collective-permute-start | bytes 368648 | tf_op jit(solution)/shard_map/ppermute | solution.py:296
  91.9 8.6 %collective-permute-start.8 = (bf16[160,384]{1,0:T(8,128)(2,1)S(1)}, bf16[160,384]{1,0:T(8,128)(2,1)S(1)}, u32[]{:S(2)}, u32[]{:S(2)}) collective-permute-start(bf16[160,384]{1,0:T(8,128)(2,1)S(1)} %fusion.1.refs_3_), channel_id=1, source_target_pairs={{0,1},{1,0},{2,3},{3,2},{4,5},{5,4},{6,7},{7,6},{8,9},{9,8},{10,11... | collective-permute-start | bytes 368648 | tf_op jit(solution)/shard_map/ppermute | solution.py:296
  95.2 8.7 %collective-permute-start.7 = (bf16[160,384]{1,0:T(8,128)(2,1)S(1)}, bf16[160,384]{1,0:T(8,128)(2,1)S(1)}, u32[]{:S(2)}, u32[]{:S(2)}) collective-permute-start(bf16[160,384]{1,0:T(8,128)(2,1)S(1)} %fusion.1.refs_3_), channel_id=1, source_target_pairs={{0,3},{1,2},{2,1},{3,0},{4,7},{5,6},{6,5},{7,4},{8,11},{9,10},{10,... | collective-permute-start | bytes 368648 | tf_op jit(solution)/shard_map/ppermute | solution.py:296
  106.3 42.9 %all-to-all-start.2 = ((bf16[16,40,256]{2,1,0:T(8,128)(2,1)}), bf16[16,40,256]{2,1,0:T(8,128)(2,1)}, u32[]{:S(2)}, u32[]{:S(2)}) async-start(bf16[16,40,256]{2,1,0:T(8,128)(2,1)} %bitcast.13), calls=%async_computation.2 | async-start | bytes 655360 | tf_op jit(solution)/shard_map/all_to_all | solution.py:283
  117.3 63.9 %copy-start.4 = (s32[128,8]{0,1:T(8,128)S(1)}, s32[128,8]{0,1:T(8,128)}, u32[]{:S(2)}) copy-start(s32[128,8]{0,1:T(8,128)} %param.6) | copy-start | bytes 12292
  117.3 64.0 %copy-start.5 = (f32[128,8]{0,1:T(8,128)S(1)}, f32[128,8]{0,1:T(8,128)}, u32[]{:S(2)}) copy-start(f32[128,8]{0,1:T(8,128)} %param.7) | copy-start | bytes 12292
  117.3 10.9 %collective-permute-start.4 = (bf16[160,768]{1,0:T(8,128)(2,1)}, bf16[160,768]{1,0:T(8,128)(2,1)S(1)}, u32[]{:S(2)}, u32[]{:S(2)}) collective-permute-start(bf16[160,768]{1,0:T(8,128)(2,1)} %copy-done.3), channel_id=1, source_target_pairs={{0,1},{1,0},{2,3},{3,2},{4,5},{5,4},{6,7},{7,6},{8,9},{9,8},{10,11... | collective-permute-start | bytes 737288 | tf_op jit(solution)/shard_map/ppermute | solution.py:321
  120.1 14.1 %collective-permute-start.3 = (bf16[160,768]{1,0:T(8,128)(2,1)}, bf16[160,768]{1,0:T(8,128)(2,1)S(1)}, u32[]{:S(2)}, u32[]{:S(2)}) collective-permute-start(bf16[160,768]{1,0:T(8,128)(2,1)} %add_convert_fusion), channel_id=1, source_target_pairs={{0,2},{1,3},{2,0},{3,1},{4,6},{5,7},{6,4},{7,5},{8,10},{9,11},{10,... | collective-permute-start | bytes 737288 | tf_op jit(solution)/shard_map/ppermute | solution.py:320
  134.3 10.1 %collective-permute-start.12 = (bf16[160,384]{1,0:T(8,128)(2,1)S(1)}, bf16[160,384]{1,0:T(8,128)(2,1)S(1)}, u32[]{:S(2)}, u32[]{:S(2)}) collective-permute-start(bf16[160,384]{1,0:T(8,128)(2,1)S(1)} %fusion.refs_3_), channel_id=1, source_target_pairs={{0,2},{1,3},{2,0},{3,1},{4,6},{5,7},{6,4},{7,5},{8,10},{9,11},{10,... | collective-permute-start | bytes 368648 | tf_op jit(solution)/shard_map/ppermute | solution.py:296
  136.3 8.8 %collective-permute-start.11 = (bf16[160,384]{1,0:T(8,128)(2,1)S(1)}, bf16[160,384]{1,0:T(8,128)(2,1)S(1)}, u32[]{:S(2)}, u32[]{:S(2)}) collective-permute-start(bf16[160,384]{1,0:T(8,128)(2,1)S(1)} %fusion.refs_3_), channel_id=1, source_target_pairs={{0,1},{1,0},{2,3},{3,2},{4,5},{5,4},{6,7},{7,6},{8,9},{9,8},{10,11... | collective-permute-start | bytes 368648 | tf_op jit(solution)/shard_map/ppermute | solution.py:296
  138.8 8.7 %collective-permute-start.10 = (bf16[160,384]{1,0:T(8,128)(2,1)S(1)}, bf16[160,384]{1,0:T(8,128)(2,1)S(1)}, u32[]{:S(2)}, u32[]{:S(2)}) collective-permute-start(bf16[160,384]{1,0:T(8,128)(2,1)S(1)} %fusion.refs_3_), channel_id=1, source_target_pairs={{0,3},{1,2},{2,1},{3,0},{4,7},{5,6},{6,5},{7,4},{8,11},{9,10},{10,... | collective-permute-start | bytes 368648 | tf_op jit(solution)/shard_map/ppermute | solution.py:296
  177.6 16.2 %collective-permute-start.13 = (bf16[640,256]{1,0:T(8,128)(2,1)S(1)}, bf16[640,256]{1,0:T(8,128)(2,1)S(1)}, u32[]{:S(2)}, u32[]{:S(2)}) collective-permute-start(bf16[640,256]{1,0:T(8,128)(2,1)S(1)} %bitcast.27), channel_id=1, source_target_pairs={{0,4},{4,0},{8,12},{12,8},{16,20},{20,16},{24,28},{28,24},{32,36},... | collective-permute-start | bytes 983048 | tf_op jit(solution)/shard_map/ppermute | solution.py:286

commit v4 on v2

--- a/solution.py
+++ b/solution.py
@@ -17,6 +17,7 @@
 PARAMS = pltpu.CompilerParams(vmem_limit_bytes=48 * 1024 * 1024)
 BLOCK = QUARTERS * CAP
 GROUP = 8
+PIECE = 128
 
 
 def mm(a, b):
@@ -96,7 +97,7 @@
 def pack(ids_t, tokens, flight):
     rows, features = tokens.shape
     places = flight * BLOCK
-    steps = 4
+    steps = 2
     whole = lambda a: pl.BlockSpec(a.shape, lambda i: (0, 0))
     return pl.pallas_call(
         functools.partial(pack_kernel, flight),
@@ -109,70 +110,70 @@
     )(ids_t, tokens)
 
 
-def first_kernel(order_ref, x_ref, weight_ref, rows_ref, out_ref):
+def first_kernel(me_ref, x_ref, weight_ref, rows_ref, out_ref):
     cols = x_ref.shape[1]
     span, slab = GROUP * BLOCK, GROUP * CAP
-
-    @pl.when(pl.program_id(0) == 0)
-    def _():
-        regroup = regroup_matrix(False)
-        for g in range(x_ref.shape[0] // span):
-            sorted_rows = mm(regroup, x_ref[g * span : (g + 1) * span, :]).astype(BF16)
-            for q in range(QUARTERS):
-                rows_ref[g * slab : (g + 1) * slab, q * cols : (q + 1) * cols] = sorted_rows[q * slab : (q + 1) * slab]
-
-    out_ref[...] = mm_t(rows_ref[...], weight_ref[0, 0]).astype(BF16)
-
-
-def first_part(order, received, weights):
+    regroup = regroup_matrix(False)
+    for g in range(x_ref.shape[0] // span):
+        sorted_rows = mm(regroup, x_ref[g * span : (g + 1) * span, :]).astype(BF16)
+        for q in range(QUARTERS):
+            rows_ref[g * slab : (g + 1) * slab, q * cols : (q + 1) * cols] = sorted_rows[q * slab : (q + 1) * slab]
+    out_ref[...] = mm_t(rows_ref[...], weight_ref[...].reshape(2 * PIECE, -1)).astype(BF16)
+
+
+def piece_of(weights, quarter, mask, piece):
+    return (quarter ^ mask) * (weights.shape[1] // QUARTERS) + piece
+
+
+def first_part(me, mask, received, weights):
     places, cols = received.shape
     rows = places // QUARTERS
     features = weights.shape[3]
-    units = weights.shape[2]
-    whole = lambda shape: pl.BlockSpec(shape, lambda h, order: (0, 0))
+    whole = lambda shape: pl.BlockSpec(shape, lambda i, me: (0, 0))
     return pl.pallas_call(
         first_kernel,
-        out_shape=(jax.ShapeDtypeStruct((rows, features), BF16), jax.ShapeDtypeStruct((rows, 2 * units), BF16)),
+        out_shape=(jax.ShapeDtypeStruct((rows, features), BF16), jax.ShapeDtypeStruct((rows, 2 * PIECE), BF16)),
         grid_spec=pltpu.PrefetchScalarGridSpec(
             num_scalar_prefetch=1,
-            grid=(2,),
+            grid=(1,),
             in_specs=[whole((places, cols)),
-                      pl.BlockSpec((1, 1, units, features), lambda h, order: (h, order[0], 0, 0))],
-            out_specs=(whole((rows, features)), pl.BlockSpec((rows, units), lambda h, order: (0, h))),
+                      pl.BlockSpec((2, 1, PIECE, features), lambda i, me: (0, piece_of(weights, me[0], mask, 0), 0, 0))],
+            out_specs=(whole((rows, features)), whole((rows, 2 * PIECE))),
         ),
         compiler_params=PARAMS,
-        cost_estimate=pl.CostEstimate(flops=4 * rows * units * features, bytes_accessed=4 * units * features, transcendentals=0),
+        cost_estimate=pl.CostEstimate(flops=4 * rows * PIECE * features, bytes_accessed=4 * PIECE * features, transcendentals=0),
         name="first",
-    )(order, received, weights)
-
-
-def rest_kernel(order_ref, rows_ref, weight_ref, *out_refs):
-    units = weight_ref.shape[2]
-    for j, out_ref in enumerate(out_refs):
-        @pl.when(pl.program_id(0) == j)
+    )(me, received, weights)
+
+
+def parts_kernel(pieces, me_ref, rows_ref, weight_ref, *out_refs):
+    steps = [(out_ref, p) for out_ref, count in zip(out_refs, pieces) for p in range(count)]
+    for i, (out_ref, p) in enumerate(steps):
+        @pl.when(pl.program_id(0) == i)
         def _():
-            for h in range(2):
-                out_ref[:, h * units : (h + 1) * units] = mm_t(rows_ref[...], weight_ref[h, 0]).astype(BF16)
-
-
-def rest_parts(order, rows_in, weights, count):
+            product = mm_t(rows_ref[...], weight_ref[...].reshape(2 * PIECE, -1))
+            out_ref[:, p * 2 * PIECE : (p + 1) * 2 * PIECE] = product.astype(BF16)
+
+
+def parts(me, mask, rows_in, weights, *pieces, start=0):
     rows, features = rows_in.shape
-    units = weights.shape[2]
-    whole = lambda shape: pl.BlockSpec(shape, lambda i, order: (0, 0))
-    return pl.pallas_call(
-        rest_kernel,
-        out_shape=(jax.ShapeDtypeStruct((rows, 2 * units), BF16),) * count,
+    steps = sum(pieces)
+    whole = lambda shape: pl.BlockSpec(shape, lambda i, me: (0, 0))
+    shapes = [(rows, 2 * PIECE * count) for count in pieces]
+    return pl.pallas_call(
+        functools.partial(parts_kernel, pieces),
+        out_shape=tuple(jax.ShapeDtypeStruct(shape, BF16) for shape in shapes),
         grid_spec=pltpu.PrefetchScalarGridSpec(
             num_scalar_prefetch=1,
-            grid=(count,),
+            grid=(steps,),
             in_specs=[whole((rows, features)),
-                      pl.BlockSpec((2, 1, units, features), lambda i, order: (0, order[i], 0, 0))],
-            out_specs=(whole((rows, 2 * units)),) * count,
+                      pl.BlockSpec((2, 1, PIECE, features), lambda i, me: (0, piece_of(weights, me[0], mask, start + i), 0, 0))],
+            out_specs=tuple(whole(shape) for shape in shapes),
         ),
         compiler_params=PARAMS,
-        cost_estimate=pl.CostEstimate(flops=4 * count * rows * units * features, bytes_accessed=4 * count * units * features, transcendentals=0),
-        name="rest",
-    )(order, rows_in, weights)
+        cost_estimate=pl.CostEstimate(flops=4 * steps * rows * PIECE * features, bytes_accessed=4 * steps * PIECE * features, transcendentals=0),
+        name="parts",
+    )(me, rows_in, weights)
 
 
 def down_kernel(hidden_ref, weight_ref, out_ref):
@@ -257,32 +258,52 @@
     )(mix, returned)
 
 
+def tie(*values):
+    return lax.optimization_barrier(values)
+
+
 def local(tokens, expert_ids, route_weight, gate_up, down_proj):
     flight = lax.axis_size("ep")
     n_tp = lax.axis_size("tp")
     features = tokens.shape[1]
     cols = features // QUARTERS
     units = gate_up.shape[2] // n_tp
-    up_weights = gate_up.reshape(2, n_tp, units, features)
+    pieces = units // PIECE
+    up_weights = gate_up.reshape(2, n_tp * pieces, PIECE, features)
     down_weights = down_proj.reshape(n_tp, units, features)
-    me = lax.axis_index("tp")
-    order = jnp.stack([me ^ 3, me ^ 1, me ^ 2, me]).astype(jnp.int32)
+    me = lax.axis_index("tp").astype(jnp.int32).reshape(1)
     near = [(i, i ^ 1) for i in range(n_tp)]
     far = [(i, i ^ 2) for i in range(n_tp)]
 
+    def pair_sum(got, keep):
+        return (got.astype(F32) + keep.astype(F32)).astype(BF16)
+
     sent = pack(expert_ids.T, tokens, flight)
     received = lax.all_to_all(sent.reshape(flight, BLOCK, cols), "ep", 0, 0, tiled=True).reshape(flight * BLOCK, cols)
 
-    row_block, for_far = first_part(order[:1], received, up_weights)
-    got_far = lax.ppermute(for_far, "tp", near)
-    for_near, keep_far, keep = rest_parts(order[1:], row_block, up_weights, 3)
-    pair_far = (got_far.astype(F32) + keep_far.astype(F32)).astype(BF16)
-    for_near, pair_far = lax.optimization_barrier((for_near, pair_far))
-    got = lax.ppermute(pair_far, "tp", far)
+    rows, far_1 = first_part(me, 3, received, up_weights)
+    got_1 = lax.ppermute(far_1, "tp", near)
+    (far_2,) = parts(me, 3, rows, up_weights, pieces - 1, start=1)
+    got_2 = lax.ppermute(far_2, "tp", near)
+    rows, far_2 = tie(rows, far_2)
+    keep_1, keep_2 = parts(me, 2, rows, up_weights, 1, pieces - 1)
+    pair_1 = pair_sum(got_1, keep_1)
+    rows, pair_1 = tie(rows, pair_1)
+    got_1 = lax.ppermute(pair_1, "tp", far)
+    (for_near,) = parts(me, 1, rows, up_weights, pieces)
     got_near = lax.ppermute(for_near, "tp", near)
-    summed = got.astype(F32) + got_near.astype(F32) + keep.astype(F32)
-    hidden = (jax.nn.silu(summed[:, :units]) * summed[:, units:]).astype(BF16)
-    hidden = lax.all_gather(hidden, "tp", axis=0, tiled=False)
+    for_near, got_2 = tie(for_near, got_2)
+    pair_2 = pair_sum(got_2, keep_2)
+    rows, pair_2, got_1 = tie(rows, pair_2, got_1)
+    got_2 = lax.ppermute(pair_2, "tp", far)
+    (keep,) = parts(me, 0, rows, up_weights, pieces)
+    got = [got_1] + [got_2[:, p * 2 * PIECE : (p + 1) * 2 * PIECE] for p in range(pieces - 1)]
+    hidden = []
+    for p in range(pieces):
+        columns = slice(p * 2 * PIECE, (p + 1) * 2 * PIECE)
+        summed = got[p].astype(F32) + got_near[:, columns].astype(F32) + keep[:, columns].astype(F32)
+        hidden.append((jax.nn.silu(summed[:, :PIECE]) * summed[:, PIECE:]).astype(BF16))
+    hidden = lax.all_gather(jnp.concatenate(hidden, axis=1), "tp", axis=0, tiled=False)
 
     result = down(hidden, down_weights)
     returned = lax.all_to_all(result.reshape(flight, BLOCK, cols), "ep", 0, 0, tiled=True).reshape(flight * BLOCK, cols)

time: 180 us -> 178 us (0.989)
  waiting for transfers between devices: 94.7 us -> 79.9 us
  starting transfers between devices: 44.1 us -> 49.4 us
  Pallas kernels: 19.4 us -> 23.3 us
  blocking collectives: 20.9 us -> 22.7 us
    ppermute x2 -> x4, waiting for transfers between devices: 22.8 us -> 12.2 us  [the longest x1 12.2 us: local(): got_2 = lax.ppermute(pair_2, 'tp', far)]
    pallas_call x1 -> x4, Pallas kernels: 5.11 us -> 10.5 us  [parts(): pl.pallas_call(functools.partial(parts_kernel, pieces), out_shape=tuple((...]
    ppermute x2 -> x4, starting transfers between devices: 6.66 us -> 12.1 us  [the longest x1 4.3 us: local(): got_1 = lax.ppermute(pair_1, 'tp', far)]
  transfers between devices with their start and end apart: 5 -> 7, of which waited for: 5 -> 4; matrix products, arithmetic and copies ran while one was open for 0% -> 0% of each run, Pallas kernels for 4% -> 8%
where the time goes in v4:
time: 178 us; the launch traced here: 176 us
  waiting for transfers between devices  79.9 us (45%)
  starting transfers between devices  49.4 us (28%)
  Pallas kernels  23.3 us (13%)
  blocking collectives  22.7 us (13%)
    all_to_all x1, waiting for transfers between devices, local(): lax.all_to_all(sent.reshape(flight, BLOCK, cols), 'ep', 0, 0, tiled=True)  37.4 us
    all_to_all x1, waiting for transfers between devices, local(): lax.all_to_all(result.reshape(flight, BLOCK, cols), 'ep', 0, 0, tiled=True)  30.3 us
    all_to_all x1, starting transfers between devices, local(): lax.all_to_all(sent.reshape(flight, BLOCK, cols), 'ep', 0, 0, tiled=True)  24.3 us
    all_gather x1, blocking collectives, local(): lax.all_gather(jnp.concatenate(hidden, axis=1), 'tp', axis=0, tiled=False)  22.7 us
    ppermute x1, waiting for transfers between devices, local(): got_2 = lax.ppermute(pair_2, 'tp', far)  12.2 us
    pallas_call x4, Pallas kernels, parts(): pl.pallas_call(functools.partial(parts_kernel, pieces), out_shape=tuple((...  10.5 us
    all_to_all x1, starting transfers between devices, local(): lax.all_to_all(result.reshape(flight, BLOCK, cols), 'ep', 0, 0, tiled=True)  9.15 us
    ppermute x1, starting transfers between devices, local(): got_1 = lax.ppermute(pair_1, 'tp', far)  4.3 us
  transfers between devices with their start and end apart: 7, of which 4 were waited for; matrix products, arithmetic and copies ran while one was open for 0% of the time, Pallas kernels for 8%

profile of v4, /device:TPU:56, one launch (start us, length us, event | category | flops | bytes accessed | tf_op | source)
XLA Modules:
  0.0 176.3 jit_solution(5371277033727836957)
XLA Ops:
  0.0 3.0 %pack.1 = bf16[1280,256]{1,0:T(8,128)(2,1)} custom-call(s32[8,128]{1,0:T(8,128)} %bitcast.19, bf16[128,1024]{1,0:T(8,128)(2,1)} %token_ref.1), custom_call_target="tpu_custom_call" | custom-call | tf_op jit(solution)/shard_map/pack/pallas_call | solution.py:102
  3.1 24.3 %all-to-all-start = ((bf16[32,40,256]{2,1,0:T(8,128)(2,1)}), bf16[32,40,256]{2,1,0:T(8,128)(2,1)S(1)}, u32[]{:S(2)}, u32[]{:S(2)}) async-start(bf16[32,40,256]{2,1,0:T(8,128)(2,1)} %bitcast.18), calls=%async_computation | async-start | bytes 1310720 | tf_op jit(solution)/shard_map/all_to_all | solution.py:282
  27.3 37.4 %all-to-all-done = bf16[32,40,256]{2,1,0:T(8,128)(2,1)S(1)} async-done(((bf16[32,40,256]{2,1,0:T(8,128)(2,1)}), bf16[32,40,256]{2,1,0:T(8,128)(2,1)S(1)}, u32[]{:S(2)}, u32[]{:S(2)}) %all-to-all-start) | async-done | bytes 655392 | tf_op jit(solution)/shard_map/all_to_all | solution.py:282
  64.7 2.0 %first.1 = (bf16[320,1024]{1,0:T(8,128)(2,1)S(1)}, bf16[320,256]{1,0:T(8,128)(2,1)S(1)}) custom-call(s32[1]{0:T(128)} %bitcast.me_ref, bf16[1280,256]{1,0:T(8,128)(2,1)S(1)} %bitcast.12, bf16[2,12,128,1024]{3,2,1,0:T(8,128)(2,1)} %bitcast.13), custom_call_target="tpu_custom_call" | custom-call | flops 167772160 | bytes 524288 | tf_op jit(solution)/shard_map/first/pallas_call | solution.py:133
  66.7 3.3 %collective-permute-start = (bf16[320,256]{1,0:T(8,128)(2,1)S(1)}, bf16[320,256]{1,0:T(8,128)(2,1)S(1)}, u32[]{:S(2)}, u32[]{:S(2)}) collective-permute-start(bf16[320,256]{1,0:T(8,128)(2,1)S(1)} %get-tuple-element.18), channel_id=1, source_target_pairs={{0,1},{1,0},{2,3},{3,2},{4,5},{5,4},{6,7},{7,6},{8,9},{9,8},{10,11... | collective-permute-start | bytes 491528 | tf_op jit(solution)/shard_map/ppermute | solution.py:285
  70.0 1.9 %parts.4 = bf16[320,512]{1,0:T(8,128)(2,1)S(1)} custom-call(s32[1]{0:T(128)} %bitcast.me_ref, bf16[320,1024]{1,0:T(8,128)(2,1)S(1)} %get-tuple-element.25.rows_ref, bf16[2,12,128,1024]{3,2,1,0:T(8,128)(2,1)} %bitcast.14), custom_call_target="tpu_custom_call" | custom-call | flops 335544320 | bytes 1048576 | tf_op jit(solution)/shard_map/parts/pallas_call | solution.py:163
  71.9 2.6 %collective-permute-start.1 = (bf16[320,512]{1,0:T(8,128)(2,1)S(1)}, bf16[320,512]{1,0:T(8,128)(2,1)S(1)}, u32[]{:S(2)}, u32[]{:S(2)}) collective-permute-start(bf16[320,512]{1,0:T(8,128)(2,1)S(1)} %parts.4), channel_id=1, source_target_pairs={{0,1},{1,0},{2,3},{3,2},{4,5},{5,4},{6,7},{7,6},{8,9},{9,8},{10,11... | collective-permute-start | bytes 983048 | tf_op jit(solution)/shard_map/ppermute | solution.py:287
  74.4 2.9 %parts.5 = (bf16[320,256]{1,0:T(8,128)(2,1)S(1)}, bf16[320,512]{1,0:T(8,128)(2,1)S(1)}) custom-call(s32[1]{0:T(128)} %bitcast.me_ref, bf16[320,1024]{1,0:T(8,128)(2,1)S(1)} %get-tuple-element.25.rows_ref, bf16[2,12,128,1024]{3,2,1,0:T(8,128)(2,1)} %bitcast.15), custom_call_target="tpu_custom_call" | custom-call | flops 503316480 | bytes 1572864 | tf_op jit(solution)/shard_map/parts/pallas_call | solution.py:163
  77.4 4.3 %collective-permute-start.2 = (bf16[320,256]{1,0:T(8,128)(2,1)S(1)}, bf16[320,256]{1,0:T(8,128)(2,1)S(1)}, u32[]{:S(2)}, u32[]{:S(2)}) collective-permute-start(bf16[320,256]{1,0:T(8,128)(2,1)S(1)} %add_convert_fusion.1), channel_id=1, source_target_pairs={{0,2},{1,3},{2,0},{3,1},{4,6},{5,7},{6,4},{7,5},{8,10},{9,11},{10,... | collective-permute-start | bytes 491528 | tf_op jit(solution)/shard_map/ppermute | solution.py:292
  81.7 2.9 %parts.6 = bf16[320,768]{1,0:T(8,128)(2,1)S(1)} custom-call(s32[1]{0:T(128)} %bitcast.me_ref, bf16[320,1024]{1,0:T(8,128)(2,1)S(1)} %get-tuple-element.25.rows_ref, bf16[2,12,128,1024]{3,2,1,0:T(8,128)(2,1)} %bitcast.16), custom_call_target="tpu_custom_call" | custom-call | flops 503316480 | bytes 1572864 | tf_op jit(solution)/shard_map/parts/pallas_call | solution.py:163
  84.6 3.9 %collective-permute-start.3 = (bf16[320,768]{1,0:T(8,128)(2,1)S(1)}, bf16[320,768]{1,0:T(8,128)(2,1)S(1)}, u32[]{:S(2)}, u32[]{:S(2)}) collective-permute-start(bf16[320,768]{1,0:T(8,128)(2,1)S(1)} %parts.6), channel_id=1, source_target_pairs={{0,1},{1,0},{2,3},{3,2},{4,5},{5,4},{6,7},{7,6},{8,9},{9,8},{10,11... | collective-permute-start | bytes 1474568 | tf_op jit(solution)/shard_map/ppermute | solution.py:294
  88.7 1.9 %collective-permute-start.4 = (bf16[320,512]{1,0:T(8,128)(2,1)S(1)}, bf16[320,512]{1,0:T(8,128)(2,1)S(1)}, u32[]{:S(2)}, u32[]{:S(2)}) collective-permute-start(bf16[320,512]{1,0:T(8,128)(2,1)S(1)} %add_convert_fusion), channel_id=1, source_target_pairs={{0,2},{1,3},{2,0},{3,1},{4,6},{5,7},{6,4},{7,5},{8,10},{9,11},{10,... | collective-permute-start | bytes 983048 | tf_op jit(solution)/shard_map/ppermute | solution.py:298
  90.6 2.9 %parts.7 = bf16[320,768]{1,0:T(8,128)(2,1)S(1)} custom-call(s32[1]{0:T(128)} %bitcast.me_ref, bf16[320,1024]{1,0:T(8,128)(2,1)S(1)} %get-tuple-element.25.rows_ref, bf16[2,12,128,1024]{3,2,1,0:T(8,128)(2,1)} %bitcast.17), custom_call_target="tpu_custom_call" | custom-call | flops 503316480 | bytes 1572864 | tf_op jit(solution)/shard_map/parts/pallas_call | solution.py:163
  93.5 12.2 %collective-permute-done.4 = bf16[320,512]{1,0:T(8,128)(2,1)S(1)} collective-permute-done((bf16[320,512]{1,0:T(8,128)(2,1)S(1)}, bf16[320,512]{1,0:T(8,128)(2,1)S(1)}, u32[]{:S(2)}, u32[]{:S(2)}) %collective-permute-start.4) | collective-permute-done | bytes 327712 | tf_op jit(solution)/shard_map/ppermute | solution.py:298
  105.6 0.1 collective-permute-done.3
  105.8 0.2 convert_add_fusion.1
  106.2 22.7 %all-gather = bf16[1280,384]{1,0:T(8,128)(2,1)S(1)} all-gather(bf16[320,384]{1,0:T(8,128)(2,1)S(1)} %pad_maximum_fusion), channel_id=2, replica_groups=mesh['dp'=8,'ep'=32,'tp'=4] {'tp'}, dimensions={0}, use_global_device_ids=true | all-gather | bytes 1228800 | tf_op jit(solution)/shard_map/all_gather | solution.py:306
  128.9 2.8 %down.1 = bf16[1280,256]{1,0:T(8,128)(2,1)} custom-call(bf16[4,320,384]{2,1,0:T(8,128)(2,1)S(1)} %bitcast.9, bf16[4,384,1024]{2,1,0:T(8,128)(2,1)S(1)} %bitcast.10), custom_call_target="tpu_custom_call" | custom-call | tf_op jit(solution)/shard_map/down/pallas_call | solution.py:197
  131.7 9.2 %all-to-all-start.1 = ((bf16[32,40,256]{2,1,0:T(8,128)(2,1)}), bf16[32,40,256]{2,1,0:T(8,128)(2,1)S(1)}, u32[]{:S(2)}, u32[]{:S(2)}) async-start(bf16[32,40,256]{2,1,0:T(8,128)(2,1)} %bitcast.7), calls=%async_computation.1 | async-start | bytes 1310720 | tf_op jit(solution)/shard_map/all_to_all | solution.py:309
  140.9 0.1 copy.10.ids_ref
  141.0 0.1 copy.11.weight_ref
  141.1 2.9 %mixer.1.mixer_ref = bf16[512,1280]{1,0:T(8,128)(2,1)S(1)} custom-call(s32[128,8]{1,0:T(8,128)S(1)} %copy.10.ids_ref, f32[128,8]{1,0:T(8,128)S(1)} %copy.11.weight_ref, bf16[128,128]{1,0:T(8,128)(2,1)S(1)} %copy-done.4, bf16[32,1280]{1,0:T(8,128)(2,1)S(1)} %copy-done.2, bf16[16,1280]{1,0:T(8,128)(2,1)S(1)} %copy-done.3, bf16[512,16]{1,0:T(8,128)(2,1)S(1)} %copy-done.1), custom_call_target="tpu_custom_call" | custom-call | tf_op jit(solution)/shard_map/mixer/pallas_call | solution.py:231
  144.0 30.3 %all-to-all-done.1 = bf16[32,40,256]{2,1,0:T(8,128)(2,1)S(1)} async-done(((bf16[32,40,256]{2,1,0:T(8,128)(2,1)}), bf16[32,40,256]{2,1,0:T(8,128)(2,1)S(1)}, u32[]{:S(2)}, u32[]{:S(2)}) %all-to-all-start.1) | async-done | bytes 655392 | tf_op jit(solution)/shard_map/all_to_all | solution.py:309
  174.3 2.0 %combine.1 = bf16[128,1024]{1,0:T(8,128)(2,1)} custom-call(bf16[512,1280]{1,0:T(8,128)(2,1)S(1)} %mixer.1.mixer_ref, bf16[1280,256]{1,0:T(8,128)(2,1)S(1)} %bitcast.11), custom_call_target="tpu_custom_call" | custom-call | tf_op jit(solution)/shard_map/combine/pallas_call | solution.py:250
  (22 shorter events, 0.4 us)
Async XLA Ops:
  3.1 61.6 %all-to-all-start = ((bf16[32,40,256]{2,1,0:T(8,128)(2,1)}), bf16[32,40,256]{2,1,0:T(8,128)(2,1)S(1)}, u32[]{:S(2)}, u32[]{:S(2)}) async-start(bf16[32,40,256]{2,1,0:T(8,128)(2,1)} %bitcast.18), calls=%async_computation | async-start | bytes 1310720 | tf_op jit(solution)/shard_map/all_to_all | solution.py:282
  66.7 10.6 %collective-permute-start = (bf16[320,256]{1,0:T(8,128)(2,1)S(1)}, bf16[320,256]{1,0:T(8,128)(2,1)S(1)}, u32[]{:S(2)}, u32[]{:S(2)}) collective-permute-start(bf16[320,256]{1,0:T(8,128)(2,1)S(1)} %get-tuple-element.18), channel_id=1, source_target_pairs={{0,1},{1,0},{2,3},{3,2},{4,5},{5,4},{6,7},{7,6},{8,9},{9,8},{10,11... | collective-permute-start | bytes 491528 | tf_op jit(solution)/shard_map/ppermute | solution.py:285
  71.9 16.7 %collective-permute-start.1 = (bf16[320,512]{1,0:T(8,128)(2,1)S(1)}, bf16[320,512]{1,0:T(8,128)(2,1)S(1)}, u32[]{:S(2)}, u32[]{:S(2)}) collective-permute-start(bf16[320,512]{1,0:T(8,128)(2,1)S(1)} %parts.4), channel_id=1, source_target_pairs={{0,1},{1,0},{2,3},{3,2},{4,5},{5,4},{6,7},{7,6},{8,9},{9,8},{10,11... | collective-permute-start | bytes 983048 | tf_op jit(solution)/shard_map/ppermute | solution.py:287
  77.4 11.2 %collective-permute-start.2 = (bf16[320,256]{1,0:T(8,128)(2,1)S(1)}, bf16[320,256]{1,0:T(8,128)(2,1)S(1)}, u32[]{:S(2)}, u32[]{:S(2)}) collective-permute-start(bf16[320,256]{1,0:T(8,128)(2,1)S(1)} %add_convert_fusion.1), channel_id=1, source_target_pairs={{0,2},{1,3},{2,0},{3,1},{4,6},{5,7},{6,4},{7,5},{8,10},{9,11},{10,... | collective-permute-start | bytes 491528 | tf_op jit(solution)/shard_map/ppermute | solution.py:292
  84.6 21.2 %collective-permute-start.3 = (bf16[320,768]{1,0:T(8,128)(2,1)S(1)}, bf16[320,768]{1,0:T(8,128)(2,1)S(1)}, u32[]{:S(2)}, u32[]{:S(2)}) collective-permute-start(bf16[320,768]{1,0:T(8,128)(2,1)S(1)} %parts.6), channel_id=1, source_target_pairs={{0,1},{1,0},{2,3},{3,2},{4,5},{5,4},{6,7},{7,6},{8,9},{9,8},{10,11... | collective-permute-start | bytes 1474568 | tf_op jit(solution)/shard_map/ppermute | solution.py:294
  88.7 17.0 %collective-permute-start.4 = (bf16[320,512]{1,0:T(8,128)(2,1)S(1)}, bf16[320,512]{1,0:T(8,128)(2,1)S(1)}, u32[]{:S(2)}, u32[]{:S(2)}) collective-permute-start(bf16[320,512]{1,0:T(8,128)(2,1)S(1)} %add_convert_fusion), channel_id=1, source_target_pairs={{0,2},{1,3},{2,0},{3,1},{4,6},{5,7},{6,4},{7,5},{8,10},{9,11},{10,... | collective-permute-start | bytes 983048 | tf_op jit(solution)/shard_map/ppermute | solution.py:298
  93.5 35.4 %copy-start = (bf16[1,1536,1024]{2,1,0:T(8,128)(2,1)S(1)}, bf16[1,1536,1024]{2,1,0:T(8,128)(2,1)}, u32[]{:S(2)}) copy-start(bf16[1,1536,1024]{2,1,0:T(8,128)(2,1)} %param.13) | copy-start | bytes 9437188
  128.9 12.0 %copy-start.5 = (s32[128,8]{0,1:T(8,128)S(1)}, s32[128,8]{0,1:T(8,128)}, u32[]{:S(2)}) copy-start(s32[128,8]{0,1:T(8,128)} %param.10) | copy-start | bytes 12292
  128.9 12.1 %copy-start.6 = (f32[128,8]{0,1:T(8,128)S(1)}, f32[128,8]{0,1:T(8,128)}, u32[]{:S(2)}) copy-start(f32[128,8]{0,1:T(8,128)} %param.11) | copy-start | bytes 12292
  128.9 12.2 %copy-start.1 = (bf16[512,16]{1,0:T(8,128)(2,1)S(1)}, bf16[512,16]{1,0:T(8,128)(2,1)}, u32[]{:S(2)}) copy-start(bf16[512,16]{1,0:T(8,128)(2,1)} %constant.20.clone.quarter_ref) | copy-start | bytes 49156
  128.9 12.2 %copy-start.2 = (bf16[32,1280]{1,0:T(8,128)(2,1)S(1)}, bf16[32,1280]{1,0:T(8,128)(2,1)}, u32[]{:S(2)}) copy-start(bf16[32,1280]{1,0:T(8,128)(2,1)} %constant.18.clone.expert_ref) | copy-start | bytes 245764
  128.9 12.2 %copy-start.3 = (bf16[16,1280]{1,0:T(8,128)(2,1)S(1)}, bf16[16,1280]{1,0:T(8,128)(2,1)}, u32[]{:S(2)}) copy-start(bf16[16,1280]{1,0:T(8,128)(2,1)} %constant.19.clone.slot_ref) | copy-start | bytes 122884
  128.9 12.2 %copy-start.4 = (bf16[128,128]{1,0:T(8,128)(2,1)S(1)}, bf16[128,128]{1,0:T(8,128)(2,1)}, u32[]{:S(2)}) copy-start(bf16[128,128]{1,0:T(8,128)(2,1)} %constant.17.clone.earlier_ref) | copy-start | bytes 98308
  131.7 42.6 %all-to-all-start.1 = ((bf16[32,40,256]{2,1,0:T(8,128)(2,1)}), bf16[32,40,256]{2,1,0:T(8,128)(2,1)S(1)}, u32[]{:S(2)}, u32[]{:S(2)}) async-start(bf16[32,40,256]{2,1,0:T(8,128)(2,1)} %bitcast.7), calls=%async_computation.1 | async-start | bytes 1310720 | tf_op jit(solution)/shard_map/all_to_all | solution.py:309

commit v5 on v4

--- a/solution.py
+++ b/solution.py
@@ -110,15 +110,29 @@
     )(ids_t, tokens)
 
 
-def first_kernel(me_ref, x_ref, weight_ref, rows_ref, out_ref):
+def first_kernel(me_ref, x_ref, weight_ref, rows_ref, first_ref, rest_ref):
     cols = x_ref.shape[1]
     span, slab = GROUP * BLOCK, GROUP * CAP
-    regroup = regroup_matrix(False)
-    for g in range(x_ref.shape[0] // span):
-        sorted_rows = mm(regroup, x_ref[g * span : (g + 1) * span, :]).astype(BF16)
-        for q in range(QUARTERS):
-            rows_ref[g * slab : (g + 1) * slab, q * cols : (q + 1) * cols] = sorted_rows[q * slab : (q + 1) * slab]
-    out_ref[...] = mm_t(rows_ref[...], weight_ref[...].reshape(2 * PIECE, -1)).astype(BF16)
+    step = pl.program_id(0)
+
+    @pl.when(step == 0)
+    def _():
+        regroup = regroup_matrix(False)
+        for g in range(x_ref.shape[0] // span):
+            sorted_rows = mm(regroup, x_ref[g * span : (g + 1) * span, :]).astype(BF16)
+            for q in range(QUARTERS):
+                rows_ref[g * slab : (g + 1) * slab, q * cols : (q + 1) * cols] = sorted_rows[q * slab : (q + 1) * slab]
+
+    product = mm_t(rows_ref[...], weight_ref[...].reshape(2 * PIECE, -1)).astype(BF16)
+
+    @pl.when(step == 0)
+    def _():
+        first_ref[...] = product
+
+    for p in range(rest_ref.shape[1] // (2 * PIECE)):
+        @pl.when(step == p + 1)
+        def _():
+            rest_ref[:, p * 2 * PIECE : (p + 1) * 2 * PIECE] = product
 
 
 def piece_of(weights, quarter, mask, piece):
@@ -129,19 +143,21 @@
     places, cols = received.shape
     rows = places // QUARTERS
     features = weights.shape[3]
+    pieces = weights.shape[1] // QUARTERS
     whole = lambda shape: pl.BlockSpec(shape, lambda i, me: (0, 0))
+    shapes = [(rows, features), (rows, 2 * PIECE), (rows, 2 * PIECE * (pieces - 1))]
     return pl.pallas_call(
         first_kernel,
-        out_shape=(jax.ShapeDtypeStruct((rows, features), BF16), jax.ShapeDtypeStruct((rows, 2 * PIECE), BF16)),
+        out_shape=tuple(jax.ShapeDtypeStruct(shape, BF16) for shape in shapes),
         grid_spec=pltpu.PrefetchScalarGridSpec(
             num_scalar_prefetch=1,
-            grid=(1,),
+            grid=(pieces,),
             in_specs=[whole((places, cols)),
-                      pl.BlockSpec((2, 1, PIECE, features), lambda i, me: (0, piece_of(weights, me[0], mask, 0), 0, 0))],
-            out_specs=(whole((rows, features)), whole((rows, 2 * PIECE))),
+                      pl.BlockSpec((2, 1, PIECE, features), lambda i, me: (0, piece_of(weights, me[0], mask, i), 0, 0))],
+            out_specs=tuple(whole(shape) for shape in shapes),
         ),
         compiler_params=PARAMS,
-        cost_estimate=pl.CostEstimate(flops=4 * rows * PIECE * features, bytes_accessed=4 * PIECE * features, transcendentals=0),
+        cost_estimate=pl.CostEstimate(flops=4 * rows * pieces * PIECE * features, bytes_accessed=4 * pieces * PIECE * features, transcendentals=0),
         name="first",
     )(me, received, weights)
 
@@ -241,19 +257,22 @@
 
 
 def combine_kernel(mixer_ref, returned_ref, out_ref):
-    out_ref[...] = mm(mixer_ref[...], returned_ref[...]).astype(BF16)
+    rows = out_ref.shape[0]
+    cols = returned_ref.shape[1]
+    for q in range(QUARTERS):
+        mixed = mm(mixer_ref[q * rows : (q + 1) * rows, :], returned_ref[...])
+        out_ref[:, q * cols : (q + 1) * cols] = mixed.astype(BF16)
 
 
 def combine(mix, returned):
-    places, cols = returned.shape
-    rows = mix.shape[0] // QUARTERS
+    cols = returned.shape[1]
+    vmem = pl.BlockSpec(memory_space=pltpu.VMEM)
     return pl.pallas_call(
         combine_kernel,
-        out_shape=jax.ShapeDtypeStruct((rows, QUARTERS * cols), BF16),
-        grid=(QUARTERS,),
-        in_specs=[pl.BlockSpec((rows, places), lambda i: (i, 0)), pl.BlockSpec((places, cols), lambda i: (0, 0))],
-        out_specs=pl.BlockSpec((rows, cols), lambda i: (0, i)),
-        compiler_params=PARAMS,
+        out_shape=jax.ShapeDtypeStruct((mix.shape[0] // QUARTERS, QUARTERS * cols), BF16),
+        in_specs=[vmem, vmem],
+        out_specs=vmem,
+        compiler_params=pltpu.CompilerParams(vmem_limit_bytes=24 * 1024 * 1024),
         name="combine",
     )(mix, returned)
 
@@ -281,11 +300,9 @@
     sent = pack(expert_ids.T, tokens, flight)
     received = lax.all_to_all(sent.reshape(flight, BLOCK, cols), "ep", 0, 0, tiled=True).reshape(flight * BLOCK, cols)
 
-    rows, far_1 = first_part(me, 3, received, up_weights)
+    rows, far_1, far_2 = first_part(me, 3, received, up_weights)
     got_1 = lax.ppermute(far_1, "tp", near)
-    (far_2,) = parts(me, 3, rows, up_weights, pieces - 1, start=1)
     got_2 = lax.ppermute(far_2, "tp", near)
-    rows, far_2 = tie(rows, far_2)
     keep_1, keep_2 = parts(me, 2, rows, up_weights, 1, pieces - 1)
     pair_1 = pair_sum(got_1, keep_1)
     rows, pair_1 = tie(rows, pair_1)

time: 178 us -> 175 us (0.983)
    ppermute x1, waiting for transfers between devices: 12.2 us -> 10.1 us  [local(): got_2 = lax.ppermute(pair_2, 'tp', far)]
    pallas_call x4 -> x3, Pallas kernels: 10.5 us -> 8.67 us  [parts(): pl.pallas_call(functools.partial(parts_kernel, pieces), out_shape=tuple((...]
  transfers between devices with their start and end apart: 7 -> 7, of which waited for: 4 -> 4; matrix products, arithmetic and copies ran while one was open for 0% -> 0% of each run, Pallas kernels for 8% -> 7%
where the time goes in v5:
time: 175 us; the launch traced here: 174 us
  waiting for transfers between devices  79.8 us (46%)
  starting transfers between devices  49.7 us (28%)
  Pallas kernels  22.1 us (13%)
  blocking collectives  21.2 us (12%)
    all_to_all x1, waiting for transfers between devices, local(): lax.all_to_all(sent.reshape(flight, BLOCK, cols), 'ep', 0, 0, tiled=True)  37.4 us
    all_to_all x1, waiting for transfers between devices, local(): lax.all_to_all(result.reshape(flight, BLOCK, cols), 'ep', 0, 0, tiled=True)  31.1 us
    all_to_all x1, starting transfers between devices, local(): lax.all_to_all(sent.reshape(flight, BLOCK, cols), 'ep', 0, 0, tiled=True)  24.3 us
    all_gather x1, blocking collectives, local(): lax.all_gather(jnp.concatenate(hidden, axis=1), 'tp', axis=0, tiled=False)  21.2 us
    ppermute x1, waiting for transfers between devices, local(): got_2 = lax.ppermute(pair_2, 'tp', far)  10.1 us
    all_to_all x1, starting transfers between devices, local(): lax.all_to_all(result.reshape(flight, BLOCK, cols), 'ep', 0, 0, tiled=True)  9.39 us
    pallas_call x3, Pallas kernels, parts(): pl.pallas_call(functools.partial(parts_kernel, pieces), out_shape=tuple((...  8.67 us
    ppermute x1, starting transfers between devices, local(): got_1 = lax.ppermute(pair_1, 'tp', far)  4.28 us
  transfers between devices with their start and end apart: 7, of which 4 were waited for; matrix products, arithmetic and copies ran while one was open for 0% of the time, Pallas kernels for 7%

profile of v5, /device:TPU:56, one launch (start us, length us, event | category | flops | bytes accessed | tf_op | source)
XLA Modules:
  0.0 173.8 jit_solution(9398856741569251595)
XLA Ops:
  0.0 3.0 %pack.1 = bf16[1280,256]{1,0:T(8,128)(2,1)} custom-call(s32[8,128]{1,0:T(8,128)} %bitcast.18, bf16[128,1024]{1,0:T(8,128)(2,1)} %token_ref.1), custom_call_target="tpu_custom_call" | custom-call | tf_op jit(solution)/shard_map/pack/pallas_call | solution.py:102
  3.1 24.3 %all-to-all-start = ((bf16[32,40,256]{2,1,0:T(8,128)(2,1)}), bf16[32,40,256]{2,1,0:T(8,128)(2,1)S(1)}, u32[]{:S(2)}, u32[]{:S(2)}) async-start(bf16[32,40,256]{2,1,0:T(8,128)(2,1)} %bitcast.17), calls=%async_computation | async-start | bytes 1310720 | tf_op jit(solution)/shard_map/all_to_all | solution.py:301
  27.3 37.4 %all-to-all-done = bf16[32,40,256]{2,1,0:T(8,128)(2,1)S(1)} async-done(((bf16[32,40,256]{2,1,0:T(8,128)(2,1)}), bf16[32,40,256]{2,1,0:T(8,128)(2,1)S(1)}, u32[]{:S(2)}, u32[]{:S(2)}) %all-to-all-start) | async-done | bytes 655392 | tf_op jit(solution)/shard_map/all_to_all | solution.py:301
  64.7 3.4 %first.1 = (bf16[320,1024]{1,0:T(8,128)(2,1)S(1)}, bf16[320,256]{1,0:T(8,128)(2,1)S(1)}, bf16[320,512]{1,0:T(8,128)(2,1)S(1)}) custom-call(s32[1]{0:T(128)} %bitcast.me_ref, bf16[1280,256]{1,0:T(8,128)(2,1)S(1)} %bitcast.12, bf16[2,12,128,1024]{3,2,1,0:T(8,128)(2,1)} %bitcast.13), custom_call_target="tpu_custom_call" | custom-call | flops 503316480 | bytes 1572864 | tf_op jit(solution)/shard_map/first/pallas_call | solution.py:149
  68.1 3.3 %collective-permute-start = (bf16[320,256]{1,0:T(8,128)(2,1)S(1)}, bf16[320,256]{1,0:T(8,128)(2,1)S(1)}, u32[]{:S(2)}, u32[]{:S(2)}) collective-permute-start(bf16[320,256]{1,0:T(8,128)(2,1)S(1)} %get-tuple-element.17), channel_id=1, source_target_pairs={{0,1},{1,0},{2,3},{3,2},{4,5},{5,4},{6,7},{7,6},{8,9},{9,8},{10,11... | collective-permute-start | bytes 491528 | tf_op jit(solution)/shard_map/ppermute | solution.py:304
  71.4 2.6 %collective-permute-start.1 = (bf16[320,512]{1,0:T(8,128)(2,1)S(1)}, bf16[320,512]{1,0:T(8,128)(2,1)S(1)}, u32[]{:S(2)}, u32[]{:S(2)}) collective-permute-start(bf16[320,512]{1,0:T(8,128)(2,1)S(1)} %get-tuple-element.20), channel_id=1, source_target_pairs={{0,1},{1,0},{2,3},{3,2},{4,5},{5,4},{6,7},{7,6},{8,9},{9,8},{10,11... | collective-permute-start | bytes 983048 | tf_op jit(solution)/shard_map/ppermute | solution.py:305
  74.0 2.9 %parts.3 = (bf16[320,256]{1,0:T(8,128)(2,1)S(1)}, bf16[320,512]{1,0:T(8,128)(2,1)S(1)}) custom-call(s32[1]{0:T(128)} %bitcast.me_ref, bf16[320,1024]{1,0:T(8,128)(2,1)S(1)} %get-tuple-element.25.rows_ref, bf16[2,12,128,1024]{3,2,1,0:T(8,128)(2,1)} %bitcast.14), custom_call_target="tpu_custom_call" | custom-call | flops 503316480 | bytes 1572864 | tf_op jit(solution)/shard_map/parts/pallas_call | solution.py:179
  76.9 4.3 %collective-permute-start.2 = (bf16[320,256]{1,0:T(8,128)(2,1)S(1)}, bf16[320,256]{1,0:T(8,128)(2,1)S(1)}, u32[]{:S(2)}, u32[]{:S(2)}) collective-permute-start(bf16[320,256]{1,0:T(8,128)(2,1)S(1)} %add_convert_fusion.1), channel_id=1, source_target_pairs={{0,2},{1,3},{2,0},{3,1},{4,6},{5,7},{6,4},{7,5},{8,10},{9,11},{10,... | collective-permute-start | bytes 491528 | tf_op jit(solution)/shard_map/ppermute | solution.py:309
  81.2 2.9 %parts.4 = bf16[320,768]{1,0:T(8,128)(2,1)S(1)} custom-call(s32[1]{0:T(128)} %bitcast.me_ref, bf16[320,1024]{1,0:T(8,128)(2,1)S(1)} %get-tuple-element.25.rows_ref, bf16[2,12,128,1024]{3,2,1,0:T(8,128)(2,1)} %bitcast.15), custom_call_target="tpu_custom_call" | custom-call | flops 503316480 | bytes 1572864 | tf_op jit(solution)/shard_map/parts/pallas_call | solution.py:179
  84.1 4.0 %collective-permute-start.3 = (bf16[320,768]{1,0:T(8,128)(2,1)S(1)}, bf16[320,768]{1,0:T(8,128)(2,1)S(1)}, u32[]{:S(2)}, u32[]{:S(2)}) collective-permute-start(bf16[320,768]{1,0:T(8,128)(2,1)S(1)} %parts.4), channel_id=1, source_target_pairs={{0,1},{1,0},{2,3},{3,2},{4,5},{5,4},{6,7},{7,6},{8,9},{9,8},{10,11... | collective-permute-start | bytes 1474568 | tf_op jit(solution)/shard_map/ppermute | solution.py:311
  88.3 1.9 %collective-permute-start.4 = (bf16[320,512]{1,0:T(8,128)(2,1)S(1)}, bf16[320,512]{1,0:T(8,128)(2,1)S(1)}, u32[]{:S(2)}, u32[]{:S(2)}) collective-permute-start(bf16[320,512]{1,0:T(8,128)(2,1)S(1)} %add_convert_fusion), channel_id=1, source_target_pairs={{0,2},{1,3},{2,0},{3,1},{4,6},{5,7},{6,4},{7,5},{8,10},{9,11},{10,... | collective-permute-start | bytes 983048 | tf_op jit(solution)/shard_map/ppermute | solution.py:315
  90.2 2.9 %parts.5 = bf16[320,768]{1,0:T(8,128)(2,1)S(1)} custom-call(s32[1]{0:T(128)} %bitcast.me_ref, bf16[320,1024]{1,0:T(8,128)(2,1)S(1)} %get-tuple-element.25.rows_ref, bf16[2,12,128,1024]{3,2,1,0:T(8,128)(2,1)} %bitcast.16), custom_call_target="tpu_custom_call" | custom-call | flops 503316480 | bytes 1572864 | tf_op jit(solution)/shard_map/parts/pallas_call | solution.py:179
  93.1 10.1 %collective-permute-done.4 = bf16[320,512]{1,0:T(8,128)(2,1)S(1)} collective-permute-done((bf16[320,512]{1,0:T(8,128)(2,1)S(1)}, bf16[320,512]{1,0:T(8,128)(2,1)S(1)}, u32[]{:S(2)}, u32[]{:S(2)}) %collective-permute-start.4) | collective-permute-done | bytes 327712 | tf_op jit(solution)/shard_map/ppermute | solution.py:315
  103.2 1.3 collective-permute-done.3
  104.5 0.2 convert_add_fusion.1
  104.8 0.1 fusion
  104.9 21.2 %all-gather = bf16[1280,384]{1,0:T(8,128)(2,1)S(1)} all-gather(bf16[320,384]{1,0:T(8,128)(2,1)S(1)} %pad_maximum_fusion), channel_id=2, replica_groups=mesh['dp'=8,'ep'=32,'tp'=4] {'tp'}, dimensions={0}, use_global_device_ids=true | all-gather | bytes 1228800 | tf_op jit(solution)/shard_map/all_gather | solution.py:323
  126.2 2.8 %down.1 = bf16[1280,256]{1,0:T(8,128)(2,1)} custom-call(bf16[4,320,384]{2,1,0:T(8,128)(2,1)S(1)} %bitcast.9, bf16[4,384,1024]{2,1,0:T(8,128)(2,1)S(1)} %bitcast.10), custom_call_target="tpu_custom_call" | custom-call | tf_op jit(solution)/shard_map/down/pallas_call | solution.py:213
  129.0 9.4 %all-to-all-start.1 = ((bf16[32,40,256]{2,1,0:T(8,128)(2,1)}), bf16[32,40,256]{2,1,0:T(8,128)(2,1)S(1)}, u32[]{:S(2)}, u32[]{:S(2)}) async-start(bf16[32,40,256]{2,1,0:T(8,128)(2,1)} %bitcast.7), calls=%async_computation.1 | async-start | bytes 1310720 | tf_op jit(solution)/shard_map/all_to_all | solution.py:326
  138.4 0.1 copy.10.ids_ref
  138.5 0.1 copy.11.weight_ref
  138.6 2.9 %mixer.1.mixer_ref = bf16[512,1280]{1,0:T(8,128)(2,1)S(1)} custom-call(s32[128,8]{1,0:T(8,128)S(1)} %copy.10.ids_ref, f32[128,8]{1,0:T(8,128)S(1)} %copy.11.weight_ref, bf16[128,128]{1,0:T(8,128)(2,1)S(1)} %copy-done.4, bf16[32,1280]{1,0:T(8,128)(2,1)S(1)} %copy-done.2, bf16[16,1280]{1,0:T(8,128)(2,1)S(1)} %copy-done.3, bf16[512,16]{1,0:T(8,128)(2,1)S(1)} %copy-done.1), custom_call_target="tpu_custom_call" | custom-call | tf_op jit(solution)/shard_map/mixer/pallas_call | solution.py:247
  141.6 31.1 %all-to-all-done.1 = bf16[32,40,256]{2,1,0:T(8,128)(2,1)S(1)} async-done(((bf16[32,40,256]{2,1,0:T(8,128)(2,1)}), bf16[32,40,256]{2,1,0:T(8,128)(2,1)S(1)}, u32[]{:S(2)}, u32[]{:S(2)}) %all-to-all-start.1) | async-done | bytes 655392 | tf_op jit(solution)/shard_map/all_to_all | solution.py:326
  172.6 1.2 combine.1
  (21 shorter events, 0.3 us)
Async XLA Ops:
  3.1 61.6 %all-to-all-start = ((bf16[32,40,256]{2,1,0:T(8,128)(2,1)}), bf16[32,40,256]{2,1,0:T(8,128)(2,1)S(1)}, u32[]{:S(2)}, u32[]{:S(2)}) async-start(bf16[32,40,256]{2,1,0:T(8,128)(2,1)} %bitcast.17), calls=%async_computation | async-start | bytes 1310720 | tf_op jit(solution)/shard_map/all_to_all | solution.py:301
  68.1 8.8 %collective-permute-start = (bf16[320,256]{1,0:T(8,128)(2,1)S(1)}, bf16[320,256]{1,0:T(8,128)(2,1)S(1)}, u32[]{:S(2)}, u32[]{:S(2)}) collective-permute-start(bf16[320,256]{1,0:T(8,128)(2,1)S(1)} %get-tuple-element.17), channel_id=1, source_target_pairs={{0,1},{1,0},{2,3},{3,2},{4,5},{5,4},{6,7},{7,6},{8,9},{9,8},{10,11... | collective-permute-start | bytes 491528 | tf_op jit(solution)/shard_map/ppermute | solution.py:304
  71.4 16.8 %collective-permute-start.1 = (bf16[320,512]{1,0:T(8,128)(2,1)S(1)}, bf16[320,512]{1,0:T(8,128)(2,1)S(1)}, u32[]{:S(2)}, u32[]{:S(2)}) collective-permute-start(bf16[320,512]{1,0:T(8,128)(2,1)S(1)} %get-tuple-element.20), channel_id=1, source_target_pairs={{0,1},{1,0},{2,3},{3,2},{4,5},{5,4},{6,7},{7,6},{8,9},{9,8},{10,11... | collective-permute-start | bytes 983048 | tf_op jit(solution)/shard_map/ppermute | solution.py:305
  76.9 11.3 %collective-permute-start.2 = (bf16[320,256]{1,0:T(8,128)(2,1)S(1)}, bf16[320,256]{1,0:T(8,128)(2,1)S(1)}, u32[]{:S(2)}, u32[]{:S(2)}) collective-permute-start(bf16[320,256]{1,0:T(8,128)(2,1)S(1)} %add_convert_fusion.1), channel_id=1, source_target_pairs={{0,2},{1,3},{2,0},{3,1},{4,6},{5,7},{6,4},{7,5},{8,10},{9,11},{10,... | collective-permute-start | bytes 491528 | tf_op jit(solution)/shard_map/ppermute | solution.py:309
  84.1 20.4 %collective-permute-start.3 = (bf16[320,768]{1,0:T(8,128)(2,1)S(1)}, bf16[320,768]{1,0:T(8,128)(2,1)S(1)}, u32[]{:S(2)}, u32[]{:S(2)}) collective-permute-start(bf16[320,768]{1,0:T(8,128)(2,1)S(1)} %parts.4), channel_id=1, source_target_pairs={{0,1},{1,0},{2,3},{3,2},{4,5},{5,4},{6,7},{7,6},{8,9},{9,8},{10,11... | collective-permute-start | bytes 1474568 | tf_op jit(solution)/shard_map/ppermute | solution.py:311
  88.3 14.9 %collective-permute-start.4 = (bf16[320,512]{1,0:T(8,128)(2,1)S(1)}, bf16[320,512]{1,0:T(8,128)(2,1)S(1)}, u32[]{:S(2)}, u32[]{:S(2)}) collective-permute-start(bf16[320,512]{1,0:T(8,128)(2,1)S(1)} %add_convert_fusion), channel_id=1, source_target_pairs={{0,2},{1,3},{2,0},{3,1},{4,6},{5,7},{6,4},{7,5},{8,10},{9,11},{10,... | collective-permute-start | bytes 983048 | tf_op jit(solution)/shard_map/ppermute | solution.py:315
  93.1 33.1 %copy-start = (bf16[1,1536,1024]{2,1,0:T(8,128)(2,1)S(1)}, bf16[1,1536,1024]{2,1,0:T(8,128)(2,1)}, u32[]{:S(2)}) copy-start(bf16[1,1536,1024]{2,1,0:T(8,128)(2,1)} %param.13) | copy-start | bytes 9437188
  126.1 12.3 %copy-start.5 = (s32[128,8]{0,1:T(8,128)S(1)}, s32[128,8]{0,1:T(8,128)}, u32[]{:S(2)}) copy-start(s32[128,8]{0,1:T(8,128)} %param.10) | copy-start | bytes 12292
  126.1 12.4 %copy-start.6 = (f32[128,8]{0,1:T(8,128)S(1)}, f32[128,8]{0,1:T(8,128)}, u32[]{:S(2)}) copy-start(f32[128,8]{0,1:T(8,128)} %param.11) | copy-start | bytes 12292
  126.1 12.5 %copy-start.1 = (bf16[512,16]{1,0:T(8,128)(2,1)S(1)}, bf16[512,16]{1,0:T(8,128)(2,1)}, u32[]{:S(2)}) copy-start(bf16[512,16]{1,0:T(8,128)(2,1)} %constant.20.clone.quarter_ref) | copy-start | bytes 49156
  126.1 12.5 %copy-start.2 = (bf16[32,1280]{1,0:T(8,128)(2,1)S(1)}, bf16[32,1280]{1,0:T(8,128)(2,1)}, u32[]{:S(2)}) copy-start(bf16[32,1280]{1,0:T(8,128)(2,1)} %constant.18.clone.expert_ref) | copy-start | bytes 245764
  126.1 12.5 %copy-start.3 = (bf16[16,1280]{1,0:T(8,128)(2,1)S(1)}, bf16[16,1280]{1,0:T(8,128)(2,1)}, u32[]{:S(2)}) copy-start(bf16[16,1280]{1,0:T(8,128)(2,1)} %constant.19.clone.slot_ref) | copy-start | bytes 122884
  126.2 12.5 %copy-start.4 = (bf16[128,128]{1,0:T(8,128)(2,1)S(1)}, bf16[128,128]{1,0:T(8,128)(2,1)}, u32[]{:S(2)}) copy-start(bf16[128,128]{1,0:T(8,128)(2,1)} %constant.17.clone.earlier_ref) | copy-start | bytes 98308
  129.0 43.6 %all-to-all-start.1 = ((bf16[32,40,256]{2,1,0:T(8,128)(2,1)}), bf16[32,40,256]{2,1,0:T(8,128)(2,1)S(1)}, u32[]{:S(2)}, u32[]{:S(2)}) async-start(bf16[32,40,256]{2,1,0:T(8,128)(2,1)} %bitcast.7), calls=%async_computation.1 | async-start | bytes 1310720 | tf_op jit(solution)/shard_map/all_to_all | solution.py:326

commit v6 on v5

--- a/solution.py
+++ b/solution.py
@@ -110,56 +110,41 @@
     )(ids_t, tokens)
 
 
-def first_kernel(me_ref, x_ref, weight_ref, rows_ref, first_ref, rest_ref):
+def first_kernel(x_ref, weight_ref, rows_ref, first_ref, rest_ref):
     cols = x_ref.shape[1]
     span, slab = GROUP * BLOCK, GROUP * CAP
-    step = pl.program_id(0)
-
-    @pl.when(step == 0)
-    def _():
-        regroup = regroup_matrix(False)
-        for g in range(x_ref.shape[0] // span):
-            sorted_rows = mm(regroup, x_ref[g * span : (g + 1) * span, :]).astype(BF16)
-            for q in range(QUARTERS):
-                rows_ref[g * slab : (g + 1) * slab, q * cols : (q + 1) * cols] = sorted_rows[q * slab : (q + 1) * slab]
-
-    product = mm_t(rows_ref[...], weight_ref[...].reshape(2 * PIECE, -1)).astype(BF16)
-
-    @pl.when(step == 0)
-    def _():
-        first_ref[...] = product
-
-    for p in range(rest_ref.shape[1] // (2 * PIECE)):
-        @pl.when(step == p + 1)
-        def _():
-            rest_ref[:, p * 2 * PIECE : (p + 1) * 2 * PIECE] = product
+    regroup = regroup_matrix(False)
+    for g in range(x_ref.shape[0] // span):
+        sorted_rows = mm(regroup, x_ref[g * span : (g + 1) * span, :]).astype(BF16)
+        for q in range(QUARTERS):
+            rows_ref[g * slab : (g + 1) * slab, q * cols : (q + 1) * cols] = sorted_rows[q * slab : (q + 1) * slab]
+    for piece in range(weight_ref.shape[1]):
+        product = mm_t(rows_ref[...], weight_ref[:, piece].reshape(2 * PIECE, -1)).astype(BF16)
+        if piece == 0:
+            first_ref[...] = product
+        else:
+            rest_ref[:, (piece - 1) * 2 * PIECE : piece * 2 * PIECE] = product
 
 
 def piece_of(weights, quarter, mask, piece):
     return (quarter ^ mask) * (weights.shape[1] // QUARTERS) + piece
 
 
-def first_part(me, mask, received, weights):
+def first_part(received, weights):
     places, cols = received.shape
-    rows = places // QUARTERS
-    features = weights.shape[3]
-    pieces = weights.shape[1] // QUARTERS
-    whole = lambda shape: pl.BlockSpec(shape, lambda i, me: (0, 0))
+    rows, features = places // QUARTERS, QUARTERS * cols
+    pieces = weights.shape[1]
     shapes = [(rows, features), (rows, 2 * PIECE), (rows, 2 * PIECE * (pieces - 1))]
+    vmem = pl.BlockSpec(memory_space=pltpu.VMEM)
     return pl.pallas_call(
         first_kernel,
         out_shape=tuple(jax.ShapeDtypeStruct(shape, BF16) for shape in shapes),
-        grid_spec=pltpu.PrefetchScalarGridSpec(
-            num_scalar_prefetch=1,
-            grid=(pieces,),
-            in_specs=[whole((places, cols)),
-                      pl.BlockSpec((2, 1, PIECE, features), lambda i, me: (0, piece_of(weights, me[0], mask, i), 0, 0))],
-            out_specs=tuple(whole(shape) for shape in shapes),
-        ),
-        compiler_params=PARAMS,
-        cost_estimate=pl.CostEstimate(flops=4 * rows * pieces * PIECE * features, bytes_accessed=4 * pieces * PIECE * features, transcendentals=0),
+        in_specs=[vmem, vmem],
+        out_specs=(vmem,) * 3,
+        compiler_params=pltpu.CompilerParams(vmem_limit_bytes=24 * 1024 * 1024),
+        cost_estimate=pl.CostEstimate(flops=2 * rows * weights.size, bytes_accessed=2 * weights.size, transcendentals=0),
         name="first",
-    )(me, received, weights)
+    )(received, weights)
 
 
 def parts_kernel(pieces, me_ref, rows_ref, weight_ref, *out_refs):
@@ -195,10 +180,8 @@
 def down_kernel(hidden_ref, weight_ref, out_ref):
     cols = out_ref.shape[1]
     span, slab = GROUP * BLOCK, GROUP * CAP
-    total = mm(hidden_ref[0], weight_ref[0])
-    for k in range(1, hidden_ref.shape[0]):
-        total += mm(hidden_ref[k], weight_ref[k])
-    total = total.astype(BF16)
+    hidden = jnp.concatenate([hidden_ref[k] for k in range(hidden_ref.shape[0])], axis=1)
+    total = mm(hidden, weight_ref[...]).astype(BF16)
     spread = regroup_matrix(True)
     for g in range(out_ref.shape[0] // span):
         block = total[g * slab : (g + 1) * slab, :]
@@ -208,7 +191,7 @@
 
 def down(hidden, weights):
     parts, rows, units = hidden.shape
-    cols = weights.shape[2] // QUARTERS
+    cols = weights.shape[1] // QUARTERS
     vmem = pl.BlockSpec(memory_space=pltpu.VMEM)
     return pl.pallas_call(
         down_kernel,
@@ -289,7 +272,6 @@
     units = gate_up.shape[2] // n_tp
     pieces = units // PIECE
     up_weights = gate_up.reshape(2, n_tp * pieces, PIECE, features)
-    down_weights = down_proj.reshape(n_tp, units, features)
     me = lax.axis_index("tp").astype(jnp.int32).reshape(1)
     near = [(i, i ^ 1) for i in range(n_tp)]
     far = [(i, i ^ 2) for i in range(n_tp)]
@@ -298,9 +280,11 @@
         return (got.astype(F32) + keep.astype(F32)).astype(BF16)
 
     sent = pack(expert_ids.T, tokens, flight)
+    sent, up_weights = tie(sent, up_weights)
+    first_weights = lax.dynamic_slice_in_dim(up_weights, (me[0] ^ 3) * pieces, pieces, axis=1)
     received = lax.all_to_all(sent.reshape(flight, BLOCK, cols), "ep", 0, 0, tiled=True).reshape(flight * BLOCK, cols)
 
-    rows, far_1, far_2 = first_part(me, 3, received, up_weights)
+    rows, far_1, far_2 = first_part(received, first_weights)
     got_1 = lax.ppermute(far_1, "tp", near)
     got_2 = lax.ppermute(far_2, "tp", near)
     keep_1, keep_2 = parts(me, 2, rows, up_weights, 1, pieces - 1)
@@ -322,7 +306,7 @@
         hidden.append((jax.nn.silu(summed[:, :PIECE]) * summed[:, PIECE:]).astype(BF16))
     hidden = lax.all_gather(jnp.concatenate(hidden, axis=1), "tp", axis=0, tiled=False)
 
-    result = down(hidden, down_weights)
+    result = down(hidden, down_proj[0])
     returned = lax.all_to_all(result.reshape(flight, BLOCK, cols), "ep", 0, 0, tiled=True).reshape(flight * BLOCK, cols)
     mix = mixer(expert_ids, route_weight, flight)
     return combine(mix, returned)

time: 175 us -> 172 us (0.983)
  Pallas kernels: 22.1 us -> 19.6 us
    pallas_call x1, Pallas kernels: 3.42 us -> 1.32 us  [first_part(): pl.pallas_call(first_kernel, out_shape=tuple((jax.ShapeDtypeStruct(shape,...]
  transfers between devices with their start and end apart: 7 -> 7, of which waited for: 4 -> 4; matrix products, arithmetic and copies ran while one was open for 0% -> 1% of each run, Pallas kernels for 7% -> 7%
where the time goes in v6:
time: 172 us; the launch traced here: 171 us
  waiting for transfers between devices  78.3 us (46%)
  starting transfers between devices  49.8 us (29%)
  blocking collectives  21.2 us (12%)
  Pallas kernels  19.6 us (11%)
  local copies, waits for them, and re-layouts  1.77 us (1%)
    all_to_all x1, waiting for transfers between devices, local(): lax.all_to_all(sent.reshape(flight, BLOCK, cols), 'ep', 0, 0, tiled=True)  35.8 us
    all_to_all x1, waiting for transfers between devices, local(): lax.all_to_all(result.reshape(flight, BLOCK, cols), 'ep', 0, 0, tiled=True)  31.1 us
    all_to_all x1, starting transfers between devices, local(): lax.all_to_all(sent.reshape(flight, BLOCK, cols), 'ep', 0, 0, tiled=True)  24.3 us
    all_gather x1, blocking collectives, local(): lax.all_gather(jnp.concatenate(hidden, axis=1), 'tp', axis=0, tiled=False)  21.2 us
    ppermute x1, waiting for transfers between devices, local(): got_2 = lax.ppermute(pair_2, 'tp', far)  10.1 us
    all_to_all x1, starting transfers between devices, local(): lax.all_to_all(result.reshape(flight, BLOCK, cols), 'ep', 0, 0, tiled=True)  9.42 us
    pallas_call x3, Pallas kernels, parts(): pl.pallas_call(functools.partial(parts_kernel, pieces), out_shape=tuple((...  8.68 us
    ppermute x1, starting transfers between devices, local(): got_1 = lax.ppermute(pair_1, 'tp', far)  4.29 us
  transfers between devices with their start and end apart: 7, of which 4 were waited for; matrix products, arithmetic and copies ran while one was open for 1% of the time, Pallas kernels for 7%

profile of v6, /device:TPU:56, one launch (start us, length us, event | category | flops | bytes accessed | tf_op | source)
XLA Modules:
  0.0 171.4 jit_solution(2117757517957842707)
XLA Ops:
  0.0 3.0 %pack.1 = bf16[1280,256]{1,0:T(8,128)(2,1)} custom-call(s32[8,128]{1,0:T(8,128)} %bitcast.18, bf16[128,1024]{1,0:T(8,128)(2,1)} %token_ref.1), custom_call_target="tpu_custom_call" | custom-call | tf_op jit(solution)/shard_map/pack/pallas_call | solution.py:102
  3.1 24.3 %all-to-all-start = ((bf16[32,40,256]{2,1,0:T(8,128)(2,1)}), bf16[32,40,256]{2,1,0:T(8,128)(2,1)S(1)}, u32[]{:S(2)}, u32[]{:S(2)}) async-start(bf16[32,40,256]{2,1,0:T(8,128)(2,1)} %bitcast.17), calls=%async_computation | async-start | bytes 1310720 | tf_op jit(solution)/shard_map/all_to_all | solution.py:285
  27.4 1.5 constant_dynamic-slice_fusion.weight_ref
  28.9 35.8 %all-to-all-done = bf16[32,40,256]{2,1,0:T(8,128)(2,1)S(1)} async-done(((bf16[32,40,256]{2,1,0:T(8,128)(2,1)}), bf16[32,40,256]{2,1,0:T(8,128)(2,1)S(1)}, u32[]{:S(2)}, u32[]{:S(2)}) %all-to-all-start) | async-done | bytes 655392 | tf_op jit(solution)/shard_map/all_to_all | solution.py:285
  64.7 1.3 first.1
  66.0 3.3 %collective-permute-start = (bf16[320,256]{1,0:T(8,128)(2,1)S(1)}, bf16[320,256]{1,0:T(8,128)(2,1)S(1)}, u32[]{:S(2)}, u32[]{:S(2)}) collective-permute-start(bf16[320,256]{1,0:T(8,128)(2,1)S(1)} %get-tuple-element.21), channel_id=1, source_target_pairs={{0,1},{1,0},{2,3},{3,2},{4,5},{5,4},{6,7},{7,6},{8,9},{9,8},{10,11... | collective-permute-start | bytes 491528 | tf_op jit(solution)/shard_map/ppermute | solution.py:288
  69.3 2.6 %collective-permute-start.1 = (bf16[320,512]{1,0:T(8,128)(2,1)S(1)}, bf16[320,512]{1,0:T(8,128)(2,1)S(1)}, u32[]{:S(2)}, u32[]{:S(2)}) collective-permute-start(bf16[320,512]{1,0:T(8,128)(2,1)S(1)} %get-tuple-element.24), channel_id=1, source_target_pairs={{0,1},{1,0},{2,3},{3,2},{4,5},{5,4},{6,7},{7,6},{8,9},{9,8},{10,11... | collective-permute-start | bytes 983048 | tf_op jit(solution)/shard_map/ppermute | solution.py:289
  71.9 2.9 %parts.3 = (bf16[320,256]{1,0:T(8,128)(2,1)S(1)}, bf16[320,512]{1,0:T(8,128)(2,1)S(1)}) custom-call(s32[1]{0:T(128)} %bitcast.4.me_ref, bf16[320,1024]{1,0:T(8,128)(2,1)S(1)} %get-tuple-element.29.rows_ref, bf16[2,12,128,1024]{3,2,1,0:T(8,128)(2,1)} %bitcast.14), custom_call_target="tpu_custom_call" | custom-call | flops 503316480 | bytes 1572864 | tf_op jit(solution)/shard_map/parts/pallas_call | solution.py:164
  74.8 4.3 %collective-permute-start.2 = (bf16[320,256]{1,0:T(8,128)(2,1)S(1)}, bf16[320,256]{1,0:T(8,128)(2,1)S(1)}, u32[]{:S(2)}, u32[]{:S(2)}) collective-permute-start(bf16[320,256]{1,0:T(8,128)(2,1)S(1)} %add_convert_fusion.1), channel_id=1, source_target_pairs={{0,2},{1,3},{2,0},{3,1},{4,6},{5,7},{6,4},{7,5},{8,10},{9,11},{10,... | collective-permute-start | bytes 491528 | tf_op jit(solution)/shard_map/ppermute | solution.py:293
  79.1 2.9 %parts.4 = bf16[320,768]{1,0:T(8,128)(2,1)S(1)} custom-call(s32[1]{0:T(128)} %bitcast.4.me_ref, bf16[320,1024]{1,0:T(8,128)(2,1)S(1)} %get-tuple-element.29.rows_ref, bf16[2,12,128,1024]{3,2,1,0:T(8,128)(2,1)} %bitcast.15), custom_call_target="tpu_custom_call" | custom-call | flops 503316480 | bytes 1572864 | tf_op jit(solution)/shard_map/parts/pallas_call | solution.py:164
  82.0 4.0 %collective-permute-start.3 = (bf16[320,768]{1,0:T(8,128)(2,1)S(1)}, bf16[320,768]{1,0:T(8,128)(2,1)S(1)}, u32[]{:S(2)}, u32[]{:S(2)}) collective-permute-start(bf16[320,768]{1,0:T(8,128)(2,1)S(1)} %parts.4), channel_id=1, source_target_pairs={{0,1},{1,0},{2,3},{3,2},{4,5},{5,4},{6,7},{7,6},{8,9},{9,8},{10,11... | collective-permute-start | bytes 1474568 | tf_op jit(solution)/shard_map/ppermute | solution.py:295
  86.2 1.9 %collective-permute-start.4 = (bf16[320,512]{1,0:T(8,128)(2,1)S(1)}, bf16[320,512]{1,0:T(8,128)(2,1)S(1)}, u32[]{:S(2)}, u32[]{:S(2)}) collective-permute-start(bf16[320,512]{1,0:T(8,128)(2,1)S(1)} %add_convert_fusion), channel_id=1, source_target_pairs={{0,2},{1,3},{2,0},{3,1},{4,6},{5,7},{6,4},{7,5},{8,10},{9,11},{10,... | collective-permute-start | bytes 983048 | tf_op jit(solution)/shard_map/ppermute | solution.py:299
  88.1 2.9 %parts.5 = bf16[320,768]{1,0:T(8,128)(2,1)S(1)} custom-call(s32[1]{0:T(128)} %bitcast.4.me_ref, bf16[320,1024]{1,0:T(8,128)(2,1)S(1)} %get-tuple-element.29.rows_ref, bf16[2,12,128,1024]{3,2,1,0:T(8,128)(2,1)} %bitcast.16), custom_call_target="tpu_custom_call" | custom-call | flops 503316480 | bytes 1572864 | tf_op jit(solution)/shard_map/parts/pallas_call | solution.py:164
  91.0 10.1 %collective-permute-done.4 = bf16[320,512]{1,0:T(8,128)(2,1)S(1)} collective-permute-done((bf16[320,512]{1,0:T(8,128)(2,1)S(1)}, bf16[320,512]{1,0:T(8,128)(2,1)S(1)}, u32[]{:S(2)}, u32[]{:S(2)}) %collective-permute-start.4) | collective-permute-done | bytes 327712 | tf_op jit(solution)/shard_map/ppermute | solution.py:299
  101.1 1.3 collective-permute-done.3
  102.4 0.2 convert_add_fusion.1
  102.8 21.2 %all-gather = bf16[1280,384]{1,0:T(8,128)(2,1)S(1)} all-gather(bf16[320,384]{1,0:T(8,128)(2,1)S(1)} %pad_maximum_fusion), channel_id=2, replica_groups=mesh['dp'=8,'ep'=32,'tp'=4] {'tp'}, dimensions={0}, use_global_device_ids=true | all-gather | bytes 1228800 | tf_op jit(solution)/shard_map/all_gather | solution.py:307
  124.1 2.5 %down.1 = bf16[1280,256]{1,0:T(8,128)(2,1)} custom-call(bf16[4,320,384]{2,1,0:T(8,128)(2,1)S(1)} %bitcast.9, bf16[1536,1024]{1,0:T(8,128)(2,1)S(1)} %bitcast.10), custom_call_target="tpu_custom_call" | custom-call | tf_op jit(solution)/shard_map/down/pallas_call | solution.py:196
  126.5 9.4 %all-to-all-start.1 = ((bf16[32,40,256]{2,1,0:T(8,128)(2,1)}), bf16[32,40,256]{2,1,0:T(8,128)(2,1)S(1)}, u32[]{:S(2)}, u32[]{:S(2)}) async-start(bf16[32,40,256]{2,1,0:T(8,128)(2,1)} %bitcast.7), calls=%async_computation.1 | async-start | bytes 1310720 | tf_op jit(solution)/shard_map/all_to_all | solution.py:310
  136.0 0.1 copy.10.ids_ref
  136.1 0.1 copy.11.weight_ref
  136.2 2.9 %mixer.1.mixer_ref = bf16[512,1280]{1,0:T(8,128)(2,1)S(1)} custom-call(s32[128,8]{1,0:T(8,128)S(1)} %copy.10.ids_ref, f32[128,8]{1,0:T(8,128)S(1)} %copy.11.weight_ref, bf16[128,128]{1,0:T(8,128)(2,1)S(1)} %copy-done.4, bf16[32,1280]{1,0:T(8,128)(2,1)S(1)} %copy-done.2, bf16[16,1280]{1,0:T(8,128)(2,1)S(1)} %copy-done.3, bf16[512,16]{1,0:T(8,128)(2,1)S(1)} %copy-done.1), custom_call_target="tpu_custom_call" | custom-call | tf_op jit(solution)/shard_map/mixer/pallas_call | solution.py:230
  139.1 31.1 %all-to-all-done.1 = bf16[32,40,256]{2,1,0:T(8,128)(2,1)S(1)} async-done(((bf16[32,40,256]{2,1,0:T(8,128)(2,1)}), bf16[32,40,256]{2,1,0:T(8,128)(2,1)S(1)}, u32[]{:S(2)}, u32[]{:S(2)}) %all-to-all-start.1) | async-done | bytes 655392 | tf_op jit(solution)/shard_map/all_to_all | solution.py:310
  170.2 1.2 combine.1
  (22 shorter events, 0.4 us)
Async XLA Ops:
  3.1 61.6 %all-to-all-start = ((bf16[32,40,256]{2,1,0:T(8,128)(2,1)}), bf16[32,40,256]{2,1,0:T(8,128)(2,1)S(1)}, u32[]{:S(2)}, u32[]{:S(2)}) async-start(bf16[32,40,256]{2,1,0:T(8,128)(2,1)} %bitcast.17), calls=%async_computation | async-start | bytes 1310720 | tf_op jit(solution)/shard_map/all_to_all | solution.py:285
  66.0 8.8 %collective-permute-start = (bf16[320,256]{1,0:T(8,128)(2,1)S(1)}, bf16[320,256]{1,0:T(8,128)(2,1)S(1)}, u32[]{:S(2)}, u32[]{:S(2)}) collective-permute-start(bf16[320,256]{1,0:T(8,128)(2,1)S(1)} %get-tuple-element.21), channel_id=1, source_target_pairs={{0,1},{1,0},{2,3},{3,2},{4,5},{5,4},{6,7},{7,6},{8,9},{9,8},{10,11... | collective-permute-start | bytes 491528 | tf_op jit(solution)/shard_map/ppermute | solution.py:288
  69.3 16.8 %collective-permute-start.1 = (bf16[320,512]{1,0:T(8,128)(2,1)S(1)}, bf16[320,512]{1,0:T(8,128)(2,1)S(1)}, u32[]{:S(2)}, u32[]{:S(2)}) collective-permute-start(bf16[320,512]{1,0:T(8,128)(2,1)S(1)} %get-tuple-element.24), channel_id=1, source_target_pairs={{0,1},{1,0},{2,3},{3,2},{4,5},{5,4},{6,7},{7,6},{8,9},{9,8},{10,11... | collective-permute-start | bytes 983048 | tf_op jit(solution)/shard_map/ppermute | solution.py:289
  74.8 11.3 %collective-permute-start.2 = (bf16[320,256]{1,0:T(8,128)(2,1)S(1)}, bf16[320,256]{1,0:T(8,128)(2,1)S(1)}, u32[]{:S(2)}, u32[]{:S(2)}) collective-permute-start(bf16[320,256]{1,0:T(8,128)(2,1)S(1)} %add_convert_fusion.1), channel_id=1, source_target_pairs={{0,2},{1,3},{2,0},{3,1},{4,6},{5,7},{6,4},{7,5},{8,10},{9,11},{10,... | collective-permute-start | bytes 491528 | tf_op jit(solution)/shard_map/ppermute | solution.py:293
  82.0 20.4 %collective-permute-start.3 = (bf16[320,768]{1,0:T(8,128)(2,1)S(1)}, bf16[320,768]{1,0:T(8,128)(2,1)S(1)}, u32[]{:S(2)}, u32[]{:S(2)}) collective-permute-start(bf16[320,768]{1,0:T(8,128)(2,1)S(1)} %parts.4), channel_id=1, source_target_pairs={{0,1},{1,0},{2,3},{3,2},{4,5},{5,4},{6,7},{7,6},{8,9},{9,8},{10,11... | collective-permute-start | bytes 1474568 | tf_op jit(solution)/shard_map/ppermute | solution.py:295
  86.2 14.9 %collective-permute-start.4 = (bf16[320,512]{1,0:T(8,128)(2,1)S(1)}, bf16[320,512]{1,0:T(8,128)(2,1)S(1)}, u32[]{:S(2)}, u32[]{:S(2)}) collective-permute-start(bf16[320,512]{1,0:T(8,128)(2,1)S(1)} %add_convert_fusion), channel_id=1, source_target_pairs={{0,2},{1,3},{2,0},{3,1},{4,6},{5,7},{6,4},{7,5},{8,10},{9,11},{10,... | collective-permute-start | bytes 983048 | tf_op jit(solution)/shard_map/ppermute | solution.py:299
  91.0 33.0 %copy-start = (bf16[1,1536,1024]{2,1,0:T(8,128)(2,1)S(1)}, bf16[1,1536,1024]{2,1,0:T(8,128)(2,1)}, u32[]{:S(2)}) copy-start(bf16[1,1536,1024]{2,1,0:T(8,128)(2,1)} %param.13) | copy-start | bytes 9437188
  124.0 12.0 %copy-start.5 = (s32[128,8]{0,1:T(8,128)S(1)}, s32[128,8]{0,1:T(8,128)}, u32[]{:S(2)}) copy-start(s32[128,8]{0,1:T(8,128)} %param.10) | copy-start | bytes 12292
  124.0 12.1 %copy-start.6 = (f32[128,8]{0,1:T(8,128)S(1)}, f32[128,8]{0,1:T(8,128)}, u32[]{:S(2)}) copy-start(f32[128,8]{0,1:T(8,128)} %param.11) | copy-start | bytes 12292
  124.0 12.2 %copy-start.1 = (bf16[512,16]{1,0:T(8,128)(2,1)S(1)}, bf16[512,16]{1,0:T(8,128)(2,1)}, u32[]{:S(2)}) copy-start(bf16[512,16]{1,0:T(8,128)(2,1)} %constant.26.clone.quarter_ref) | copy-start | bytes 49156
  124.0 12.2 %copy-start.2 = (bf16[32,1280]{1,0:T(8,128)(2,1)S(1)}, bf16[32,1280]{1,0:T(8,128)(2,1)}, u32[]{:S(2)}) copy-start(bf16[32,1280]{1,0:T(8,128)(2,1)} %constant.24.clone.expert_ref) | copy-start | bytes 245764
  124.0 12.2 %copy-start.3 = (bf16[16,1280]{1,0:T(8,128)(2,1)S(1)}, bf16[16,1280]{1,0:T(8,128)(2,1)}, u32[]{:S(2)}) copy-start(bf16[16,1280]{1,0:T(8,128)(2,1)} %constant.25.clone.slot_ref) | copy-start | bytes 122884
  124.0 12.2 %copy-start.4 = (bf16[128,128]{1,0:T(8,128)(2,1)S(1)}, bf16[128,128]{1,0:T(8,128)(2,1)}, u32[]{:S(2)}) copy-start(bf16[128,128]{1,0:T(8,128)(2,1)} %constant.23.clone.earlier_ref) | copy-start | bytes 98308
  126.5 43.7 %all-to-all-start.1 = ((bf16[32,40,256]{2,1,0:T(8,128)(2,1)}), bf16[32,40,256]{2,1,0:T(8,128)(2,1)S(1)}, u32[]{:S(2)}, u32[]{:S(2)}) async-start(bf16[32,40,256]{2,1,0:T(8,128)(2,1)} %bitcast.7), calls=%async_computation.1 | async-start | bytes 1310720 | tf_op jit(solution)/shard_map/all_to_all | solution.py:310

commit v7 on v6

--- a/solution.py
+++ b/solution.py
@@ -97,7 +97,7 @@
 def pack(ids_t, tokens, flight):
     rows, features = tokens.shape
     places = flight * BLOCK
-    steps = 2
+    steps = 1
     whole = lambda a: pl.BlockSpec(a.shape, lambda i: (0, 0))
     return pl.pallas_call(
         functools.partial(pack_kernel, flight),
@@ -126,10 +126,6 @@
             rest_ref[:, (piece - 1) * 2 * PIECE : piece * 2 * PIECE] = product
 
 
-def piece_of(weights, quarter, mask, piece):
-    return (quarter ^ mask) * (weights.shape[1] // QUARTERS) + piece
-
-
 def first_part(received, weights):
     places, cols = received.shape
     rows, features = places // QUARTERS, QUARTERS * cols
@@ -147,32 +143,38 @@
     )(received, weights)
 
 
-def parts_kernel(pieces, me_ref, rows_ref, weight_ref, *out_refs):
-    steps = [(out_ref, p) for out_ref, count in zip(out_refs, pieces) for p in range(count)]
-    for i, (out_ref, p) in enumerate(steps):
-        @pl.when(pl.program_id(0) == i)
-        def _():
-            product = mm_t(rows_ref[...], weight_ref[...].reshape(2 * PIECE, -1))
+def parts_kernel(mask, me_ref, rows_ref, weight_ref, *refs):
+    *out_refs, held, arrived = refs
+    pieces = held.shape[1]
+    base = (me_ref[0] ^ mask) * pieces
+    copies = [
+        pltpu.make_async_copy(weight_ref.at[:, pl.ds(base + p, 1)], held.at[:, pl.ds(p, 1)], arrived.at[p])
+        for p in range(pieces)
+    ]
+    for copy in copies:
+        copy.start()
+    piece = 0
+    for out_ref in out_refs:
+        for p in range(out_ref.shape[1] // (2 * PIECE)):
+            copies[piece].wait()
+            product = mm_t(rows_ref[...], held[:, piece].reshape(2 * PIECE, -1))
             out_ref[:, p * 2 * PIECE : (p + 1) * 2 * PIECE] = product.astype(BF16)
-
-
-def parts(me, mask, rows_in, weights, *pieces, start=0):
+            piece += 1
+
+
+def parts(me, mask, rows_in, weights, *pieces):
     rows, features = rows_in.shape
-    steps = sum(pieces)
-    whole = lambda shape: pl.BlockSpec(shape, lambda i, me: (0, 0))
-    shapes = [(rows, 2 * PIECE * count) for count in pieces]
-    return pl.pallas_call(
-        functools.partial(parts_kernel, pieces),
+    count = sum(pieces)
+    shapes = [(rows, 2 * PIECE * number) for number in pieces]
+    vmem = pl.BlockSpec(memory_space=pltpu.VMEM)
+    return pl.pallas_call(
+        functools.partial(parts_kernel, mask),
         out_shape=tuple(jax.ShapeDtypeStruct(shape, BF16) for shape in shapes),
-        grid_spec=pltpu.PrefetchScalarGridSpec(
-            num_scalar_prefetch=1,
-            grid=(steps,),
-            in_specs=[whole((rows, features)),
-                      pl.BlockSpec((2, 1, PIECE, features), lambda i, me: (0, piece_of(weights, me[0], mask, start + i), 0, 0))],
-            out_specs=tuple(whole(shape) for shape in shapes),
-        ),
+        in_specs=[pl.BlockSpec(memory_space=pltpu.SMEM), vmem, pl.BlockSpec(memory_space=pl.ANY)],
+        out_specs=(vmem,) * len(shapes),
+        scratch_shapes=[pltpu.VMEM((2, count, PIECE, features), BF16), pltpu.SemaphoreType.DMA((count,))],
         compiler_params=PARAMS,
-        cost_estimate=pl.CostEstimate(flops=4 * steps * rows * PIECE * features, bytes_accessed=4 * steps * PIECE * features, transcendentals=0),
+        cost_estimate=pl.CostEstimate(flops=4 * count * rows * PIECE * features, bytes_accessed=4 * count * PIECE * features, transcendentals=0),
         name="parts",
     )(me, rows_in, weights)
 

time: 172 us -> 170 us (0.988)
  transfers between devices with their start and end apart: 7 -> 7, of which waited for: 4 -> 5; matrix products, arithmetic and copies ran while one was open for 1% -> 1% of each run, Pallas kernels for 7% -> 6%
where the time goes in v7:
time: 170 us; the launch traced here: 169 us
  waiting for transfers between devices  77.3 us (45%)
  starting transfers between devices  50.3 us (30%)
  blocking collectives  20.5 us (12%)
  Pallas kernels  18.4 us (11%)
  local copies, waits for them, and re-layouts  1.77 us (1%)
    all_to_all x1, waiting for transfers between devices, local(): lax.all_to_all(sent.reshape(flight, BLOCK, cols), 'ep', 0, 0, tiled=True)  35.8 us
    all_to_all x1, waiting for transfers between devices, local(): lax.all_to_all(result.reshape(flight, BLOCK, cols), 'ep', 0, 0, tiled=True)  29.7 us
    all_to_all x1, starting transfers between devices, local(): lax.all_to_all(sent.reshape(flight, BLOCK, cols), 'ep', 0, 0, tiled=True)  24.3 us
    all_gather x1, blocking collectives, local(): lax.all_gather(jnp.concatenate(hidden, axis=1), 'tp', axis=0, tiled=False)  20.5 us
    ppermute x1, waiting for transfers between devices, local(): got_2 = lax.ppermute(pair_2, 'tp', far)  9.79 us
    all_to_all x1, starting transfers between devices, local(): lax.all_to_all(result.reshape(flight, BLOCK, cols), 'ep', 0, 0, tiled=True)  9.78 us
    pallas_call x3, Pallas kernels, parts(): pl.pallas_call(functools.partial(parts_kernel, mask), out_shape=tuple((ja...  7.46 us
    ppermute x1, starting transfers between devices, local(): got_1 = lax.ppermute(pair_1, 'tp', far)  4.05 us
  transfers between devices with their start and end apart: 7, of which 5 were waited for; matrix products, arithmetic and copies ran while one was open for 1% of the time, Pallas kernels for 6%

profile of v7, /device:TPU:56, one launch (start us, length us, event | category | flops | bytes accessed | tf_op | source)
XLA Modules:
  0.0 169.0 jit_solution(16562472024868156203)
XLA Ops:
  0.0 3.0 %pack.1 = bf16[1280,256]{1,0:T(8,128)(2,1)} custom-call(s32[8,128]{1,0:T(8,128)} %bitcast.18, bf16[128,1024]{1,0:T(8,128)(2,1)} %token_ref.1), custom_call_target="tpu_custom_call" | custom-call | tf_op jit(solution)/shard_map/pack/pallas_call | solution.py:102
  3.0 24.3 %all-to-all-start = ((bf16[32,40,256]{2,1,0:T(8,128)(2,1)}), bf16[32,40,256]{2,1,0:T(8,128)(2,1)S(1)}, u32[]{:S(2)}, u32[]{:S(2)}) async-start(bf16[32,40,256]{2,1,0:T(8,128)(2,1)} %bitcast.17), calls=%async_computation | async-start | bytes 1310720 | tf_op jit(solution)/shard_map/all_to_all | solution.py:287
  27.3 1.5 constant_dynamic-slice_fusion.weight_ref
  28.8 35.8 %all-to-all-done = bf16[32,40,256]{2,1,0:T(8,128)(2,1)S(1)} async-done(((bf16[32,40,256]{2,1,0:T(8,128)(2,1)}), bf16[32,40,256]{2,1,0:T(8,128)(2,1)S(1)}, u32[]{:S(2)}, u32[]{:S(2)}) %all-to-all-start) | async-done | bytes 655392 | tf_op jit(solution)/shard_map/all_to_all | solution.py:287
  64.6 1.3 first.1
  66.0 3.3 %collective-permute-start = (bf16[320,256]{1,0:T(8,128)(2,1)S(1)}, bf16[320,256]{1,0:T(8,128)(2,1)S(1)}, u32[]{:S(2)}, u32[]{:S(2)}) collective-permute-start(bf16[320,256]{1,0:T(8,128)(2,1)S(1)} %get-tuple-element.21), channel_id=1, source_target_pairs={{0,1},{1,0},{2,3},{3,2},{4,5},{5,4},{6,7},{7,6},{8,9},{9,8},{10,11... | collective-permute-start | bytes 491528 | tf_op jit(solution)/shard_map/ppermute | solution.py:290
  69.2 2.6 %collective-permute-start.1 = (bf16[320,512]{1,0:T(8,128)(2,1)S(1)}, bf16[320,512]{1,0:T(8,128)(2,1)S(1)}, u32[]{:S(2)}, u32[]{:S(2)}) collective-permute-start(bf16[320,512]{1,0:T(8,128)(2,1)S(1)} %get-tuple-element.24), channel_id=1, source_target_pairs={{0,1},{1,0},{2,3},{3,2},{4,5},{5,4},{6,7},{7,6},{8,9},{9,8},{10,11... | collective-permute-start | bytes 983048 | tf_op jit(solution)/shard_map/ppermute | solution.py:291
  71.8 2.5 %parts.3 = (bf16[320,256]{1,0:T(8,128)(2,1)S(1)}, bf16[320,512]{1,0:T(8,128)(2,1)S(1)}) custom-call(s32[1]{0:T(128)} %bitcast.4.me_ref, bf16[320,1024]{1,0:T(8,128)(2,1)S(1)} %get-tuple-element.29.rows_ref, bf16[2,12,128,1024]{3,2,1,0:T(8,128)(2,1)} %bitcast.14), custom_call_target="tpu_custom_call" | custom-call | flops 503316480 | bytes 1572864 | tf_op jit(solution)/shard_map/parts/pallas_call | solution.py:170
  74.4 4.0 %collective-permute-start.2 = (bf16[320,256]{1,0:T(8,128)(2,1)S(1)}, bf16[320,256]{1,0:T(8,128)(2,1)S(1)}, u32[]{:S(2)}, u32[]{:S(2)}) collective-permute-start(bf16[320,256]{1,0:T(8,128)(2,1)S(1)} %add_convert_fusion.1), channel_id=1, source_target_pairs={{0,2},{1,3},{2,0},{3,1},{4,6},{5,7},{6,4},{7,5},{8,10},{9,11},{10,... | collective-permute-start | bytes 491528 | tf_op jit(solution)/shard_map/ppermute | solution.py:295
  78.4 2.5 %parts.4 = bf16[320,768]{1,0:T(8,128)(2,1)S(1)} custom-call(s32[1]{0:T(128)} %bitcast.4.me_ref, bf16[320,1024]{1,0:T(8,128)(2,1)S(1)} %get-tuple-element.29.rows_ref, bf16[2,12,128,1024]{3,2,1,0:T(8,128)(2,1)} %bitcast.15), custom_call_target="tpu_custom_call" | custom-call | flops 503316480 | bytes 1572864 | tf_op jit(solution)/shard_map/parts/pallas_call | solution.py:170
  80.9 3.4 %collective-permute-start.3 = (bf16[320,768]{1,0:T(8,128)(2,1)S(1)}, bf16[320,768]{1,0:T(8,128)(2,1)S(1)}, u32[]{:S(2)}, u32[]{:S(2)}) collective-permute-start(bf16[320,768]{1,0:T(8,128)(2,1)S(1)} %parts.4), channel_id=1, source_target_pairs={{0,1},{1,0},{2,3},{3,2},{4,5},{5,4},{6,7},{7,6},{8,9},{9,8},{10,11... | collective-permute-start | bytes 1474568 | tf_op jit(solution)/shard_map/ppermute | solution.py:297
  84.4 0.5 collective-permute-done.2
  84.9 3.0 %collective-permute-start.4 = (bf16[320,512]{1,0:T(8,128)(2,1)S(1)}, bf16[320,512]{1,0:T(8,128)(2,1)S(1)}, u32[]{:S(2)}, u32[]{:S(2)}) collective-permute-start(bf16[320,512]{1,0:T(8,128)(2,1)S(1)} %add_convert_fusion), channel_id=1, source_target_pairs={{0,2},{1,3},{2,0},{3,1},{4,6},{5,7},{6,4},{7,5},{8,10},{9,11},{10,... | collective-permute-start | bytes 983048 | tf_op jit(solution)/shard_map/ppermute | solution.py:301
  88.0 2.5 %parts.5 = bf16[320,768]{1,0:T(8,128)(2,1)S(1)} custom-call(s32[1]{0:T(128)} %bitcast.4.me_ref, bf16[320,1024]{1,0:T(8,128)(2,1)S(1)} %get-tuple-element.29.rows_ref, bf16[2,12,128,1024]{3,2,1,0:T(8,128)(2,1)} %bitcast.16), custom_call_target="tpu_custom_call" | custom-call | flops 503316480 | bytes 1572864 | tf_op jit(solution)/shard_map/parts/pallas_call | solution.py:170
  90.5 9.8 %collective-permute-done.4 = bf16[320,512]{1,0:T(8,128)(2,1)S(1)} collective-permute-done((bf16[320,512]{1,0:T(8,128)(2,1)S(1)}, bf16[320,512]{1,0:T(8,128)(2,1)S(1)}, u32[]{:S(2)}, u32[]{:S(2)}) %collective-permute-start.4) | collective-permute-done | bytes 327712 | tf_op jit(solution)/shard_map/ppermute | solution.py:301
  100.3 1.4 collective-permute-done.3
  101.7 0.2 convert_add_fusion.1
  102.1 20.5 %all-gather = bf16[1280,384]{1,0:T(8,128)(2,1)S(1)} all-gather(bf16[320,384]{1,0:T(8,128)(2,1)S(1)} %pad_maximum_fusion), channel_id=2, replica_groups=mesh['dp'=8,'ep'=32,'tp'=4] {'tp'}, dimensions={0}, use_global_device_ids=true | all-gather | bytes 1228800 | tf_op jit(solution)/shard_map/all_gather | solution.py:309
  122.6 2.5 %down.1 = bf16[1280,256]{1,0:T(8,128)(2,1)} custom-call(bf16[4,320,384]{2,1,0:T(8,128)(2,1)S(1)} %bitcast.9, bf16[1536,1024]{1,0:T(8,128)(2,1)S(1)} %bitcast.10), custom_call_target="tpu_custom_call" | custom-call | tf_op jit(solution)/shard_map/down/pallas_call | solution.py:198
  125.1 9.8 %all-to-all-start.1 = ((bf16[32,40,256]{2,1,0:T(8,128)(2,1)}), bf16[32,40,256]{2,1,0:T(8,128)(2,1)S(1)}, u32[]{:S(2)}, u32[]{:S(2)}) async-start(bf16[32,40,256]{2,1,0:T(8,128)(2,1)} %bitcast.7), calls=%async_computation.1 | async-start | bytes 1310720 | tf_op jit(solution)/shard_map/all_to_all | solution.py:312
  134.9 0.1 copy.10.ids_ref
  135.1 2.9 %mixer.1.mixer_ref = bf16[512,1280]{1,0:T(8,128)(2,1)S(1)} custom-call(s32[128,8]{1,0:T(8,128)S(1)} %copy.10.ids_ref, f32[128,8]{1,0:T(8,128)S(1)} %copy.11.weight_ref, bf16[128,128]{1,0:T(8,128)(2,1)S(1)} %copy-done.4, bf16[32,1280]{1,0:T(8,128)(2,1)S(1)} %copy-done.2, bf16[16,1280]{1,0:T(8,128)(2,1)S(1)} %copy-done.3, bf16[512,16]{1,0:T(8,128)(2,1)S(1)} %copy-done.1), custom_call_target="tpu_custom_call" | custom-call | tf_op jit(solution)/shard_map/mixer/pallas_call | solution.py:232
  138.0 29.7 %all-to-all-done.1 = bf16[32,40,256]{2,1,0:T(8,128)(2,1)S(1)} async-done(((bf16[32,40,256]{2,1,0:T(8,128)(2,1)}), bf16[32,40,256]{2,1,0:T(8,128)(2,1)S(1)}, u32[]{:S(2)}, u32[]{:S(2)}) %all-to-all-start.1) | async-done | bytes 655392 | tf_op jit(solution)/shard_map/all_to_all | solution.py:312
  167.8 1.2 combine.1
  (22 shorter events, 0.5 us)
Async XLA Ops:
  3.0 61.6 %all-to-all-start = ((bf16[32,40,256]{2,1,0:T(8,128)(2,1)}), bf16[32,40,256]{2,1,0:T(8,128)(2,1)S(1)}, u32[]{:S(2)}, u32[]{:S(2)}) async-start(bf16[32,40,256]{2,1,0:T(8,128)(2,1)} %bitcast.17), calls=%async_computation | async-start | bytes 1310720 | tf_op jit(solution)/shard_map/all_to_all | solution.py:287
  66.0 8.4 %collective-permute-start = (bf16[320,256]{1,0:T(8,128)(2,1)S(1)}, bf16[320,256]{1,0:T(8,128)(2,1)S(1)}, u32[]{:S(2)}, u32[]{:S(2)}) collective-permute-start(bf16[320,256]{1,0:T(8,128)(2,1)S(1)} %get-tuple-element.21), channel_id=1, source_target_pairs={{0,1},{1,0},{2,3},{3,2},{4,5},{5,4},{6,7},{7,6},{8,9},{9,8},{10,11... | collective-permute-start | bytes 491528 | tf_op jit(solution)/shard_map/ppermute | solution.py:290
  69.2 15.1 %collective-permute-start.1 = (bf16[320,512]{1,0:T(8,128)(2,1)S(1)}, bf16[320,512]{1,0:T(8,128)(2,1)S(1)}, u32[]{:S(2)}, u32[]{:S(2)}) collective-permute-start(bf16[320,512]{1,0:T(8,128)(2,1)S(1)} %get-tuple-element.24), channel_id=1, source_target_pairs={{0,1},{1,0},{2,3},{3,2},{4,5},{5,4},{6,7},{7,6},{8,9},{9,8},{10,11... | collective-permute-start | bytes 983048 | tf_op jit(solution)/shard_map/ppermute | solution.py:291
  74.4 10.6 %collective-permute-start.2 = (bf16[320,256]{1,0:T(8,128)(2,1)S(1)}, bf16[320,256]{1,0:T(8,128)(2,1)S(1)}, u32[]{:S(2)}, u32[]{:S(2)}) collective-permute-start(bf16[320,256]{1,0:T(8,128)(2,1)S(1)} %add_convert_fusion.1), channel_id=1, source_target_pairs={{0,2},{1,3},{2,0},{3,1},{4,6},{5,7},{6,4},{7,5},{8,10},{9,11},{10,... | collective-permute-start | bytes 491528 | tf_op jit(solution)/shard_map/ppermute | solution.py:295
  80.9 20.8 %collective-permute-start.3 = (bf16[320,768]{1,0:T(8,128)(2,1)S(1)}, bf16[320,768]{1,0:T(8,128)(2,1)S(1)}, u32[]{:S(2)}, u32[]{:S(2)}) collective-permute-start(bf16[320,768]{1,0:T(8,128)(2,1)S(1)} %parts.4), channel_id=1, source_target_pairs={{0,1},{1,0},{2,3},{3,2},{4,5},{5,4},{6,7},{7,6},{8,9},{9,8},{10,11... | collective-permute-start | bytes 1474568 | tf_op jit(solution)/shard_map/ppermute | solution.py:297
  84.9 15.3 %collective-permute-start.4 = (bf16[320,512]{1,0:T(8,128)(2,1)S(1)}, bf16[320,512]{1,0:T(8,128)(2,1)S(1)}, u32[]{:S(2)}, u32[]{:S(2)}) collective-permute-start(bf16[320,512]{1,0:T(8,128)(2,1)S(1)} %add_convert_fusion), channel_id=1, source_target_pairs={{0,2},{1,3},{2,0},{3,1},{4,6},{5,7},{6,4},{7,5},{8,10},{9,11},{10,... | collective-permute-start | bytes 983048 | tf_op jit(solution)/shard_map/ppermute | solution.py:301
  90.5 32.2 %copy-start = (bf16[1,1536,1024]{2,1,0:T(8,128)(2,1)S(1)}, bf16[1,1536,1024]{2,1,0:T(8,128)(2,1)}, u32[]{:S(2)}) copy-start(bf16[1,1536,1024]{2,1,0:T(8,128)(2,1)} %param.13) | copy-start | bytes 9437188
  122.6 12.3 %copy-start.5 = (s32[128,8]{0,1:T(8,128)S(1)}, s32[128,8]{0,1:T(8,128)}, u32[]{:S(2)}) copy-start(s32[128,8]{0,1:T(8,128)} %param.10) | copy-start | bytes 12292
  122.6 12.4 %copy-start.6 = (f32[128,8]{0,1:T(8,128)S(1)}, f32[128,8]{0,1:T(8,128)}, u32[]{:S(2)}) copy-start(f32[128,8]{0,1:T(8,128)} %param.11) | copy-start | bytes 12292
  122.6 12.5 %copy-start.1 = (bf16[512,16]{1,0:T(8,128)(2,1)S(1)}, bf16[512,16]{1,0:T(8,128)(2,1)}, u32[]{:S(2)}) copy-start(bf16[512,16]{1,0:T(8,128)(2,1)} %constant.26.clone.quarter_ref) | copy-start | bytes 49156
  122.6 12.5 %copy-start.2 = (bf16[32,1280]{1,0:T(8,128)(2,1)S(1)}, bf16[32,1280]{1,0:T(8,128)(2,1)}, u32[]{:S(2)}) copy-start(bf16[32,1280]{1,0:T(8,128)(2,1)} %constant.24.clone.expert_ref) | copy-start | bytes 245764
  122.6 12.5 %copy-start.3 = (bf16[16,1280]{1,0:T(8,128)(2,1)S(1)}, bf16[16,1280]{1,0:T(8,128)(2,1)}, u32[]{:S(2)}) copy-start(bf16[16,1280]{1,0:T(8,128)(2,1)} %constant.25.clone.slot_ref) | copy-start | bytes 122884
  122.6 12.5 %copy-start.4 = (bf16[128,128]{1,0:T(8,128)(2,1)S(1)}, bf16[128,128]{1,0:T(8,128)(2,1)}, u32[]{:S(2)}) copy-start(bf16[128,128]{1,0:T(8,128)(2,1)} %constant.23.clone.earlier_ref) | copy-start | bytes 98308
  125.1 42.7 %all-to-all-start.1 = ((bf16[32,40,256]{2,1,0:T(8,128)(2,1)}), bf16[32,40,256]{2,1,0:T(8,128)(2,1)S(1)}, u32[]{:S(2)}, u32[]{:S(2)}) async-start(bf16[32,40,256]{2,1,0:T(8,128)(2,1)} %bitcast.7), calls=%async_computation.1 | async-start | bytes 1310720 | tf_op jit(solution)/shard_map/all_to_all | solution.py:312

commit v8 on v7

--- a/solution.py
+++ b/solution.py
@@ -69,9 +69,18 @@
     return jnp.where(counter((span, span), 1) == column, 1.0, 0.0).astype(BF16)
 
 
+def spread(rows, out_ref):
+    cols = out_ref.shape[1]
+    span, slab = GROUP * BLOCK, GROUP * CAP
+    matrix = regroup_matrix(True)
+    for g in range(out_ref.shape[0] // span):
+        block = rows[g * slab : (g + 1) * slab, :]
+        stacked = jnp.concatenate([block[:, q * cols : (q + 1) * cols] for q in range(QUARTERS)], axis=0)
+        out_ref[g * span : (g + 1) * span, :] = mm(matrix, stacked).astype(BF16)
+
+
 def pack_kernel(flight, ids_ref, token_ref, out_ref):
     top, rows = ids_ref.shape
-    places, cols = out_ref.shape
     expert = lax.broadcasted_iota(jnp.int32, (flight, rows), 0)
     named = jnp.zeros((flight, rows), F32)
     for k in range(top):
@@ -79,32 +88,27 @@
     earlier = jnp.where(counter((rows, rows), 0) < counter((rows, rows), 1), 1.0, 0.0).astype(BF16)
     slot = jnp.where(named > 0, mm(named.astype(BF16), earlier), FAR)
 
-    line = counter((16, rows), 0)
-    other = [jnp.where((line <= QUARTERS) & (line != q + 1), 1.0, 0.0) for q in range(QUARTERS)]
-    code = jnp.concatenate([jnp.concatenate([slot, o], axis=0) for o in other], axis=1).astype(BF16)
-    place = counter((places, 1), 0) + (pl.program_id(0) * places).astype(F32)
-    owner, rest = split(place, BLOCK)
-    quarter, place_slot = split(rest, CAP)
+    ones = jnp.where(counter((16, rows), 0) == 0, 1.0, 0.0)
+    code = jnp.concatenate([slot, ones], axis=0).astype(BF16)
+    places = flight * CAP
+    owner, place_slot = split(counter((places, 1), 0), CAP)
     column = counter((places, flight + 16), 1)
     place_code = jnp.where(column == owner, 1.0, 0.0) + jnp.where(column == flight, -place_slot, 0.0)
-    place_code += jnp.where(column == flight + 1 + quarter, APART, 0.0)
     gap = mm(place_code.astype(BF16), code)
     selector = jnp.where(gap == 0, 1.0, 0.0).astype(BF16)
-    stacked = jnp.concatenate([token_ref[:, q * cols : (q + 1) * cols] for q in range(QUARTERS)], axis=0)
-    out_ref[...] = mm(selector, stacked).astype(BF16)
+    spread(mm(selector, token_ref[...]).astype(BF16), out_ref)
 
 
 def pack(ids_t, tokens, flight):
-    rows, features = tokens.shape
-    places = flight * BLOCK
-    steps = 1
-    whole = lambda a: pl.BlockSpec(a.shape, lambda i: (0, 0))
+    features = tokens.shape[1]
+    whole = lambda shape: pl.BlockSpec(shape, lambda i: (0, 0))
+    shape = (flight * BLOCK, features // QUARTERS)
     return pl.pallas_call(
         functools.partial(pack_kernel, flight),
-        out_shape=jax.ShapeDtypeStruct((places, features // QUARTERS), BF16),
-        grid=(steps,),
-        in_specs=[whole(ids_t), whole(tokens)],
-        out_specs=pl.BlockSpec((places // steps, features // QUARTERS), lambda i: (i, 0)),
+        out_shape=jax.ShapeDtypeStruct(shape, BF16),
+        grid=(1,),
+        in_specs=[whole(ids_t.shape), whole(tokens.shape)],
+        out_specs=whole(shape),
         compiler_params=pltpu.CompilerParams(vmem_limit_bytes=60 * 1024 * 1024),
         name="pack",
     )(ids_t, tokens)
@@ -180,15 +184,8 @@
 
 
 def down_kernel(hidden_ref, weight_ref, out_ref):
-    cols = out_ref.shape[1]
-    span, slab = GROUP * BLOCK, GROUP * CAP
     hidden = jnp.concatenate([hidden_ref[k] for k in range(hidden_ref.shape[0])], axis=1)
-    total = mm(hidden, weight_ref[...]).astype(BF16)
-    spread = regroup_matrix(True)
-    for g in range(out_ref.shape[0] // span):
-        block = total[g * slab : (g + 1) * slab, :]
-        stacked = jnp.concatenate([block[:, q * cols : (q + 1) * cols] for q in range(QUARTERS)], axis=0)
-        out_ref[g * span : (g + 1) * span, :] = mm(spread, stacked).astype(BF16)
+    spread(mm(hidden, weight_ref[...]).astype(BF16), out_ref)
 
 
 def down(hidden, weights):

time: 170 us -> 169 us (level)
  no operation moved by 1% of the time
where the time goes in v8:
time: 169 us
  waiting for transfers between devices  77.4 us (46%)
  starting transfers between devices  50.1 us (30%)
  blocking collectives  20.6 us (12%)
  Pallas kernels  18.2 us (11%)
  local copies, waits for them, and re-layouts  1.77 us (1%)
    all_to_all x1, waiting for transfers between devices, local(): lax.all_to_all(sent.reshape(flight, BLOCK, cols), 'ep', 0, 0, tiled=True)  35.8 us
    all_to_all x1, waiting for transfers between devices, local(): lax.all_to_all(result.reshape(flight, BLOCK, cols), 'ep', 0, 0, tiled=True)  29.7 us
    all_to_all x1, starting transfers between devices, local(): lax.all_to_all(sent.reshape(flight, BLOCK, cols), 'ep', 0, 0, tiled=True)  24.3 us
    all_gather x1, blocking collectives, local(): lax.all_gather(jnp.concatenate(hidden, axis=1), 'tp', axis=0, tiled=False)  20.6 us
    ppermute x1, waiting for transfers between devices, local(): got_2 = lax.ppermute(pair_2, 'tp', far)  9.77 us
    all_to_all x1, starting transfers between devices, local(): lax.all_to_all(result.reshape(flight, BLOCK, cols), 'ep', 0, 0, tiled=True)  9.66 us
    pallas_call x3, Pallas kernels, parts(): pl.pallas_call(functools.partial(parts_kernel, mask), out_shape=tuple((ja...  7.49 us
    ppermute x1, starting transfers between devices, local(): got_1 = lax.ppermute(pair_1, 'tp', far)  4.04 us
  transfers between devices with their start and end apart: 7, of which 5 were waited for; matrix products, arithmetic and copies ran while one was open for 1% of the time, Pallas kernels for 6%

profile of v8, /device:TPU:56, one launch (start us, length us, event | category | flops | bytes accessed | tf_op | source)
XLA Modules:
  0.0 168.8 jit_solution(12711754531462815604)
XLA Ops:
  0.0 2.8 %pack.1 = bf16[1280,256]{1,0:T(8,128)(2,1)} custom-call(s32[8,128]{1,0:T(8,128)} %bitcast.18, bf16[128,1024]{1,0:T(8,128)(2,1)} %token_ref.1), custom_call_target="tpu_custom_call" | custom-call | tf_op jit(solution)/shard_map/pack/pallas_call | solution.py:106
  2.8 24.3 %all-to-all-start = ((bf16[32,40,256]{2,1,0:T(8,128)(2,1)}), bf16[32,40,256]{2,1,0:T(8,128)(2,1)S(1)}, u32[]{:S(2)}, u32[]{:S(2)}) async-start(bf16[32,40,256]{2,1,0:T(8,128)(2,1)} %bitcast.17), calls=%async_computation | async-start | bytes 1310720 | tf_op jit(solution)/shard_map/all_to_all | solution.py:284
  27.1 1.5 constant_dynamic-slice_fusion.weight_ref
  28.6 35.8 %all-to-all-done = bf16[32,40,256]{2,1,0:T(8,128)(2,1)S(1)} async-done(((bf16[32,40,256]{2,1,0:T(8,128)(2,1)}), bf16[32,40,256]{2,1,0:T(8,128)(2,1)S(1)}, u32[]{:S(2)}, u32[]{:S(2)}) %all-to-all-start) | async-done | bytes 655392 | tf_op jit(solution)/shard_map/all_to_all | solution.py:284
  64.5 1.3 first.1
  65.8 3.3 %collective-permute-start = (bf16[320,256]{1,0:T(8,128)(2,1)S(1)}, bf16[320,256]{1,0:T(8,128)(2,1)S(1)}, u32[]{:S(2)}, u32[]{:S(2)}) collective-permute-start(bf16[320,256]{1,0:T(8,128)(2,1)S(1)} %get-tuple-element.21), channel_id=1, source_target_pairs={{0,1},{1,0},{2,3},{3,2},{4,5},{5,4},{6,7},{7,6},{8,9},{9,8},{10,11... | collective-permute-start | bytes 491528 | tf_op jit(solution)/shard_map/ppermute | solution.py:287
  69.0 2.6 %collective-permute-start.1 = (bf16[320,512]{1,0:T(8,128)(2,1)S(1)}, bf16[320,512]{1,0:T(8,128)(2,1)S(1)}, u32[]{:S(2)}, u32[]{:S(2)}) collective-permute-start(bf16[320,512]{1,0:T(8,128)(2,1)S(1)} %get-tuple-element.24), channel_id=1, source_target_pairs={{0,1},{1,0},{2,3},{3,2},{4,5},{5,4},{6,7},{7,6},{8,9},{9,8},{10,11... | collective-permute-start | bytes 983048 | tf_op jit(solution)/shard_map/ppermute | solution.py:288
  71.6 2.5 %parts.3 = (bf16[320,256]{1,0:T(8,128)(2,1)S(1)}, bf16[320,512]{1,0:T(8,128)(2,1)S(1)}) custom-call(s32[1]{0:T(128)} %bitcast.4.me_ref, bf16[320,1024]{1,0:T(8,128)(2,1)S(1)} %get-tuple-element.29.rows_ref, bf16[2,12,128,1024]{3,2,1,0:T(8,128)(2,1)} %bitcast.14), custom_call_target="tpu_custom_call" | custom-call | flops 503316480 | bytes 1572864 | tf_op jit(solution)/shard_map/parts/pallas_call | solution.py:174
  74.2 4.0 %collective-permute-start.2 = (bf16[320,256]{1,0:T(8,128)(2,1)S(1)}, bf16[320,256]{1,0:T(8,128)(2,1)S(1)}, u32[]{:S(2)}, u32[]{:S(2)}) collective-permute-start(bf16[320,256]{1,0:T(8,128)(2,1)S(1)} %add_convert_fusion.1), channel_id=1, source_target_pairs={{0,2},{1,3},{2,0},{3,1},{4,6},{5,7},{6,4},{7,5},{8,10},{9,11},{10,... | collective-permute-start | bytes 491528 | tf_op jit(solution)/shard_map/ppermute | solution.py:292
  78.2 2.5 %parts.4 = bf16[320,768]{1,0:T(8,128)(2,1)S(1)} custom-call(s32[1]{0:T(128)} %bitcast.4.me_ref, bf16[320,1024]{1,0:T(8,128)(2,1)S(1)} %get-tuple-element.29.rows_ref, bf16[2,12,128,1024]{3,2,1,0:T(8,128)(2,1)} %bitcast.15), custom_call_target="tpu_custom_call" | custom-call | flops 503316480 | bytes 1572864 | tf_op jit(solution)/shard_map/parts/pallas_call | solution.py:174
  80.7 3.4 %collective-permute-start.3 = (bf16[320,768]{1,0:T(8,128)(2,1)S(1)}, bf16[320,768]{1,0:T(8,128)(2,1)S(1)}, u32[]{:S(2)}, u32[]{:S(2)}) collective-permute-start(bf16[320,768]{1,0:T(8,128)(2,1)S(1)} %parts.4), channel_id=1, source_target_pairs={{0,1},{1,0},{2,3},{3,2},{4,5},{5,4},{6,7},{7,6},{8,9},{9,8},{10,11... | collective-permute-start | bytes 1474568 | tf_op jit(solution)/shard_map/ppermute | solution.py:294
  84.2 0.6 collective-permute-done.2
  84.8 3.0 %collective-permute-start.4 = (bf16[320,512]{1,0:T(8,128)(2,1)S(1)}, bf16[320,512]{1,0:T(8,128)(2,1)S(1)}, u32[]{:S(2)}, u32[]{:S(2)}) collective-permute-start(bf16[320,512]{1,0:T(8,128)(2,1)S(1)} %add_convert_fusion), channel_id=1, source_target_pairs={{0,2},{1,3},{2,0},{3,1},{4,6},{5,7},{6,4},{7,5},{8,10},{9,11},{10,... | collective-permute-start | bytes 983048 | tf_op jit(solution)/shard_map/ppermute | solution.py:298
  87.8 2.5 %parts.5 = bf16[320,768]{1,0:T(8,128)(2,1)S(1)} custom-call(s32[1]{0:T(128)} %bitcast.4.me_ref, bf16[320,1024]{1,0:T(8,128)(2,1)S(1)} %get-tuple-element.29.rows_ref, bf16[2,12,128,1024]{3,2,1,0:T(8,128)(2,1)} %bitcast.16), custom_call_target="tpu_custom_call" | custom-call | flops 503316480 | bytes 1572864 | tf_op jit(solution)/shard_map/parts/pallas_call | solution.py:174
  90.3 9.8 %collective-permute-done.4 = bf16[320,512]{1,0:T(8,128)(2,1)S(1)} collective-permute-done((bf16[320,512]{1,0:T(8,128)(2,1)S(1)}, bf16[320,512]{1,0:T(8,128)(2,1)S(1)}, u32[]{:S(2)}, u32[]{:S(2)}) %collective-permute-start.4) | collective-permute-done | bytes 327712 | tf_op jit(solution)/shard_map/ppermute | solution.py:298
  100.1 1.4 collective-permute-done.3
  101.5 0.2 convert_add_fusion.1
  101.9 20.6 %all-gather = bf16[1280,384]{1,0:T(8,128)(2,1)S(1)} all-gather(bf16[320,384]{1,0:T(8,128)(2,1)S(1)} %pad_maximum_fusion), channel_id=2, replica_groups=mesh['dp'=8,'ep'=32,'tp'=4] {'tp'}, dimensions={0}, use_global_device_ids=true | all-gather | bytes 1228800 | tf_op jit(solution)/shard_map/all_gather | solution.py:306
  122.5 2.5 %down.1 = bf16[1280,256]{1,0:T(8,128)(2,1)} custom-call(bf16[4,320,384]{2,1,0:T(8,128)(2,1)S(1)} %bitcast.9, bf16[1536,1024]{1,0:T(8,128)(2,1)S(1)} %bitcast.10), custom_call_target="tpu_custom_call" | custom-call | tf_op jit(solution)/shard_map/down/pallas_call | solution.py:195
  125.0 9.7 %all-to-all-start.1 = ((bf16[32,40,256]{2,1,0:T(8,128)(2,1)}), bf16[32,40,256]{2,1,0:T(8,128)(2,1)S(1)}, u32[]{:S(2)}, u32[]{:S(2)}) async-start(bf16[32,40,256]{2,1,0:T(8,128)(2,1)} %bitcast.7), calls=%async_computation.1 | async-start | bytes 1310720 | tf_op jit(solution)/shard_map/all_to_all | solution.py:309
  134.7 0.1 copy.10.ids_ref
  134.9 2.9 %mixer.1.mixer_ref = bf16[512,1280]{1,0:T(8,128)(2,1)S(1)} custom-call(s32[128,8]{1,0:T(8,128)S(1)} %copy.10.ids_ref, f32[128,8]{1,0:T(8,128)S(1)} %copy.11.weight_ref, bf16[128,128]{1,0:T(8,128)(2,1)S(1)} %copy-done.4, bf16[32,1280]{1,0:T(8,128)(2,1)S(1)} %copy-done.2, bf16[16,1280]{1,0:T(8,128)(2,1)S(1)} %copy-done.3, bf16[512,16]{1,0:T(8,128)(2,1)S(1)} %copy-done.1), custom_call_target="tpu_custom_call" | custom-call | tf_op jit(solution)/shard_map/mixer/pallas_call | solution.py:229
  137.8 29.7 %all-to-all-done.1 = bf16[32,40,256]{2,1,0:T(8,128)(2,1)S(1)} async-done(((bf16[32,40,256]{2,1,0:T(8,128)(2,1)}), bf16[32,40,256]{2,1,0:T(8,128)(2,1)S(1)}, u32[]{:S(2)}, u32[]{:S(2)}) %all-to-all-start.1) | async-done | bytes 655392 | tf_op jit(solution)/shard_map/all_to_all | solution.py:309
  167.5 1.2 combine.1
  (22 shorter events, 0.5 us)
Async XLA Ops:
  2.8 61.6 %all-to-all-start = ((bf16[32,40,256]{2,1,0:T(8,128)(2,1)}), bf16[32,40,256]{2,1,0:T(8,128)(2,1)S(1)}, u32[]{:S(2)}, u32[]{:S(2)}) async-start(bf16[32,40,256]{2,1,0:T(8,128)(2,1)} %bitcast.17), calls=%async_computation | async-start | bytes 1310720 | tf_op jit(solution)/shard_map/all_to_all | solution.py:284
  65.8 8.4 %collective-permute-start = (bf16[320,256]{1,0:T(8,128)(2,1)S(1)}, bf16[320,256]{1,0:T(8,128)(2,1)S(1)}, u32[]{:S(2)}, u32[]{:S(2)}) collective-permute-start(bf16[320,256]{1,0:T(8,128)(2,1)S(1)} %get-tuple-element.21), channel_id=1, source_target_pairs={{0,1},{1,0},{2,3},{3,2},{4,5},{5,4},{6,7},{7,6},{8,9},{9,8},{10,11... | collective-permute-start | bytes 491528 | tf_op jit(solution)/shard_map/ppermute | solution.py:287
  69.0 15.1 %collective-permute-start.1 = (bf16[320,512]{1,0:T(8,128)(2,1)S(1)}, bf16[320,512]{1,0:T(8,128)(2,1)S(1)}, u32[]{:S(2)}, u32[]{:S(2)}) collective-permute-start(bf16[320,512]{1,0:T(8,128)(2,1)S(1)} %get-tuple-element.24), channel_id=1, source_target_pairs={{0,1},{1,0},{2,3},{3,2},{4,5},{5,4},{6,7},{7,6},{8,9},{9,8},{10,11... | collective-permute-start | bytes 983048 | tf_op jit(solution)/shard_map/ppermute | solution.py:288
  74.2 10.6 %collective-permute-start.2 = (bf16[320,256]{1,0:T(8,128)(2,1)S(1)}, bf16[320,256]{1,0:T(8,128)(2,1)S(1)}, u32[]{:S(2)}, u32[]{:S(2)}) collective-permute-start(bf16[320,256]{1,0:T(8,128)(2,1)S(1)} %add_convert_fusion.1), channel_id=1, source_target_pairs={{0,2},{1,3},{2,0},{3,1},{4,6},{5,7},{6,4},{7,5},{8,10},{9,11},{10,... | collective-permute-start | bytes 491528 | tf_op jit(solution)/shard_map/ppermute | solution.py:292
  80.7 20.8 %collective-permute-start.3 = (bf16[320,768]{1,0:T(8,128)(2,1)S(1)}, bf16[320,768]{1,0:T(8,128)(2,1)S(1)}, u32[]{:S(2)}, u32[]{:S(2)}) collective-permute-start(bf16[320,768]{1,0:T(8,128)(2,1)S(1)} %parts.4), channel_id=1, source_target_pairs={{0,1},{1,0},{2,3},{3,2},{4,5},{5,4},{6,7},{7,6},{8,9},{9,8},{10,11... | collective-permute-start | bytes 1474568 | tf_op jit(solution)/shard_map/ppermute | solution.py:294
  84.8 15.3 %collective-permute-start.4 = (bf16[320,512]{1,0:T(8,128)(2,1)S(1)}, bf16[320,512]{1,0:T(8,128)(2,1)S(1)}, u32[]{:S(2)}, u32[]{:S(2)}) collective-permute-start(bf16[320,512]{1,0:T(8,128)(2,1)S(1)} %add_convert_fusion), channel_id=1, source_target_pairs={{0,2},{1,3},{2,0},{3,1},{4,6},{5,7},{6,4},{7,5},{8,10},{9,11},{10,... | collective-permute-start | bytes 983048 | tf_op jit(solution)/shard_map/ppermute | solution.py:298
  90.3 32.2 %copy-start = (bf16[1,1536,1024]{2,1,0:T(8,128)(2,1)S(1)}, bf16[1,1536,1024]{2,1,0:T(8,128)(2,1)}, u32[]{:S(2)}) copy-start(bf16[1,1536,1024]{2,1,0:T(8,128)(2,1)} %param.13) | copy-start | bytes 9437188
  122.5 12.2 %copy-start.5 = (s32[128,8]{0,1:T(8,128)S(1)}, s32[128,8]{0,1:T(8,128)}, u32[]{:S(2)}) copy-start(s32[128,8]{0,1:T(8,128)} %param.10) | copy-start | bytes 12292
  122.5 12.3 %copy-start.6 = (f32[128,8]{0,1:T(8,128)S(1)}, f32[128,8]{0,1:T(8,128)}, u32[]{:S(2)}) copy-start(f32[128,8]{0,1:T(8,128)} %param.11) | copy-start | bytes 12292
  122.5 12.4 %copy-start.1 = (bf16[512,16]{1,0:T(8,128)(2,1)S(1)}, bf16[512,16]{1,0:T(8,128)(2,1)}, u32[]{:S(2)}) copy-start(bf16[512,16]{1,0:T(8,128)(2,1)} %constant.26.clone.quarter_ref) | copy-start | bytes 49156
  122.5 12.4 %copy-start.2 = (bf16[32,1280]{1,0:T(8,128)(2,1)S(1)}, bf16[32,1280]{1,0:T(8,128)(2,1)}, u32[]{:S(2)}) copy-start(bf16[32,1280]{1,0:T(8,128)(2,1)} %constant.24.clone.expert_ref) | copy-start | bytes 245764
  122.5 12.4 %copy-start.3 = (bf16[16,1280]{1,0:T(8,128)(2,1)S(1)}, bf16[16,1280]{1,0:T(8,128)(2,1)}, u32[]{:S(2)}) copy-start(bf16[16,1280]{1,0:T(8,128)(2,1)} %constant.25.clone.slot_ref) | copy-start | bytes 122884
  122.5 12.4 %copy-start.4 = (bf16[128,128]{1,0:T(8,128)(2,1)S(1)}, bf16[128,128]{1,0:T(8,128)(2,1)}, u32[]{:S(2)}) copy-start(bf16[128,128]{1,0:T(8,128)(2,1)} %constant.23.clone.earlier_ref) | copy-start | bytes 98308
  125.0 42.6 %all-to-all-start.1 = ((bf16[32,40,256]{2,1,0:T(8,128)(2,1)}), bf16[32,40,256]{2,1,0:T(8,128)(2,1)S(1)}, u32[]{:S(2)}, u32[]{:S(2)}) async-start(bf16[32,40,256]{2,1,0:T(8,128)(2,1)} %bitcast.7), calls=%async_computation.1 | async-start | bytes 1310720 | tf_op jit(solution)/shard_map/all_to_all | solution.py:309

commit v9 on v8

--- a/solution.py
+++ b/solution.py
@@ -285,8 +285,9 @@
 
     rows, far_1, far_2 = first_part(received, first_weights)
     got_1 = lax.ppermute(far_1, "tp", near)
+    keep_1, keep_2 = parts(me, 2, rows, up_weights, 1, pieces - 1)
+    far_2, keep_1 = tie(far_2, keep_1)
     got_2 = lax.ppermute(far_2, "tp", near)
-    keep_1, keep_2 = parts(me, 2, rows, up_weights, 1, pieces - 1)
     pair_1 = pair_sum(got_1, keep_1)
     rows, pair_1 = tie(rows, pair_1)
     got_1 = lax.ppermute(pair_1, "tp", far)

time: 169 us -> 172 us (1.018)
  waiting for transfers between devices: 77.4 us -> 80.5 us
    ppermute x1, waiting for transfers between devices: 0.01 us -> 3.27 us  [local(): got_2 = lax.ppermute(far_2, 'tp', near)]
where the time goes in v9:
time: 172 us
  waiting for transfers between devices  80.5 us (47%)
  starting transfers between devices  49.4 us (29%)
  blocking collectives  21 us (12%)
  Pallas kernels  18.2 us (11%)
  local copies, waits for them, and re-layouts  1.77 us (1%)
    all_to_all x1, waiting for transfers between devices, local(): lax.all_to_all(sent.reshape(flight, BLOCK, cols), 'ep', 0, 0, tiled=True)  35.8 us
    all_to_all x1, waiting for transfers between devices, local(): lax.all_to_all(result.reshape(flight, BLOCK, cols), 'ep', 0, 0, tiled=True)  31 us
    all_to_all x1, starting transfers between devices, local(): lax.all_to_all(sent.reshape(flight, BLOCK, cols), 'ep', 0, 0, tiled=True)  24.3 us
    all_gather x1, blocking collectives, local(): lax.all_gather(jnp.concatenate(hidden, axis=1), 'tp', axis=0, tiled=False)  21 us
    all_to_all x1, starting transfers between devices, local(): lax.all_to_all(result.reshape(flight, BLOCK, cols), 'ep', 0, 0, tiled=True)  9.27 us
    ppermute x1, waiting for transfers between devices, local(): got_2 = lax.ppermute(pair_2, 'tp', far)  8.67 us
    pallas_call x3, Pallas kernels, parts(): pl.pallas_call(functools.partial(parts_kernel, mask), out_shape=tuple((ja...  7.48 us
    ppermute x1, starting transfers between devices, local(): got_1 = lax.ppermute(pair_1, 'tp', far)  4.06 us
  transfers between devices with their start and end apart: 7, of which 5 were waited for; matrix products, arithmetic and copies ran while one was open for 1% of the time, Pallas kernels for 6%

profile of v9, /device:TPU:56, one launch (start us, length us, event | category | flops | bytes accessed | tf_op | source)
XLA Modules:
  0.0 171.7 jit_solution(10810873608728940220)
XLA Ops:
  0.0 2.8 %pack.1 = bf16[1280,256]{1,0:T(8,128)(2,1)} custom-call(s32[8,128]{1,0:T(8,128)} %bitcast.18, bf16[128,1024]{1,0:T(8,128)(2,1)} %token_ref.1), custom_call_target="tpu_custom_call" | custom-call | tf_op jit(solution)/shard_map/pack/pallas_call | solution.py:106
  2.8 24.3 %all-to-all-start = ((bf16[32,40,256]{2,1,0:T(8,128)(2,1)}), bf16[32,40,256]{2,1,0:T(8,128)(2,1)S(1)}, u32[]{:S(2)}, u32[]{:S(2)}) async-start(bf16[32,40,256]{2,1,0:T(8,128)(2,1)} %bitcast.17), calls=%async_computation | async-start | bytes 1310720 | tf_op jit(solution)/shard_map/all_to_all | solution.py:284
  27.1 1.5 constant_dynamic-slice_fusion.weight_ref
  28.6 35.8 %all-to-all-done = bf16[32,40,256]{2,1,0:T(8,128)(2,1)S(1)} async-done(((bf16[32,40,256]{2,1,0:T(8,128)(2,1)}), bf16[32,40,256]{2,1,0:T(8,128)(2,1)S(1)}, u32[]{:S(2)}, u32[]{:S(2)}) %all-to-all-start) | async-done | bytes 655392 | tf_op jit(solution)/shard_map/all_to_all | solution.py:284
  64.5 1.3 first.1
  65.8 3.3 %collective-permute-start = (bf16[320,256]{1,0:T(8,128)(2,1)S(1)}, bf16[320,256]{1,0:T(8,128)(2,1)S(1)}, u32[]{:S(2)}, u32[]{:S(2)}) collective-permute-start(bf16[320,256]{1,0:T(8,128)(2,1)S(1)} %get-tuple-element.23), channel_id=1, source_target_pairs={{0,1},{1,0},{2,3},{3,2},{4,5},{5,4},{6,7},{7,6},{8,9},{9,8},{10,11... | collective-permute-start | bytes 491528 | tf_op jit(solution)/shard_map/ppermute | solution.py:287
  69.0 2.5 %parts.3 = (bf16[320,256]{1,0:T(8,128)(2,1)S(1)}, bf16[320,512]{1,0:T(8,128)(2,1)S(1)}) custom-call(s32[1]{0:T(128)} %bitcast.4.me_ref, bf16[320,1024]{1,0:T(8,128)(2,1)S(1)} %get-tuple-element.33.rows_ref, bf16[2,12,128,1024]{3,2,1,0:T(8,128)(2,1)} %bitcast.14), custom_call_target="tpu_custom_call" | custom-call | flops 503316480 | bytes 1572864 | tf_op jit(solution)/shard_map/parts/pallas_call | solution.py:174
  71.5 2.6 %collective-permute-start.1 = (bf16[320,512]{1,0:T(8,128)(2,1)S(1)}, bf16[320,512]{1,0:T(8,128)(2,1)S(1)}, u32[]{:S(2)}, u32[]{:S(2)}) collective-permute-start(bf16[320,512]{1,0:T(8,128)(2,1)S(1)} %get-tuple-element.28), channel_id=1, source_target_pairs={{0,1},{1,0},{2,3},{3,2},{4,5},{5,4},{6,7},{7,6},{8,9},{9,8},{10,11... | collective-permute-start | bytes 983048 | tf_op jit(solution)/shard_map/ppermute | solution.py:290
  74.2 4.1 %collective-permute-start.2 = (bf16[320,256]{1,0:T(8,128)(2,1)S(1)}, bf16[320,256]{1,0:T(8,128)(2,1)S(1)}, u32[]{:S(2)}, u32[]{:S(2)}) collective-permute-start(bf16[320,256]{1,0:T(8,128)(2,1)S(1)} %add_convert_fusion.1), channel_id=1, source_target_pairs={{0,2},{1,3},{2,0},{3,1},{4,6},{5,7},{6,4},{7,5},{8,10},{9,11},{10,... | collective-permute-start | bytes 491528 | tf_op jit(solution)/shard_map/ppermute | solution.py:293
  78.3 2.5 %parts.4 = bf16[320,768]{1,0:T(8,128)(2,1)S(1)} custom-call(s32[1]{0:T(128)} %bitcast.4.me_ref, bf16[320,1024]{1,0:T(8,128)(2,1)S(1)} %get-tuple-element.33.rows_ref, bf16[2,12,128,1024]{3,2,1,0:T(8,128)(2,1)} %bitcast.15), custom_call_target="tpu_custom_call" | custom-call | flops 503316480 | bytes 1572864 | tf_op jit(solution)/shard_map/parts/pallas_call | solution.py:174
  80.8 3.2 %collective-permute-start.3 = (bf16[320,768]{1,0:T(8,128)(2,1)S(1)}, bf16[320,768]{1,0:T(8,128)(2,1)S(1)}, u32[]{:S(2)}, u32[]{:S(2)}) collective-permute-start(bf16[320,768]{1,0:T(8,128)(2,1)S(1)} %parts.4), channel_id=1, source_target_pairs={{0,1},{1,0},{2,3},{3,2},{4,5},{5,4},{6,7},{7,6},{8,9},{9,8},{10,11... | collective-permute-start | bytes 1474568 | tf_op jit(solution)/shard_map/ppermute | solution.py:295
  84.0 3.3 %collective-permute-done.1 = bf16[320,512]{1,0:T(8,128)(2,1)S(1)} collective-permute-done((bf16[320,512]{1,0:T(8,128)(2,1)S(1)}, bf16[320,512]{1,0:T(8,128)(2,1)S(1)}, u32[]{:S(2)}, u32[]{:S(2)}) %collective-permute-start.1) | collective-permute-done | bytes 327712 | tf_op jit(solution)/shard_map/ppermute | solution.py:290
  87.4 2.7 %collective-permute-start.4 = (bf16[320,512]{1,0:T(8,128)(2,1)S(1)}, bf16[320,512]{1,0:T(8,128)(2,1)S(1)}, u32[]{:S(2)}, u32[]{:S(2)}) collective-permute-start(bf16[320,512]{1,0:T(8,128)(2,1)S(1)} %add_convert_fusion), channel_id=1, source_target_pairs={{0,2},{1,3},{2,0},{3,1},{4,6},{5,7},{6,4},{7,5},{8,10},{9,11},{10,... | collective-permute-start | bytes 983048 | tf_op jit(solution)/shard_map/ppermute | solution.py:299
  90.1 2.5 %parts.5 = bf16[320,768]{1,0:T(8,128)(2,1)S(1)} custom-call(s32[1]{0:T(128)} %bitcast.4.me_ref, bf16[320,1024]{1,0:T(8,128)(2,1)S(1)} %get-tuple-element.33.rows_ref, bf16[2,12,128,1024]{3,2,1,0:T(8,128)(2,1)} %bitcast.16), custom_call_target="tpu_custom_call" | custom-call | flops 503316480 | bytes 1572864 | tf_op jit(solution)/shard_map/parts/pallas_call | solution.py:174
  92.6 8.7 %collective-permute-done.4 = bf16[320,512]{1,0:T(8,128)(2,1)S(1)} collective-permute-done((bf16[320,512]{1,0:T(8,128)(2,1)S(1)}, bf16[320,512]{1,0:T(8,128)(2,1)S(1)}, u32[]{:S(2)}, u32[]{:S(2)}) %collective-permute-start.4) | collective-permute-done | bytes 327712 | tf_op jit(solution)/shard_map/ppermute | solution.py:299
  101.3 1.8 %collective-permute-done.3 = bf16[320,768]{1,0:T(8,128)(2,1)S(1)} collective-permute-done((bf16[320,768]{1,0:T(8,128)(2,1)S(1)}, bf16[320,768]{1,0:T(8,128)(2,1)S(1)}, u32[]{:S(2)}, u32[]{:S(2)}) %collective-permute-start.3) | collective-permute-done | bytes 491552 | tf_op jit(solution)/shard_map/ppermute | solution.py:295
  103.0 0.2 convert_add_fusion.1
  103.4 21.0 %all-gather = bf16[1280,384]{1,0:T(8,128)(2,1)S(1)} all-gather(bf16[320,384]{1,0:T(8,128)(2,1)S(1)} %pad_maximum_fusion), channel_id=2, replica_groups=mesh['dp'=8,'ep'=32,'tp'=4] {'tp'}, dimensions={0}, use_global_device_ids=true | all-gather | bytes 1228800 | tf_op jit(solution)/shard_map/all_gather | solution.py:307
  124.5 2.5 %down.1 = bf16[1280,256]{1,0:T(8,128)(2,1)} custom-call(bf16[4,320,384]{2,1,0:T(8,128)(2,1)S(1)} %bitcast.9, bf16[1536,1024]{1,0:T(8,128)(2,1)S(1)} %bitcast.10), custom_call_target="tpu_custom_call" | custom-call | tf_op jit(solution)/shard_map/down/pallas_call | solution.py:195
  127.0 9.3 %all-to-all-start.1 = ((bf16[32,40,256]{2,1,0:T(8,128)(2,1)}), bf16[32,40,256]{2,1,0:T(8,128)(2,1)S(1)}, u32[]{:S(2)}, u32[]{:S(2)}) async-start(bf16[32,40,256]{2,1,0:T(8,128)(2,1)} %bitcast.7), calls=%async_computation.1 | async-start | bytes 1310720 | tf_op jit(solution)/shard_map/all_to_all | solution.py:310
  136.4 0.1 copy.11.weight_ref
  136.5 2.9 %mixer.1.mixer_ref = bf16[512,1280]{1,0:T(8,128)(2,1)S(1)} custom-call(s32[128,8]{1,0:T(8,128)S(1)} %copy.10.ids_ref, f32[128,8]{1,0:T(8,128)S(1)} %copy.11.weight_ref, bf16[128,128]{1,0:T(8,128)(2,1)S(1)} %copy-done.4, bf16[32,1280]{1,0:T(8,128)(2,1)S(1)} %copy-done.2, bf16[16,1280]{1,0:T(8,128)(2,1)S(1)} %copy-done.3, bf16[512,16]{1,0:T(8,128)(2,1)S(1)} %copy-done.1), custom_call_target="tpu_custom_call" | custom-call | tf_op jit(solution)/shard_map/mixer/pallas_call | solution.py:229
  139.4 31.0 %all-to-all-done.1 = bf16[32,40,256]{2,1,0:T(8,128)(2,1)S(1)} async-done(((bf16[32,40,256]{2,1,0:T(8,128)(2,1)}), bf16[32,40,256]{2,1,0:T(8,128)(2,1)S(1)}, u32[]{:S(2)}, u32[]{:S(2)}) %all-to-all-start.1) | async-done | bytes 655392 | tf_op jit(solution)/shard_map/all_to_all | solution.py:310
  170.4 1.2 combine.1
  (22 shorter events, 0.5 us)
Async XLA Ops:
  2.8 61.6 %all-to-all-start = ((bf16[32,40,256]{2,1,0:T(8,128)(2,1)}), bf16[32,40,256]{2,1,0:T(8,128)(2,1)S(1)}, u32[]{:S(2)}, u32[]{:S(2)}) async-start(bf16[32,40,256]{2,1,0:T(8,128)(2,1)} %bitcast.17), calls=%async_computation | async-start | bytes 1310720 | tf_op jit(solution)/shard_map/all_to_all | solution.py:284
  65.8 8.4 %collective-permute-start = (bf16[320,256]{1,0:T(8,128)(2,1)S(1)}, bf16[320,256]{1,0:T(8,128)(2,1)S(1)}, u32[]{:S(2)}, u32[]{:S(2)}) collective-permute-start(bf16[320,256]{1,0:T(8,128)(2,1)S(1)} %get-tuple-element.23), channel_id=1, source_target_pairs={{0,1},{1,0},{2,3},{3,2},{4,5},{5,4},{6,7},{7,6},{8,9},{9,8},{10,11... | collective-permute-start | bytes 491528 | tf_op jit(solution)/shard_map/ppermute | solution.py:287
  71.5 15.7 %collective-permute-start.1 = (bf16[320,512]{1,0:T(8,128)(2,1)S(1)}, bf16[320,512]{1,0:T(8,128)(2,1)S(1)}, u32[]{:S(2)}, u32[]{:S(2)}) collective-permute-start(bf16[320,512]{1,0:T(8,128)(2,1)S(1)} %get-tuple-element.28), channel_id=1, source_target_pairs={{0,1},{1,0},{2,3},{3,2},{4,5},{5,4},{6,7},{7,6},{8,9},{9,8},{10,11... | collective-permute-start | bytes 983048 | tf_op jit(solution)/shard_map/ppermute | solution.py:290
  74.2 13.2 %collective-permute-start.2 = (bf16[320,256]{1,0:T(8,128)(2,1)S(1)}, bf16[320,256]{1,0:T(8,128)(2,1)S(1)}, u32[]{:S(2)}, u32[]{:S(2)}) collective-permute-start(bf16[320,256]{1,0:T(8,128)(2,1)S(1)} %add_convert_fusion.1), channel_id=1, source_target_pairs={{0,2},{1,3},{2,0},{3,1},{4,6},{5,7},{6,4},{7,5},{8,10},{9,11},{10,... | collective-permute-start | bytes 491528 | tf_op jit(solution)/shard_map/ppermute | solution.py:293
  80.8 22.3 %collective-permute-start.3 = (bf16[320,768]{1,0:T(8,128)(2,1)S(1)}, bf16[320,768]{1,0:T(8,128)(2,1)S(1)}, u32[]{:S(2)}, u32[]{:S(2)}) collective-permute-start(bf16[320,768]{1,0:T(8,128)(2,1)S(1)} %parts.4), channel_id=1, source_target_pairs={{0,1},{1,0},{2,3},{3,2},{4,5},{5,4},{6,7},{7,6},{8,9},{9,8},{10,11... | collective-permute-start | bytes 1474568 | tf_op jit(solution)/shard_map/ppermute | solution.py:295
  87.4 13.9 %collective-permute-start.4 = (bf16[320,512]{1,0:T(8,128)(2,1)S(1)}, bf16[320,512]{1,0:T(8,128)(2,1)S(1)}, u32[]{:S(2)}, u32[]{:S(2)}) collective-permute-start(bf16[320,512]{1,0:T(8,128)(2,1)S(1)} %add_convert_fusion), channel_id=1, source_target_pairs={{0,2},{1,3},{2,0},{3,1},{4,6},{5,7},{6,4},{7,5},{8,10},{9,11},{10,... | collective-permute-start | bytes 983048 | tf_op jit(solution)/shard_map/ppermute | solution.py:299
  92.6 31.9 %copy-start = (bf16[1,1536,1024]{2,1,0:T(8,128)(2,1)S(1)}, bf16[1,1536,1024]{2,1,0:T(8,128)(2,1)}, u32[]{:S(2)}) copy-start(bf16[1,1536,1024]{2,1,0:T(8,128)(2,1)} %param.13) | copy-start | bytes 9437188
  124.4 11.8 %copy-start.5 = (s32[128,8]{0,1:T(8,128)S(1)}, s32[128,8]{0,1:T(8,128)}, u32[]{:S(2)}) copy-start(s32[128,8]{0,1:T(8,128)} %param.10) | copy-start | bytes 12292
  124.4 11.9 %copy-start.6 = (f32[128,8]{0,1:T(8,128)S(1)}, f32[128,8]{0,1:T(8,128)}, u32[]{:S(2)}) copy-start(f32[128,8]{0,1:T(8,128)} %param.11) | copy-start | bytes 12292
  124.4 12.0 %copy-start.1 = (bf16[512,16]{1,0:T(8,128)(2,1)S(1)}, bf16[512,16]{1,0:T(8,128)(2,1)}, u32[]{:S(2)}) copy-start(bf16[512,16]{1,0:T(8,128)(2,1)} %constant.26.clone.quarter_ref) | copy-start | bytes 49156
  124.4 12.0 %copy-start.2 = (bf16[32,1280]{1,0:T(8,128)(2,1)S(1)}, bf16[32,1280]{1,0:T(8,128)(2,1)}, u32[]{:S(2)}) copy-start(bf16[32,1280]{1,0:T(8,128)(2,1)} %constant.24.clone.expert_ref) | copy-start | bytes 245764
  124.5 12.0 %copy-start.3 = (bf16[16,1280]{1,0:T(8,128)(2,1)S(1)}, bf16[16,1280]{1,0:T(8,128)(2,1)}, u32[]{:S(2)}) copy-start(bf16[16,1280]{1,0:T(8,128)(2,1)} %constant.25.clone.slot_ref) | copy-start | bytes 122884
  124.5 12.0 %copy-start.4 = (bf16[128,128]{1,0:T(8,128)(2,1)S(1)}, bf16[128,128]{1,0:T(8,128)(2,1)}, u32[]{:S(2)}) copy-start(bf16[128,128]{1,0:T(8,128)(2,1)} %constant.23.clone.earlier_ref) | copy-start | bytes 98308
  127.0 43.5 %all-to-all-start.1 = ((bf16[32,40,256]{2,1,0:T(8,128)(2,1)}), bf16[32,40,256]{2,1,0:T(8,128)(2,1)S(1)}, u32[]{:S(2)}, u32[]{:S(2)}) async-start(bf16[32,40,256]{2,1,0:T(8,128)(2,1)} %bitcast.7), calls=%async_computation.1 | async-start | bytes 1310720 | tf_op jit(solution)/shard_map/all_to_all | solution.py:310

commit v10 on v8

--- a/solution.py
+++ b/solution.py
@@ -279,10 +279,12 @@
         return (got.astype(F32) + keep.astype(F32)).astype(BF16)
 
     sent = pack(expert_ids.T, tokens, flight)
-    sent, up_weights = tie(sent, up_weights)
+    sent, up_weights, ids, weight = tie(sent, up_weights, expert_ids, route_weight)
+    mix = mixer(ids, weight, flight)
     first_weights = lax.dynamic_slice_in_dim(up_weights, (me[0] ^ 3) * pieces, pieces, axis=1)
     received = lax.all_to_all(sent.reshape(flight, BLOCK, cols), "ep", 0, 0, tiled=True).reshape(flight * BLOCK, cols)
 
+    received, mix = tie(received, mix)
     rows, far_1, far_2 = first_part(received, first_weights)
     got_1 = lax.ppermute(far_1, "tp", near)
     got_2 = lax.ppermute(far_2, "tp", near)
@@ -307,7 +309,6 @@
 
     result = down(hidden, down_proj[0])
     returned = lax.all_to_all(result.reshape(flight, BLOCK, cols), "ep", 0, 0, tiled=True).reshape(flight * BLOCK, cols)
-    mix = mixer(expert_ids, route_weight, flight)
     return combine(mix, returned)
 
 

time: 169 us -> 168 us (level)
  blocking collectives: 20.6 us -> 62.9 us
  waiting for transfers between devices: 77.4 us -> 39.8 us
  starting transfers between devices: 50.1 us -> 40.5 us
  local copies, waits for them, and re-layouts: 1.77 us -> 6.44 us
    all_to_all x0 -> x1, blocking collectives: none -> 42.4 us  [local(): lax.all_to_all(result.reshape(flight, BLOCK, cols), 'ep', 0, 0, tiled=True)]
    all_to_all x1 -> x0, waiting for transfers between devices: 29.7 us -> none  [local(): lax.all_to_all(result.reshape(flight, BLOCK, cols), 'ep', 0, 0, tiled=True)]
    all_to_all x1 -> x0, starting transfers between devices: 9.66 us -> none  [local(): lax.all_to_all(result.reshape(flight, BLOCK, cols), 'ep', 0, 0, tiled=True)]
    all_to_all x1, waiting for transfers between devices: 35.8 us -> 28 us  [local(): lax.all_to_all(sent.reshape(flight, BLOCK, cols), 'ep', 0, 0, tiled=True)]
    unnamed x16 -> x10, local copies, waits for them, and re-layouts: 0.24 us -> 3.33 us
  transfers between devices with their start and end apart: 7 -> 6, of which waited for: 5 -> 4; matrix products, arithmetic and copies ran while one was open for 1% -> 2% of each run, Pallas kernels for 6% -> 6%
where the time goes in v10:
time: 168 us
  blocking collectives  62.9 us (37%)
  starting transfers between devices  40.5 us (24%)
  waiting for transfers between devices  39.8 us (24%)
  Pallas kernels  17.3 us (10%)
  local copies, waits for them, and re-layouts  6.44 us (4%)
    all_to_all x1, blocking collectives, local(): lax.all_to_all(result.reshape(flight, BLOCK, cols), 'ep', 0, 0, tiled=True)  42.4 us
    all_to_all x1, waiting for transfers between devices, local(): lax.all_to_all(sent.reshape(flight, BLOCK, cols), 'ep', 0, 0, tiled=True)  28 us
    all_to_all x1, starting transfers between devices, local(): lax.all_to_all(sent.reshape(flight, BLOCK, cols), 'ep', 0, 0, tiled=True)  24.3 us
    all_gather x1, blocking collectives, local(): lax.all_gather(jnp.concatenate(hidden, axis=1), 'tp', axis=0, tiled=False)  20.6 us
    ppermute x1, waiting for transfers between devices, local(): got_2 = lax.ppermute(pair_2, 'tp', far)  9.77 us
    pallas_call x3, Pallas kernels, parts(): pl.pallas_call(functools.partial(parts_kernel, mask), out_shape=tuple((ja...  7.49 us
    ppermute x1, starting transfers between devices, local(): got_1 = lax.ppermute(pair_1, 'tp', far)  4.04 us
  transfers between devices with their start and end apart: 6, of which 4 were waited for; matrix products, arithmetic and copies ran while one was open for 2% of the time, Pallas kernels for 6%

profile of v10, /device:TPU:56, one launch (start us, length us, event | category | flops | bytes accessed | tf_op | source)
XLA Modules:
  0.0 167.7 jit_solution(17442680552354821705)
XLA Ops:
  0.0 2.8 %pack.1 = bf16[1280,256]{1,0:T(8,128)(2,1)} custom-call(s32[8,128]{1,0:T(8,128)} %bitcast.19, bf16[128,1024]{1,0:T(8,128)(2,1)} %token_ref.1), custom_call_target="tpu_custom_call" | custom-call | tf_op jit(solution)/shard_map/pack/pallas_call | solution.py:106
  2.8 24.3 %all-to-all-start = ((bf16[32,40,256]{2,1,0:T(8,128)(2,1)}), bf16[32,40,256]{2,1,0:T(8,128)(2,1)S(1)}, u32[]{:S(2)}, u32[]{:S(2)}) async-start(bf16[32,40,256]{2,1,0:T(8,128)(2,1)} %bitcast.18), calls=%async_computation | async-start | bytes 1310720 | tf_op jit(solution)/shard_map/all_to_all | solution.py:285
  27.1 0.8 copy.10.ids_ref
  27.9 0.8 copy.11.weight_ref
  28.7 0.9 copy-done.1
  29.6 0.9 copy-done.2
  32.0 2.9 %mixer.1.mixer_ref = bf16[512,1280]{1,0:T(8,128)(2,1)S(1)} custom-call(s32[128,8]{1,0:T(8,128)S(1)} %copy.10.ids_ref, f32[128,8]{1,0:T(8,128)S(1)} %copy.11.weight_ref, bf16[128,128]{1,0:T(8,128)(2,1)S(1)} %copy-done.4, bf16[32,1280]{1,0:T(8,128)(2,1)S(1)} %copy-done.2, bf16[16,1280]{1,0:T(8,128)(2,1)S(1)} %copy-done.3, bf16[512,16]{1,0:T(8,128)(2,1)S(1)} %copy-done.1), custom_call_target="tpu_custom_call" | custom-call | tf_op jit(solution)/shard_map/mixer/pallas_call | solution.py:229
  34.9 1.5 constant_dynamic-slice_fusion.weight_ref
  36.4 28.0 %all-to-all-done = bf16[32,40,256]{2,1,0:T(8,128)(2,1)S(1)} async-done(((bf16[32,40,256]{2,1,0:T(8,128)(2,1)}), bf16[32,40,256]{2,1,0:T(8,128)(2,1)S(1)}, u32[]{:S(2)}, u32[]{:S(2)}) %all-to-all-start) | async-done | bytes 655392 | tf_op jit(solution)/shard_map/all_to_all | solution.py:285
  64.4 1.3 first.1
  65.8 3.3 %collective-permute-start = (bf16[320,256]{1,0:T(8,128)(2,1)S(1)}, bf16[320,256]{1,0:T(8,128)(2,1)S(1)}, u32[]{:S(2)}, u32[]{:S(2)}) collective-permute-start(bf16[320,256]{1,0:T(8,128)(2,1)S(1)} %get-tuple-element.29), channel_id=1, source_target_pairs={{0,1},{1,0},{2,3},{3,2},{4,5},{5,4},{6,7},{7,6},{8,9},{9,8},{10,11... | collective-permute-start | bytes 491528 | tf_op jit(solution)/shard_map/ppermute | solution.py:289
  69.0 2.6 %collective-permute-start.1 = (bf16[320,512]{1,0:T(8,128)(2,1)S(1)}, bf16[320,512]{1,0:T(8,128)(2,1)S(1)}, u32[]{:S(2)}, u32[]{:S(2)}) collective-permute-start(bf16[320,512]{1,0:T(8,128)(2,1)S(1)} %get-tuple-element.32), channel_id=1, source_target_pairs={{0,1},{1,0},{2,3},{3,2},{4,5},{5,4},{6,7},{7,6},{8,9},{9,8},{10,11... | collective-permute-start | bytes 983048 | tf_op jit(solution)/shard_map/ppermute | solution.py:290
  71.6 2.5 %parts.3 = (bf16[320,256]{1,0:T(8,128)(2,1)S(1)}, bf16[320,512]{1,0:T(8,128)(2,1)S(1)}) custom-call(s32[1]{0:T(128)} %bitcast.4.me_ref, bf16[320,1024]{1,0:T(8,128)(2,1)S(1)} %get-tuple-element.37.rows_ref, bf16[2,12,128,1024]{3,2,1,0:T(8,128)(2,1)} %bitcast.15), custom_call_target="tpu_custom_call" | custom-call | flops 503316480 | bytes 1572864 | tf_op jit(solution)/shard_map/parts/pallas_call | solution.py:174
  74.2 4.0 %collective-permute-start.2 = (bf16[320,256]{1,0:T(8,128)(2,1)S(1)}, bf16[320,256]{1,0:T(8,128)(2,1)S(1)}, u32[]{:S(2)}, u32[]{:S(2)}) collective-permute-start(bf16[320,256]{1,0:T(8,128)(2,1)S(1)} %add_convert_fusion.1), channel_id=1, source_target_pairs={{0,2},{1,3},{2,0},{3,1},{4,6},{5,7},{6,4},{7,5},{8,10},{9,11},{10,... | collective-permute-start | bytes 491528 | tf_op jit(solution)/shard_map/ppermute | solution.py:294
  78.2 2.5 %parts.4 = bf16[320,768]{1,0:T(8,128)(2,1)S(1)} custom-call(s32[1]{0:T(128)} %bitcast.4.me_ref, bf16[320,1024]{1,0:T(8,128)(2,1)S(1)} %get-tuple-element.37.rows_ref, bf16[2,12,128,1024]{3,2,1,0:T(8,128)(2,1)} %bitcast.16), custom_call_target="tpu_custom_call" | custom-call | flops 503316480 | bytes 1572864 | tf_op jit(solution)/shard_map/parts/pallas_call | solution.py:174
  80.8 3.3 %collective-permute-start.3 = (bf16[320,768]{1,0:T(8,128)(2,1)S(1)}, bf16[320,768]{1,0:T(8,128)(2,1)S(1)}, u32[]{:S(2)}, u32[]{:S(2)}) collective-permute-start(bf16[320,768]{1,0:T(8,128)(2,1)S(1)} %parts.4), channel_id=1, source_target_pairs={{0,1},{1,0},{2,3},{3,2},{4,5},{5,4},{6,7},{7,6},{8,9},{9,8},{10,11... | collective-permute-start | bytes 1474568 | tf_op jit(solution)/shard_map/ppermute | solution.py:296
  84.8 3.0 %collective-permute-start.4 = (bf16[320,512]{1,0:T(8,128)(2,1)S(1)}, bf16[320,512]{1,0:T(8,128)(2,1)S(1)}, u32[]{:S(2)}, u32[]{:S(2)}) collective-permute-start(bf16[320,512]{1,0:T(8,128)(2,1)S(1)} %add_convert_fusion), channel_id=1, source_target_pairs={{0,2},{1,3},{2,0},{3,1},{4,6},{5,7},{6,4},{7,5},{8,10},{9,11},{10,... | collective-permute-start | bytes 983048 | tf_op jit(solution)/shard_map/ppermute | solution.py:300
  87.8 2.5 %parts.5 = bf16[320,768]{1,0:T(8,128)(2,1)S(1)} custom-call(s32[1]{0:T(128)} %bitcast.4.me_ref, bf16[320,1024]{1,0:T(8,128)(2,1)S(1)} %get-tuple-element.37.rows_ref, bf16[2,12,128,1024]{3,2,1,0:T(8,128)(2,1)} %bitcast.17), custom_call_target="tpu_custom_call" | custom-call | flops 503316480 | bytes 1572864 | tf_op jit(solution)/shard_map/parts/pallas_call | solution.py:174
  90.3 9.8 %collective-permute-done.4 = bf16[320,512]{1,0:T(8,128)(2,1)S(1)} collective-permute-done((bf16[320,512]{1,0:T(8,128)(2,1)S(1)}, bf16[320,512]{1,0:T(8,128)(2,1)S(1)}, u32[]{:S(2)}, u32[]{:S(2)}) %collective-permute-start.4) | collective-permute-done | bytes 327712 | tf_op jit(solution)/shard_map/ppermute | solution.py:300
  100.1 1.5 collective-permute-done.3
  101.9 20.6 %all-gather = bf16[1280,384]{1,0:T(8,128)(2,1)S(1)} all-gather(bf16[320,384]{1,0:T(8,128)(2,1)S(1)} %pad_maximum_fusion), channel_id=2, replica_groups=mesh['dp'=8,'ep'=32,'tp'=4] {'tp'}, dimensions={0}, use_global_device_ids=true | all-gather | bytes 1228800 | tf_op jit(solution)/shard_map/all_gather | solution.py:308
  122.5 1.6 down.1
  124.1 42.4 %all_to_all.10 = bf16[32,40,256]{2,1,0:T(8,128)(2,1)S(1)} all-to-all(bf16[32,40,256]{2,1,0:T(8,128)(2,1)S(1)} %bitcast.11), channel_id=1, replica_groups=mesh['dp'=8,'ep'=32,'tp'=4] {'ep'}, dimensions={0} | all-to-all | bytes 1310720 | tf_op jit(solution)/shard_map/all_to_all | solution.py:311
  166.4 1.2 combine.1
  (17 shorter events, 2.6 us)
Async XLA Ops:
  2.8 61.6 %all-to-all-start = ((bf16[32,40,256]{2,1,0:T(8,128)(2,1)}), bf16[32,40,256]{2,1,0:T(8,128)(2,1)S(1)}, u32[]{:S(2)}, u32[]{:S(2)}) async-start(bf16[32,40,256]{2,1,0:T(8,128)(2,1)} %bitcast.18), calls=%async_computation | async-start | bytes 1310720 | tf_op jit(solution)/shard_map/all_to_all | solution.py:285
  28.7 0.9 copy-start.1
  29.6 0.9 copy-start.2
  30.5 0.8 copy-start.3
  31.3 0.8 copy-start.4
  65.8 8.4 %collective-permute-start = (bf16[320,256]{1,0:T(8,128)(2,1)S(1)}, bf16[320,256]{1,0:T(8,128)(2,1)S(1)}, u32[]{:S(2)}, u32[]{:S(2)}) collective-permute-start(bf16[320,256]{1,0:T(8,128)(2,1)S(1)} %get-tuple-element.29), channel_id=1, source_target_pairs={{0,1},{1,0},{2,3},{3,2},{4,5},{5,4},{6,7},{7,6},{8,9},{9,8},{10,11... | collective-permute-start | bytes 491528 | tf_op jit(solution)/shard_map/ppermute | solution.py:289
  69.0 15.1 %collective-permute-start.1 = (bf16[320,512]{1,0:T(8,128)(2,1)S(1)}, bf16[320,512]{1,0:T(8,128)(2,1)S(1)}, u32[]{:S(2)}, u32[]{:S(2)}) collective-permute-start(bf16[320,512]{1,0:T(8,128)(2,1)S(1)} %get-tuple-element.32), channel_id=1, source_target_pairs={{0,1},{1,0},{2,3},{3,2},{4,5},{5,4},{6,7},{7,6},{8,9},{9,8},{10,11... | collective-permute-start | bytes 983048 | tf_op jit(solution)/shard_map/ppermute | solution.py:290
  74.2 10.6 %collective-permute-start.2 = (bf16[320,256]{1,0:T(8,128)(2,1)S(1)}, bf16[320,256]{1,0:T(8,128)(2,1)S(1)}, u32[]{:S(2)}, u32[]{:S(2)}) collective-permute-start(bf16[320,256]{1,0:T(8,128)(2,1)S(1)} %add_convert_fusion.1), channel_id=1, source_target_pairs={{0,2},{1,3},{2,0},{3,1},{4,6},{5,7},{6,4},{7,5},{8,10},{9,11},{10,... | collective-permute-start | bytes 491528 | tf_op jit(solution)/shard_map/ppermute | solution.py:294
  80.8 20.8 %collective-permute-start.3 = (bf16[320,768]{1,0:T(8,128)(2,1)S(1)}, bf16[320,768]{1,0:T(8,128)(2,1)S(1)}, u32[]{:S(2)}, u32[]{:S(2)}) collective-permute-start(bf16[320,768]{1,0:T(8,128)(2,1)S(1)} %parts.4), channel_id=1, source_target_pairs={{0,1},{1,0},{2,3},{3,2},{4,5},{5,4},{6,7},{7,6},{8,9},{9,8},{10,11... | collective-permute-start | bytes 1474568 | tf_op jit(solution)/shard_map/ppermute | solution.py:296
  84.8 15.3 %collective-permute-start.4 = (bf16[320,512]{1,0:T(8,128)(2,1)S(1)}, bf16[320,512]{1,0:T(8,128)(2,1)S(1)}, u32[]{:S(2)}, u32[]{:S(2)}) collective-permute-start(bf16[320,512]{1,0:T(8,128)(2,1)S(1)} %add_convert_fusion), channel_id=1, source_target_pairs={{0,2},{1,3},{2,0},{3,1},{4,6},{5,7},{6,4},{7,5},{8,10},{9,11},{10,... | collective-permute-start | bytes 983048 | tf_op jit(solution)/shard_map/ppermute | solution.py:300
  90.3 32.2 %copy-start = (bf16[1,1536,1024]{2,1,0:T(8,128)(2,1)S(1)}, bf16[1,1536,1024]{2,1,0:T(8,128)(2,1)}, u32[]{:S(2)}) copy-start(bf16[1,1536,1024]{2,1,0:T(8,128)(2,1)} %param.13) | copy-start | bytes 9437188
